TPU v7x, 32 devices: a whole 2x2x4 slice. The times are simulated.
32 devices in a mesh: row: 4 (over z), col: 8 (over y, x, core).
Axes of the slice: x: 2, y: 2, z: 4, core: 2. Of those that a mesh axis runs over, the one named last changes fastest.
Arguments:
- tiles: float32 [2, 2304, 4608], P(None, 'row', 'col'), may hold values from -5 to 5
- pupils: float32 [2, 512, 1024], P(None, 'row', 'col'), may hold values from -5 to 5
- intensity: float32 [16, 512, 1024], P(None, 'row', 'col'), may hold values from 0.2 to 3
- offsets: int32 [4, 8, 2, 16], P('row', 'col'), may hold values from 0 to 448
Outputs:
- refocused: float32 [2, 2048, 4096], P(None, 'row', 'col')
Inputs may be any that keep to these rules, and one draw needn't show every extreme that they name: `offsets`: each window lies inside the tile's spectrum.
All inputs are finite; a program needn't handle non-finite values.
Results may differ from a plain program's by a relative error of at most 0.00017.
Values sent between devices are 32-bit elements; how exact they have to be, the bound alone decides.
No kernel may reach another device: no remote copies, remote signals or barrier semaphores. Data moves between devices by JAX's collectives and lax.ppermute only.
A program may use at most 128 MiB of HBM per device.

v0:
```python
import math

import jax
import jax.numpy as jnp
from jax import lax
from jax.sharding import PartitionSpec as P

OVL = 64


STEP_SIZE = 0.05
TWO_PI = 2.0 * math.pi


def from_behind(value, axis, steps):
    count = lax.axis_size(axis)
    pairs = [(source, (source + steps) % count) for source in range(count)]
    return lax.ppermute(value, axis, pairs)


def propagator(rows, cols, total_rows, total_cols, fresnel):
    signed_rows = jnp.where(rows < total_rows // 2, rows, rows - total_rows)
    signed_cols = jnp.where(cols < total_cols // 2, cols, cols - total_cols)
    square_rows = (signed_rows * signed_rows).astype(jnp.float32)
    square_cols = (signed_cols * signed_cols).astype(jnp.float32)
    turns_rows = square_rows * (fresnel / (total_rows * total_rows))
    turns_rows = turns_rows - jnp.floor(turns_rows)
    turns_cols = square_cols * (fresnel / (total_cols * total_cols))
    turns_cols = turns_cols - jnp.floor(turns_cols)
    angle = -TWO_PI * (turns_rows[:, None] + turns_cols[None, :])
    decay = jnp.exp(
        -2.0
        * (
            square_rows[:, None] / (total_rows * total_rows)
            + square_cols[None, :] / (total_cols * total_cols)
        )
    )
    return (decay * jnp.cos(angle), decay * jnp.sin(angle))


def dft_table(length, sign, scale):
    index = jnp.arange(length, dtype=jnp.int32)
    product = index[:, None] * index[None, :] % length
    angle = product.astype(jnp.float32) * (TWO_PI / length)
    return (jnp.cos(angle) * scale, sign * scale * jnp.sin(angle))


def complex_apply(form, matrix_real, matrix_imag, value_real, value_imag):

    def product(left, right):
        return jnp.einsum(form, left, right, precision=lax.Precision.HIGHEST)

    out_real = product(matrix_real, value_real) - product(matrix_imag, value_imag)
    out_imag = product(matrix_real, value_imag) + product(matrix_imag, value_real)
    return (out_real, out_imag)


def complex_mul(left_real, left_imag, right_real, right_imag):
    return (
        left_real * right_real - left_imag * right_imag,
        left_real * right_imag + left_imag * right_real,
    )


def forward_pass(field, axis_dim, count, position, swapper):
    size = field.shape[1]
    segment = size // count
    length = size * count
    small_real, small_imag = dft_table(count, -1.0, 1.0)
    big_real, big_imag = dft_table(size, -1.0, 1.0)
    freq_low = jnp.arange(count, dtype=jnp.int32)[:, None]
    place_high = position * segment + jnp.arange(segment, dtype=jnp.int32)[None, :]
    turn_angle = (freq_low * place_high % length).astype(jnp.float32) * (-TWO_PI / length)
    turn_real, turn_imag = (jnp.cos(turn_angle), jnp.sin(turn_angle))
    mixed = swapper(field)
    if axis_dim == 1:
        block_real = mixed[0].reshape(count, segment, size)
        block_imag = mixed[1].reshape(count, segment, size)
        block_real, block_imag = complex_apply(
            "kp,psj->ksj", small_real, small_imag, block_real, block_imag
        )
        block_real, block_imag = complex_mul(
            block_real, block_imag, turn_real[:, :, None], turn_imag[:, :, None]
        )
        joined = swapper(jnp.stack([block_real, block_imag]).reshape(2, size, size))
        out_real, out_imag = complex_apply("ks,sj->kj", big_real, big_imag, joined[0], joined[1])
    else:
        block_real = mixed[0].reshape(size, count, segment)
        block_imag = mixed[1].reshape(size, count, segment)
        block_real, block_imag = complex_apply(
            "kp,jps->jks", small_real, small_imag, block_real, block_imag
        )
        block_real, block_imag = complex_mul(
            block_real, block_imag, turn_real[None], turn_imag[None]
        )
        joined = swapper(jnp.stack([block_real, block_imag]).reshape(2, size, size))
        out_real, out_imag = complex_apply("ks,js->jk", big_real, big_imag, joined[0], joined[1])
    return jnp.stack([out_real, out_imag])


def inverse_pass(field, axis_dim, count, position, swapper):
    size = field.shape[1]
    segment = size // count
    length = size * count
    small_real, small_imag = dft_table(count, 1.0, 1.0 / length)
    big_real, big_imag = dft_table(size, 1.0, 1.0)
    places = jnp.arange(size, dtype=jnp.int32)
    turn_angle = (places * position % length).astype(jnp.float32) * (TWO_PI / length)
    turn_real, turn_imag = (jnp.cos(turn_angle), jnp.sin(turn_angle))
    if axis_dim == 1:
        local_real, local_imag = complex_apply("sk,kj->sj", big_real, big_imag, field[0], field[1])
        local_real, local_imag = complex_mul(
            local_real, local_imag, turn_real[:, None], turn_imag[:, None]
        )
        joined = swapper(jnp.stack([local_real, local_imag]))
        block_real = joined[0].reshape(count, segment, size)
        block_imag = joined[1].reshape(count, segment, size)
        block_real, block_imag = complex_apply(
            "pk,ksj->psj", small_real, small_imag, block_real, block_imag
        )
    else:
        local_real, local_imag = complex_apply("sk,jk->js", big_real, big_imag, field[0], field[1])
        local_real, local_imag = complex_mul(
            local_real, local_imag, turn_real[None, :], turn_imag[None, :]
        )
        joined = swapper(jnp.stack([local_real, local_imag]))
        block_real = joined[0].reshape(size, count, segment)
        block_imag = joined[1].reshape(size, count, segment)
        block_real, block_imag = complex_apply(
            "pk,jks->jps", small_real, small_imag, block_real, block_imag
        )
    return swapper(jnp.stack([block_real, block_imag]).reshape(2, size, size))


def row_swap(values):
    return lax.all_to_all(values, "row", split_axis=1, concat_axis=1, tiled=True)


def column_swap(values):
    return lax.all_to_all(values, "col", split_axis=2, concat_axis=2, tiled=True)


def local(tiles, pupils, intensity, offsets):
    tile_len = tiles.shape[1]
    window = pupils.shape[1]
    margin = OVL
    stride = tile_len - margin
    led_count = intensity.shape[0]
    tile_real, tile_imag = dft_table(tile_len, -1.0, 1.0 / math.sqrt(tile_len))
    spec_real, spec_imag = complex_apply("jk,kl->jl", tile_real, tile_imag, tiles[0], tiles[1])
    spec_real, spec_imag = complex_apply("lk,jk->jl", tile_real, tile_imag, spec_real, spec_imag)
    spectrum = jnp.stack([spec_real, spec_imag])
    starts = offsets[0, 0]

    def cut(row_start, col_start):
        return lax.dynamic_slice(
            spectrum, (jnp.int32(0), row_start, col_start), (2, window, window)
        )

    crops = jax.vmap(cut)(starts[0], starts[1])
    win_real, win_imag = dft_table(window, -1.0, 1.0 / math.sqrt(window))
    lens_real, lens_imag = (pupils[0], pupils[1])
    wave_real, wave_imag = complex_mul(lens_real, lens_imag, crops[:, 0], crops[:, 1])
    wave_real, wave_imag = complex_apply("jk,nkl->njl", win_real, -win_imag, wave_real, wave_imag)
    wave_real, wave_imag = complex_apply("lk,njk->njl", win_real, -win_imag, wave_real, wave_imag)
    excess = wave_real * wave_real + wave_imag * wave_imag - intensity
    grad_real, grad_imag = complex_apply(
        "jk,nkl->njl", win_real, win_imag, wave_real * excess, wave_imag * excess
    )
    grad_real, grad_imag = complex_apply("lk,njk->njl", win_real, win_imag, grad_real, grad_imag)
    update_real = lens_real * grad_real + lens_imag * grad_imag
    update_imag = lens_real * grad_imag - lens_imag * grad_real
    updates = jnp.stack([update_real, update_imag], axis=1)

    def place(led, total):
        corner = (jnp.int32(0), starts[0, led], starts[1, led])
        current = lax.dynamic_slice(total, corner, (2, window, window))
        return lax.dynamic_update_slice(total, current + updates[led], corner)

    total = lax.fori_loop(0, led_count, place, jnp.zeros_like(spectrum))
    new_spec = spectrum - STEP_SIZE * total
    obj_real, obj_imag = complex_apply("jk,kl->jl", tile_real, -tile_imag, new_spec[0], new_spec[1])
    obj_real, obj_imag = complex_apply("lk,jk->jl", tile_real, -tile_imag, obj_real, obj_imag)
    refined = jnp.stack([obj_real, obj_imag])
    ramp = (jnp.arange(margin, dtype=jnp.float32) + 0.5) / margin
    lower = from_behind(refined[:, stride:, :], "row", 1)
    top = ramp[:, None] * refined[:, :margin, :] + (1.0 - ramp)[:, None] * lower
    rowed = jnp.concatenate([top, refined[:, margin:stride, :]], axis=1)
    packed = rowed[:, :, stride:].reshape(2, stride * margin // 128, 128)
    left = from_behind(packed, "col", 1).reshape(2, stride, margin)
    front = ramp * rowed[:, :, :margin] + (1.0 - ramp) * left
    field = jnp.concatenate([front, rowed[:, :, margin:stride]], axis=2)
    row_count = lax.axis_size("row")
    col_count = lax.axis_size("col")
    row_place = lax.axis_index("row")
    col_place = lax.axis_index("col")
    fresnel = stride * row_count // 2
    local_index = jnp.arange(stride, dtype=jnp.int32)
    field = forward_pass(field, 1, row_count, row_place, row_swap)
    field = forward_pass(field, 2, col_count, col_place, column_swap)
    freq_rows = local_index * row_count + row_place
    freq_cols = local_index * col_count + col_place
    prop_real, prop_imag = propagator(
        freq_rows, freq_cols, stride * row_count, stride * col_count, fresnel
    )
    shifted_real, shifted_imag = complex_mul(field[0], field[1], prop_real, prop_imag)
    field = jnp.stack([shifted_real, shifted_imag])
    field = inverse_pass(field, 2, col_count, col_place, column_swap)
    field = inverse_pass(field, 1, row_count, row_place, row_swap)
    return field


def solution(mesh):
    placed = (
        P(None, "row", "col"),
        P(None, "row", "col"),
        P(None, "row", "col"),
        P("row", "col", None, None),
    )
    return jax.shard_map(
        local, mesh=mesh, in_specs=placed, out_specs=P(None, "row", "col"), check_vma=False
    )
```

profile of v0, /device:TPU:8, one launch (start us, length us, event | category | flops | bytes accessed | tf_op | source)
XLA Modules:
  0.0 909.8 jit_solution(7899662348539163753)
XLA Ops:
  0.0 12.2 %fusion.3 = f32[576,576]{1,0:T(8,128)} fusion(f32[2,576,576]{2,1,0:T(8,128)} %param.6), kind=kOutput, calls=%fused_computation.27 | convolution fusion | flops 2296553472 | bytes 2801664 | tf_op jit(solution)/shard_map/jk,kl->jl/dot_general | solution.py:51
  12.2 11.1 %fusion.5 = f32[576,576]{1,0:T(8,128)} fusion(f32[2,576,576]{2,1,0:T(8,128)S(1)} %copy-done.4), kind=kOutput, calls=%fused_computation.29 | convolution fusion | flops 2296553472 | bytes 2801664 | tf_op jit(solution)/shard_map/jk,kl->jl/dot_general | solution.py:51
  23.4 11.7 %fusion.17 = f32[576,576]{1,0:T(8,128)S(1)} fusion(f32[576,576]{1,0:T(8,128)} %fusion.3, f32[2,576,576]{2,1,0:T(8,128)} %param.6), kind=kOutput, calls=%fused_computation.46 | convolution fusion | flops 2296885248 | bytes 4276224 | tf_op jit(solution)/shard_map/jk,kl->jl/dot_general | solution.py:51
  35.1 9.9 %fusion.39 = f32[576,576]{1,0:T(8,128)S(1)} fusion(f32[576,576]{1,0:T(8,128)S(1)} %fusion.17), kind=kOutput, calls=%fused_computation.92 | convolution fusion | flops 2296553472 | bytes 2654208 | tf_op jit(solution)/shard_map/lk,jk->jl/dot_general | solution.py:51
  45.0 10.1 %fusion.14 = f32[576,576]{1,0:T(8,128)S(1)} fusion(f32[576,576]{1,0:T(8,128)S(1)} %copy-done.6, f32[2,576,576]{2,1,0:T(8,128)S(1)} %copy-done.5), kind=kOutput, calls=%fused_computation.45 | convolution fusion | flops 2296885248 | bytes 4276224 | tf_op jit(solution)/shard_map/jk,kl->jl/dot_general | solution.py:51
  55.2 9.6 %fusion.40 = f32[576,576]{1,0:T(8,128)S(1)} fusion(f32[576,576]{1,0:T(8,128)S(1)} %fusion.14), kind=kOutput, calls=%fused_computation.93 | convolution fusion | flops 2296553472 | bytes 2654208 | tf_op jit(solution)/shard_map/lk,jk->jl/dot_general | solution.py:51
  64.8 11.0 %add_bitcast_fusion.1 = f32[1,576,576]{2,1,0:T(8,128)} fusion(f32[576,576]{1,0:T(8,128)S(1)} %fusion.39, f32[576,576]{1,0:T(8,128)S(1)} %fusion.14), kind=kOutput, calls=%fused_computation.37 | convolution fusion | flops 2296885248 | bytes 3981312 | tf_op jit(solution)/shard_map/lk,jk->jl/dot_general | solution.py:51
  75.8 11.2 %subtract_bitcast_fusion.1 = f32[1,576,576]{2,1,0:T(8,128)} fusion(f32[576,576]{1,0:T(8,128)S(1)} %fusion.40, f32[576,576]{1,0:T(8,128)S(1)} %fusion.17), kind=kOutput, calls=%fused_computation.38 | convolution fusion | flops 2296885248 | bytes 3981312 | tf_op jit(solution)/shard_map/lk,jk->jl/dot_general | solution.py:51
  90.6 46.7 %while.15 = (s32[]{:T(128)}, f32[2,576,576]{2,1,0:T(8,128)}, s32[16,3]{0,1:T(4,128)S(1)}, f32[16,2,128,128]{3,2,0,1:T(8,128)S(1)}, s32[]{:T(128)}) while((s32[]{:T(128)}, f32[2,576,576]{2,1,0:T(8,128)}, s32[16,3]{0,1:T(4,128)S(1)}, f32[16,2,128,128]{3,2,0,1:T(8,128)S(1)}, s32[]{:T(128)}) %tuple.71), condition=%wide.while_cond, body=%wide.while_body.sunk | while | flops 2 | bytes 262261 | solution.py:156
  174.8 124.3 %while.14 = (s32[]{:T(128)}, f32[2,576,576]{2,1,0:T(8,128)S(1)}, s32[2,16]{1,0:T(2,128)S(1)}, f32[16,2,128,128]{3,2,0,1:T(8,128)}, s32[]{:T(128)}, /*index=5*/s32[]{:T(128)}, s32[]{:T(128)}) while((s32[]{:T(128)}, f32[2,576,576]{2,1,0:T(8,128)S(1)}, s32[2,16]{1,0:T(2,128)S(1)}, f32[16,2,128,128]{3,2,0,1:T(8,128)}, s32[]{:T(128)}, ...), condition=%wide.region_1.2_spmd, body=%wide.region_0.1_spmd.sunk | while | flops 32776 | bytes 655541 | solution.py:180
  301.3 9.7 %fusion.20 = f32[576,576]{1,0:T(8,128)S(1)} fusion(f32[2,576,576]{2,1,0:T(8,128)S(1)} %multiply_subtract_fusion), kind=kOutput, calls=%fused_computation.49 | convolution fusion | flops 2296553472 | bytes 2801664 | tf_op jit(solution)/shard_map/jk,kl->jl/dot_general | solution.py:51
  311.0 9.9 %fusion.21 = f32[576,576]{1,0:T(8,128)S(1)} fusion(f32[2,576,576]{2,1,0:T(8,128)S(1)} %multiply_subtract_fusion), kind=kOutput, calls=%fused_computation.50 | convolution fusion | flops 2296553472 | bytes 2801664 | tf_op jit(solution)/shard_map/jk,kl->jl/dot_general | solution.py:51
  320.9 9.9 %convolution_subtract_fusion = f32[576,576]{1,0:T(8,128)S(1)} fusion(f32[576,576]{1,0:T(8,128)S(1)} %fusion.20, f32[2,576,576]{2,1,0:T(8,128)S(1)} %multiply_subtract_fusion), kind=kOutput, calls=%fused_computation.48 | convolution fusion | flops 2297217024 | bytes 4276224 | tf_op jit(solution)/shard_map/jk,kl->jl/dot_general | solution.py:51
  330.8 10.1 %fusion.38 = f32[576,576]{1,0:T(8,128)S(1)} fusion(f32[576,576]{1,0:T(8,128)S(1)} %convolution_subtract_fusion), kind=kOutput, calls=%fused_computation.91 | convolution fusion | flops 2296553472 | bytes 2654208 | tf_op jit(solution)/shard_map/lk,jk->jl/dot_general | solution.py:51
  340.9 10.0 %convolution_add_fusion = f32[576,576]{1,0:T(8,128)S(1)} fusion(f32[576,576]{1,0:T(8,128)S(1)} %fusion.21, f32[2,576,576]{2,1,0:T(8,128)S(1)} %multiply_subtract_fusion), kind=kOutput, calls=%fused_computation.47 | convolution fusion | flops 2297217024 | bytes 4276224 | tf_op jit(solution)/shard_map/jk,kl->jl/dot_general | solution.py:51
  350.9 9.6 %fusion.37 = f32[576,576]{1,0:T(8,128)S(1)} fusion(f32[576,576]{1,0:T(8,128)S(1)} %convolution_add_fusion), kind=kOutput, calls=%fused_computation.90 | convolution fusion | flops 2296553472 | bytes 2654208 | tf_op jit(solution)/shard_map/lk,jk->jl/dot_general | solution.py:51
  360.5 9.9 %subtract_bitcast_fusion = f32[1,576,576]{2,1,0:T(8,128)S(1)} fusion(f32[576,576]{1,0:T(8,128)S(1)} %fusion.38, f32[576,576]{1,0:T(8,128)S(1)} %convolution_add_fusion), kind=kOutput, calls=%fused_computation.36 | convolution fusion | flops 2297217024 | bytes 3981312 | tf_op jit(solution)/shard_map/lk,jk->jl/dot_general | solution.py:51
  370.5 10.2 %add_bitcast_fusion = f32[1,576,576]{2,1,0:T(8,128)S(1)} fusion(f32[576,576]{1,0:T(8,128)S(1)} %fusion.37, f32[576,576]{1,0:T(8,128)S(1)} %convolution_subtract_fusion), kind=kOutput, calls=%fused_computation.35 | convolution fusion | flops 2297217024 | bytes 3981312 | tf_op jit(solution)/shard_map/lk,jk->jl/dot_general | solution.py:51
  381.9 8.0 collective-permute-done
  392.5 4.9 collective-permute-done.1
  403.7 5.8 all-to-all-start
  409.8 43.4 %all-to-all-done = f32[2,512,512]{2,0,1:T(2,128)S(1)} async-done(((f32[2,512,512]{2,0,1:T(2,128)}), f32[2,512,512]{2,0,1:T(2,128)S(1)}, u32[]{:S(2)}, u32[]{:S(2)}) %all-to-all-start) | async-done | bytes 2097184 | tf_op jit(solution)/shard_map/all_to_all | solution.py:136
  468.0 51.7 %all_to_all.40 = f32[2,512,512]{2,0,1:T(2,128)S(1)} all-to-all(f32[2,512,512]{2,0,1:T(2,128)S(1)} %copy.225), channel_id=1, replica_groups=mesh['row'=4,'col'=8] {'row'}, dimensions={1} | all-to-all | bytes 4194304 | tf_op jit(solution)/shard_map/all_to_all | solution.py:136
  521.3 5.7 fusion.60
  527.0 5.9 fusion.56
  532.9 5.8 fusion.31
  538.7 6.2 fusion.30
  547.6 3.6 all-to-all-start.2
  551.4 26.3 %all-to-all-done.2 = f32[2,512,512]{1,0,2:T(2,128)S(1)} async-done(((f32[2,512,512]{1,0,2:T(2,128)}), f32[2,512,512]{1,0,2:T(2,128)S(1)}, u32[]{:S(2)}, u32[]{:S(2)}) %all-to-all-start.2) | async-done | bytes 2097184 | tf_op jit(solution)/shard_map/all_to_all | solution.py:140
  591.2 3.6 all-to-all-start.3
  594.9 26.5 %all-to-all-done.3 = f32[2,512,512]{1,0,2:T(2,128)S(1)} async-done(((f32[2,512,512]{1,0,2:T(2,128)}), f32[2,512,512]{1,0,2:T(2,128)S(1)}, u32[]{:S(2)}, u32[]{:S(2)}) %all-to-all-start.3) | async-done | bytes 2097184 | tf_op jit(solution)/shard_map/all_to_all | solution.py:140
  623.0 7.1 fusion.54
  630.1 7.5 fusion.50
  637.6 7.2 convolution_subtract_fusion.5
  644.8 7.3 convolution_add_fusion.5
  652.1 10.1 %fusion.188 = f32[512,512]{1,0:T(8,128)S(1)} fusion(f32[512,512]{1,0:T(8,128)S(1)} %convolution_add_fusion.5, f32[512,512]{1,0:T(8,128)S(1)} %convolution_subtract_fusion.5, f32[512]{0:T(512)S(1)} %get-tuple-element.171, f32[512]{0:T(512)S(1)} %get-tuple-element.167, f32[512]{0:T(512)S(1)} %get-tuple-element.172, f32[512]{0:T(512)S(1)} %get-tuple-element.168), kind=kOutput, calls=%fused_computation.240 | convolution fusion | flops 1616642048 | bytes 3153920 | tf_op jit(solution)/shard_map/sk,jk->js/dot_general | solution.py:51
  662.2 10.2 %fusion.186 = f32[512,512]{1,0:T(8,128)S(1)} fusion(f32[512,512]{1,0:T(8,128)S(1)} %convolution_add_fusion.5, f32[512,512]{1,0:T(8,128)S(1)} %convolution_subtract_fusion.5, f32[512]{0:T(512)S(1)} %get-tuple-element.171, f32[512]{0:T(512)S(1)} %get-tuple-element.167, f32[512]{0:T(512)S(1)} %get-tuple-element.172, f32[512]{0:T(512)S(1)} %get-tuple-element.168), kind=kOutput, calls=%fused_computation.239 | convolution fusion | flops 1616642048 | bytes 3153920 | tf_op jit(solution)/shard_map/sk,jk->js/dot_general | solution.py:51
  672.5 10.1 %convolution_add_fusion.4 = f32[512,512]{1,0:T(8,128)S(1)} fusion(f32[512,512]{1,0:T(8,128)S(1)} %fusion.186, f32[512,512]{1,0:T(8,128)S(1)} %convolution_add_fusion.5, f32[512,512]{1,0:T(8,128)S(1)} %convolution_subtract_fusion.5, f32[512]{0:T(512)S(1)} %get-tuple-element.171, f32[512]{0:T(512)S(1)} %get-tuple-element.167, f32[512]{0:T(512)S(1)} %get-tuple-element.172, ...), kind=kOutput, calls=%fused_computation.63 | convolution fusion | flops 1616904192 | bytes 4202496 | tf_op jit(solution)/shard_map/sk,jk->js/dot_general | solution.py:51
  682.5 10.1 %subtract_bitcast_fusion.3 = (f32[1,512,512]{2,1,0:T(8,128)S(1)}, f32[1,512,512]{2,1,0:T(8,128)S(1)}) fusion(f32[512,512]{1,0:T(8,128)S(1)} %convolution_add_fusion.4, f32[512]{0:T(512)S(1)} %get-tuple-element.173, f32[512]{0:T(512)S(1)} %get-tuple-element.174, f32[512,512]{1,0:T(8,128)S(1)} %fusion.188, f32[512,512]{1,0:T(8,128)S(1)} %convolution_add_fusion.5, ...), kind=kOutput, calls=%fused_computation.124 | convolution fusion | flops 1618477056 | bytes 6303744 | tf_op jit(solution)/shard_map/sk,jk->js/dot_general | solution.py:51
  695.2 30.3 %all_to_all.41 = f32[2,512,512]{1,0,2:T(2,128)S(1)} all-to-all(f32[2,512,512]{1,0,2:T(2,128)} %copy.238), channel_id=1, replica_groups=mesh['row'=4,'col'=8] {'col'}, dimensions={2} | all-to-all | bytes 4194304 | tf_op jit(solution)/shard_map/all_to_all | solution.py:140
  738.6 4.1 all-to-all-start.5
  742.7 26.1 %all-to-all-done.5 = f32[2,512,512]{1,0,2:T(2,128)S(1)} async-done(((f32[2,512,512]{1,0,2:T(2,128)}), f32[2,512,512]{1,0,2:T(2,128)S(1)}, u32[]{:S(2)}, u32[]{:S(2)}) %all-to-all-start.5) | async-done | bytes 2097184 | tf_op jit(solution)/shard_map/all_to_all | solution.py:140
  770.4 5.7 fusion.44
  776.1 5.9 fusion.48
  782.0 5.8 convolution_add_fusion.2
  787.9 6.2 subtract_bitcast_fusion.2
  795.8 48.1 %all_to_all.42 = f32[2,512,512]{2,0,1:T(2,128)S(1)} all-to-all(f32[2,512,512]{2,0,1:T(2,128)S(1)} %copy.248), channel_id=1, replica_groups=mesh['row'=4,'col'=8] {'row'}, dimensions={1} | all-to-all | bytes 4194304 | tf_op jit(solution)/shard_map/all_to_all | solution.py:136
  858.2 49.5 %all_to_all.43 = f32[2,512,512]{2,0,1:T(2,128)S(1)} all-to-all(f32[2,512,512]{2,0,1:T(2,128)S(1)} %copy.257), channel_id=1, replica_groups=mesh['row'=4,'col'=8] {'row'}, dimensions={1} | all-to-all | bytes 4194304 | tf_op jit(solution)/shard_map/all_to_all | solution.py:136
  (214 shorter events, 234.1 us)
Async XLA Ops:
  0.0 12.2 %copy-start.4 = (f32[2,576,576]{2,1,0:T(8,128)S(1)}, f32[2,576,576]{2,1,0:T(8,128)}, u32[]{:S(2)}) copy-start(f32[2,576,576]{2,1,0:T(8,128)} %param.6) | copy-start | bytes 7962628
  35.1 9.9 %copy-start.5 = (f32[2,576,576]{2,1,0:T(8,128)S(1)}, f32[2,576,576]{2,1,0:T(8,128)}, u32[]{:S(2)}) copy-start(f32[2,576,576]{2,1,0:T(8,128)} %param.6) | copy-start | bytes 7962628
  35.1 9.9 %copy-start.6 = (f32[576,576]{1,0:T(8,128)S(1)}, f32[576,576]{1,0:T(8,128)}, u32[]{:S(2)}) copy-start(f32[576,576]{1,0:T(8,128)} %fusion.5) | copy-start | bytes 3981316
  75.8 11.2 %copy-start.3 = (s32[1,1,2,16]{3,2,1,0:T(2,128)S(1)}, s32[1,1,2,16]{3,2,1,0:T(2,128)}, u32[]{:S(2)}) copy-start(s32[1,1,2,16]{3,2,1,0:T(2,128)} %param.9) | copy-start | bytes 388
  90.6 46.7 %copy-start.2 = (f32[2,128,128]{2,1,0:T(8,128)S(1)}, f32[2,128,128]{2,1,0:T(8,128)}, u32[]{:S(2)}) copy-start(f32[2,128,128]{2,1,0:T(8,128)} %param.7) | copy-start | bytes 393220
  151.3 1.9 copy-start
  159.4 3.4 copy-start.1
  380.7 9.3 %collective-permute-start = (f32[2,64,576]{2,1,0:T(8,128)S(1)}, f32[2,64,576]{2,1,0:T(8,128)S(1)}, u32[]{:S(2)}, u32[]{:S(2)}) collective-permute-start(f32[2,64,576]{2,1,0:T(8,128)S(1)} %pad_maximum_fusion.10), channel_id=1, source_target_pairs={{0,8},{8,16},{16,24},{24,0},{1,9},{9,17},{17,25},{25,1},{2,10},{10... | collective-permute-start | bytes 884744 | tf_op jit(solution)/shard_map/ppermute | solution.py:18
  390.5 6.9 collective-permute-start.1
  403.7 49.5 %all-to-all-start = ((f32[2,512,512]{2,0,1:T(2,128)}), f32[2,512,512]{2,0,1:T(2,128)S(1)}, u32[]{:S(2)}, u32[]{:S(2)}) async-start(f32[2,512,512]{2,0,1:T(2,128)} %copy.214), calls=%async_computation | async-start | bytes 4194304 | tf_op jit(solution)/shard_map/all_to_all | solution.py:136
  547.6 30.2 %all-to-all-start.2 = ((f32[2,512,512]{1,0,2:T(2,128)}), f32[2,512,512]{1,0,2:T(2,128)S(1)}, u32[]{:S(2)}, u32[]{:S(2)}) async-start(f32[2,512,512]{1,0,2:T(2,128)} %copy.226), calls=%async_computation.2 | async-start | bytes 4194304 | tf_op jit(solution)/shard_map/all_to_all | solution.py:140
  591.2 30.2 %all-to-all-start.3 = ((f32[2,512,512]{1,0,2:T(2,128)}), f32[2,512,512]{1,0,2:T(2,128)S(1)}, u32[]{:S(2)}, u32[]{:S(2)}) async-start(f32[2,512,512]{1,0,2:T(2,128)} %copy.237), calls=%async_computation.3 | async-start | bytes 4194304 | tf_op jit(solution)/shard_map/all_to_all | solution.py:140
  738.6 30.2 %all-to-all-start.5 = ((f32[2,512,512]{1,0,2:T(2,128)}), f32[2,512,512]{1,0,2:T(2,128)S(1)}, u32[]{:S(2)}, u32[]{:S(2)}) async-start(f32[2,512,512]{1,0,2:T(2,128)} %copy.247), calls=%async_computation.5 | async-start | bytes 4194304 | tf_op jit(solution)/shard_map/all_to_all | solution.py:140
where the time goes:
time: 925 us; the launch traced here: 910 us
  matrix products  353 us (38%)
  blocking collectives  180 us (19%)
  local copies, waits for them, and re-layouts  135 us (15%)
  waiting for transfers between devices  135 us (15%)
  loops' own time  59.4 us (6%)
  other arithmetic  27.7 us (3%)
  starting transfers between devices  18.4 us (2%)
    dot_general x64, matrix products, product(): return jnp.einsum(form, left, right, precision=lax.Precision.HIGHEST)  353 us
    all_to_all x3, blocking collectives, row_swap(): lax.all_to_all(values, 'row', split_axis=1, concat_axis=1, tiled=True)  149 us
    all_to_all x3, waiting for transfers between devices, column_swap(): lax.all_to_all(values, 'col', split_axis=2, concat_axis=2, tiled=True)  78.9 us
    another operation x1, loops' own time, local(): total = lax.fori_loop(0, led_count, place, jnp.zeros_like(spectrum))  59.1 us
    gather x48, local copies, waits for them, and re-layouts  46.4 us
    all_to_all x1, waiting for transfers between devices, row_swap(): lax.all_to_all(values, 'row', split_axis=1, concat_axis=1, tiled=True)  43.4 us
    dynamic_update_slice x16, local copies, waits for them, and re-layouts, place(): return lax.dynamic_update_slice(total, current + updates[led], corner)  39.1 us
    all_to_all x1, blocking collectives, column_swap(): lax.all_to_all(values, 'col', split_axis=2, concat_axis=2, tiled=True)  30.3 us
  transfers between devices with their start and end apart: 6, of which 6 were waited for; matrix products, arithmetic and copies ran while one was open for 0% of the time, Pallas kernels for 0%

commit v1 on v0

v1 whole, which is shorter than its diff:
```python
import functools
import math

import jax
import jax.numpy as jnp
import ml_dtypes
import numpy as np
from jax import lax
from jax.experimental import pallas as pl
from jax.experimental.pallas import tpu as pltpu
from jax.sharding import PartitionSpec as P

OVL = 64
STEP_SIZE = 0.05
LANES = 128
RADIX = 4
BF16 = jnp.bfloat16
F32 = jnp.float32


def halves(table):
    table = np.asarray(table, np.float64)
    high = table.astype(np.float32).astype(ml_dtypes.bfloat16)
    low = (table - high.astype(np.float64)).astype(np.float32).astype(ml_dtypes.bfloat16)
    return high, low


def left_block(matrix):
    return np.block([[matrix.real, -matrix.imag], [matrix.imag, matrix.real]])


def right_block(matrix):
    return np.block([[matrix.real, matrix.imag], [-matrix.imag, matrix.real]])


def along_left(block):
    high, low = halves(block)
    return np.concatenate([high, high, low], axis=-1)


def along_right(block):
    high, low = halves(block)
    return np.concatenate([high, high, low], axis=-2)


def dft_matrix(length, sign):
    index = np.arange(length)
    turns = (index[:, None] * index[None, :]) % length
    return np.exp(sign * 2j * np.pi * turns / length) / math.sqrt(length)


def tile_tables(length, sign):
    part = length // RADIX
    index = np.arange(part)
    tables = []
    for residue in range(RADIX):
        turns = (index[None, :] * (residue + RADIX * index[:, None])) % length
        matrix = np.exp(sign * 2j * np.pi * turns / length) / math.sqrt(length)
        tables.append(along_left(left_block(matrix)))
    return np.stack(tables)


def spread_tables(length, fresnel, count, block_of):
    signed = np.arange(length, dtype=np.float64)
    signed = np.where(signed < length // 2, signed, signed - length)
    square = signed * signed
    turns = square * (fresnel / (length * length))
    turns = turns - np.floor(turns)
    kernel = np.fft.ifft(np.exp(-2.0 * square / (length * length)) * np.exp(-2j * np.pi * turns))
    part = length // count
    shift = np.arange(part)[:, None] - np.arange(part)[None, :]
    places = (np.arange(count)[:, None] * part + np.arange(1 - part, part)[None, :]) % length
    classes = np.fft.fft(kernel[places], axis=0) / count
    pairs = [halves(block_of(line[shift + part - 1])) for line in classes]
    return np.stack([pair[0] for pair in pairs]), np.stack([pair[1] for pair in pairs])


def split(value):
    high = value.astype(BF16)
    low = (value - high.astype(F32)).astype(BF16)
    return high, low


def turned(value, eighth_turns, sign):
    real, imag = value
    angle = sign * 2.0 * math.pi * eighth_turns
    if eighth_turns == 0:
        return real, imag
    if eighth_turns == 0.25:
        return (imag, -real) if sign < 0 else (-imag, real)
    cosine, sine = math.cos(angle), math.sin(angle)
    return real * cosine - imag * sine, real * sine + imag * cosine


def short_fft(values, sign):
    count = len(values)
    if count == 1:
        return values
    even = short_fft(values[0::2], sign)
    odd = short_fft(values[1::2], sign)
    low, high = [], []
    for index in range(count // 2):
        real, imag = turned(odd[index], index / count, sign)
        low.append((even[index][0] + real, even[index][1] + imag))
        high.append((even[index][0] - real, even[index][1] - imag))
    return low + high


def tile_pass(source, target, table, operand, sign):
    chunks, length = source.shape[1], source.shape[2]
    part = length // RADIX
    for chunk in range(chunks):
        values = [
            tuple(source[side, chunk, pl.ds(part * step, part), :] for side in range(2))
            for step in range(RADIX)
        ]
        for residue, (real, imag) in enumerate(short_fft(values, sign)):
            lanes = pl.ds(chunk * LANES, LANES)
            for side, value in enumerate((real, imag)):
                high, low = split(value)
                operand[residue, pl.ds(side * part, part), lanes] = high
                operand[residue, pl.ds((2 + side) * part, part), lanes] = low
                operand[residue, pl.ds((4 + side) * part, part), lanes] = high
    for residue in range(RADIX):
        result = jnp.dot(table[residue], operand[residue], preferred_element_type=F32)
        for chunk in range(chunks):
            for side in range(2):
                target[side, chunk, pl.ds(residue, part, stride=RADIX), :] = result[
                    side * part : (side + 1) * part, chunk * LANES : (chunk + 1) * LANES
                ]


def transpose_all(source, target):
    chunks, length = source.shape[1], source.shape[2]
    for side in range(2):
        for chunk in range(chunks):
            rows = min(LANES, length - chunk * LANES)
            for other in range(chunks):
                width = min(LANES, length - other * LANES)
                block = source[side, chunk, pl.ds(other * LANES, width), :]
                target[side, other, pl.ds(chunk * LANES, rows), pl.ds(0, width)] = block.T[:rows]


def refine_kernel(
    starts, tiles, pupils, intensity, to_spectrum, to_object, row_back, col_back, row_fore, col_fore,
    out, first, second, operand, updates,
):
    length = tiles.shape[1]
    window = pupils.shape[1]
    leds = intensity.shape[0]
    chunks = first.shape[1]
    for side in range(2):
        for chunk in range(chunks):
            width = min(LANES, length - chunk * LANES)
            first[side, chunk, :, pl.ds(0, width)] = tiles[side, :, pl.ds(chunk * LANES, width)]
    tile_pass(first, second, to_spectrum, operand, -1)
    transpose_all(second, first)
    tile_pass(first, second, to_spectrum, operand, -1)
    lens_real, lens_imag = pupils[0].T, pupils[1].T
    lane = lax.broadcasted_iota(jnp.int32, (window, LANES), 1)
    group = 8 if leds % 8 == 0 else 1

    def place_of(led):
        start = starts[0, led]
        chunk = start // LANES
        return chunk, start - chunk * LANES, starts[1, led]

    def step(index, carry):
        rows = []
        for member in range(group):
            chunk, shift, row = place_of(index * group + member)
            crop = []
            for side in range(2):
                here = second[side, chunk, pl.ds(row, window), :]
                beyond = second[side, chunk + 1, pl.ds(row, window), :]
                joined = jnp.where(lane >= shift, here, beyond)
                crop.append(pltpu.roll(joined, lax.rem(LANES - shift, LANES), 1))
            rows.append(
                jnp.concatenate(
                    [
                        lens_real * crop[0] - lens_imag * crop[1],
                        lens_real * crop[1] + lens_imag * crop[0],
                    ],
                    axis=1,
                )
            )
        high, low = split(jnp.concatenate(rows, axis=0))
        wave = jnp.dot(
            jnp.concatenate([high, low, high], axis=1), row_back[...], preferred_element_type=F32
        )
        wave = jnp.concatenate(
            [
                jnp.concatenate(
                    [wave[m * window : (m + 1) * window, :window], wave[m * window : (m + 1) * window, window:]],
                    axis=0,
                )
                for m in range(group)
            ],
            axis=1,
        )
        high, low = split(wave)
        wave = jnp.dot(
            col_back[...], jnp.concatenate([high, low, high], axis=0), preferred_element_type=F32
        )
        real, imag = wave[:window], wave[window:]
        measured = jnp.concatenate([intensity[index * group + m].T for m in range(group)], axis=1)
        excess = real * real + imag * imag - measured
        high, low = split(jnp.concatenate([real * excess, imag * excess], axis=0))
        grad = jnp.dot(
            col_fore[...], jnp.concatenate([high, low, high], axis=0), preferred_element_type=F32
        )
        grad = jnp.concatenate(
            [
                jnp.concatenate(
                    [grad[:window, m * window : (m + 1) * window], grad[window:, m * window : (m + 1) * window]],
                    axis=1,
                )
                for m in range(group)
            ],
            axis=0,
        )
        high, low = split(grad)
        grad = jnp.dot(
            jnp.concatenate([high, low, high], axis=1), row_fore[...], preferred_element_type=F32
        )
        for m in range(group):
            real = grad[m * window : (m + 1) * window, :window]
            imag = grad[m * window : (m + 1) * window, window:]
            led = index * group + m
            updates[led, 0] = -STEP_SIZE * (lens_real * real + lens_imag * imag)
            updates[led, 1] = -STEP_SIZE * (lens_real * imag - lens_imag * real)
        return carry

    lax.fori_loop(0, leds // group, step, 0)

    def place(led, carry):
        chunk, shift, row = place_of(led)
        for side in range(2):
            moved = pltpu.roll(updates[led, side], shift, 1)
            second[side, chunk, pl.ds(row, window), :] += jnp.where(lane >= shift, moved, 0.0)
            second[side, chunk + 1, pl.ds(row, window), :] += jnp.where(lane >= shift, 0.0, moved)
        return carry

    lax.fori_loop(0, leds, place, 0)
    tile_pass(second, first, to_object, operand, 1)
    transpose_all(first, second)
    tile_pass(second, first, to_object, operand, 1)
    whole = (length - OVL) // LANES
    count, rows = out.shape[0], out.shape[2]
    for part in range(count):
        have = max(0, min(rows, length - part * rows))
        if have < rows:
            out[part] = jnp.zeros(out.shape[1:], F32)
        if have == 0:
            continue
        here = pl.ds(part * rows, have)
        for side in range(2):
            for chunk in range(whole):
                out[part, side * whole + chunk, pl.ds(0, have), :] = first[side, chunk, here, :]
        halo = first[0, whole, here, :]
        other = pltpu.roll(first[1, whole, here, :], OVL, 1)
        low = lax.broadcasted_iota(jnp.int32, halo.shape, 1) < OVL
        out[part, 2 * whole, pl.ds(0, have), :] = jnp.where(low, halo, other)


def ramp_of(index):
    return (index.astype(F32) + 0.5) / OVL


def col_kernel(values, high_table, low_table, out, held):
    tiles, pieces, rows, _ = values.shape
    whole = (pieces - 1) // 2
    width = out.shape[3] // 2
    per = LANES // width

    def enter(strip, carry):
        here = pl.ds(pl.multiple_of(strip * 8, 8), 8)
        lane = lax.broadcasted_iota(jnp.int32, (8, LANES), 1)
        ramp = jnp.where(lane < OVL, ramp_of(lane), 1.0)
        rest = 1.0 - ramp
        segments = []
        for tile in range(tiles):
            halo = values[(tile - 1) % tiles, 2 * whole, here, :]
            for chunk in range(whole):
                real = values[tile, chunk, here, :]
                imag = values[tile, whole + chunk, here, :]
                if chunk == 0:
                    real = ramp * real + rest * halo
                    imag = ramp * imag + rest * pltpu.roll(halo, OVL, 1)
                segments.append((real, imag))
        for index, (real, imag) in enumerate(short_fft(segments, -1)):
            held[index, here, pl.ds(0, LANES)] = real
            held[index, here, pl.ds(LANES, LANES)] = imag
        return carry

    lax.fori_loop(0, rows // 8, enter, 0)

    def multiply(index, carry):
        value = held[index]
        high = value.astype(BF16)
        both = jnp.concatenate([value, value - high.astype(F32)], axis=0).astype(BF16)
        main = jnp.dot(both, high_table[index], preferred_element_type=F32)
        rest = jnp.dot(high, low_table[index], preferred_element_type=F32)
        held[index] = main[:rows] + (main[rows:] + rest)
        return carry

    lax.fori_loop(0, tiles * whole, multiply, 0)

    def leave(strip, carry):
        here = pl.ds(pl.multiple_of(strip * 8, 8), 8)
        segments = [
            (held[index, here, pl.ds(0, LANES)], held[index, here, pl.ds(LANES, LANES)])
            for index in range(tiles * whole)
        ]
        for index, (real, imag) in enumerate(short_fft(segments, 1)):
            tile, chunk = index // whole, index % whole
            for piece in range(per):
                cut = slice(piece * width, (piece + 1) * width)
                out[chunk * per + piece, tile, here, pl.ds(0, width)] = real[:, cut]
                out[chunk * per + piece, tile, here, pl.ds(width, width)] = imag[:, cut]
        return carry

    lax.fori_loop(0, rows // 8, leave, 0)


def row_kernel(values, high_table, low_table, out, held):
    tiles, _, both = values.shape
    width = both // 2
    stride = out.shape[1]
    part = high_table.shape[1] // 2
    whole = stride // part

    def enter(strip, carry):
        segments = []
        for tile in range(tiles):
            for chunk in range(whole):
                here = pl.ds(pl.multiple_of(chunk * part + strip * 8, 8), 8)
                value = values[tile, here, :]
                if chunk == 0:
                    row = strip * 8 + lax.broadcasted_iota(jnp.int32, (8, both), 0)
                    ramp = jnp.where(row < OVL, ramp_of(row), 1.0)
                    behind = pl.ds(pl.multiple_of(stride + jnp.minimum(strip * 8, OVL - 8), 8), 8)
                    prior = values[(tile - 1) % tiles, behind, :]
                    value = jnp.where(row < OVL, ramp * value + (1.0 - ramp) * prior, value)
                segments.append((value[:, :width], value[:, width:]))
        for index, (real, imag) in enumerate(short_fft(segments, -1)):
            held[index, pl.ds(pl.multiple_of(strip * 8, 8), 8), :] = real
            held[index, pl.ds(pl.multiple_of(part + strip * 8, 8), 8), :] = imag
        return carry

    lax.fori_loop(0, part // 8, enter, 0)

    def multiply(index, carry):
        high, low = split(held[index])
        main = jnp.dot(
            high_table[index], jnp.concatenate([high, low], axis=1), preferred_element_type=F32
        )
        rest = jnp.dot(low_table[index], high, preferred_element_type=F32)
        held[index] = main[:, :width] + (main[:, width:] + rest)
        return carry

    lax.fori_loop(0, tiles * whole, multiply, 0)

    def leave(strip, carry):
        segments = [
            (
                held[index, pl.ds(pl.multiple_of(strip * 8, 8), 8), :],
                held[index, pl.ds(pl.multiple_of(part + strip * 8, 8), 8), :],
            )
            for index in range(tiles * whole)
        ]
        for index, (real, imag) in enumerate(short_fft(segments, 1)):
            tile, chunk = index // whole, index % whole
            here = pl.ds(pl.multiple_of(chunk * part + strip * 8, 8), 8)
            out[tile, here, pl.ds(0, width)] = real
            out[tile, here, pl.ds(width, width)] = imag
        return carry

    lax.fori_loop(0, part // 8, leave, 0)


VMEM = pl.BlockSpec(memory_space=pltpu.VMEM)
SMEM = pl.BlockSpec(memory_space=pltpu.SMEM)


def call(kernel, shape, scratch, limit, *operands, specs=None):
    return pl.pallas_call(
        kernel,
        out_shape=jax.ShapeDtypeStruct(shape, F32),
        in_specs=specs or [VMEM] * len(operands),
        out_specs=VMEM,
        scratch_shapes=scratch,
        compiler_params=pltpu.CompilerParams(vmem_limit_bytes=limit << 20),
    )(*operands)


def local(row_count, col_count, tiles, pupils, intensity, offsets):
    length = tiles.shape[1]
    window = pupils.shape[1]
    leds = intensity.shape[0]
    stride = length - OVL
    whole = stride // LANES
    chunks = whole + 1
    rows = -(-length // (8 * col_count)) * 8
    width = stride // row_count
    fresnel = stride * row_count // 2
    fore, back = dft_matrix(window, -1), dft_matrix(window, 1)
    part = length // RADIX
    field = call(
        refine_kernel,
        (col_count, 2 * whole + 1, rows, LANES),
        [
            pltpu.VMEM((2, chunks, length, LANES), F32),
            pltpu.VMEM((2, chunks, length, LANES), F32),
            pltpu.VMEM((RADIX, 6 * part, chunks * LANES), BF16),
            pltpu.VMEM((leds, 2, window, window), F32),
        ],
        56,
        offsets[0, 0],
        tiles,
        pupils,
        intensity,
        tile_tables(length, -1),
        tile_tables(length, 1),
        along_right(right_block(back)),
        along_left(left_block(back)),
        along_right(right_block(fore)),
        along_left(left_block(fore)),
        specs=[SMEM] + [VMEM] * 9,
    )
    field = lax.all_to_all(field, "col", split_axis=0, concat_axis=0, tiled=True)
    col_classes = col_count * whole
    field = call(
        col_kernel,
        (row_count, col_count, rows, 2 * width),
        [pltpu.VMEM((col_classes, rows, 2 * LANES), F32)],
        40,
        field,
        *spread_tables(stride * col_count, fresnel, col_classes, lambda m: right_block(m.T)),
    )
    field = lax.all_to_all(
        field.reshape(row_count * col_count, rows, 2 * width),
        ("row", "col"),
        split_axis=0,
        concat_axis=0,
        tiled=True,
    )
    row_classes = row_count * whole
    field = call(
        row_kernel,
        (row_count, stride, 2 * width),
        [pltpu.VMEM((row_classes, 2 * LANES, width), F32)],
        40,
        field.reshape(row_count, col_count * rows, 2 * width),
        *spread_tables(stride * row_count, fresnel, row_classes, left_block),
    )
    field = lax.all_to_all(field, "row", split_axis=0, concat_axis=0, tiled=True)
    field = field.reshape(row_count, stride, 2, width).transpose(2, 1, 0, 3)
    return field.reshape(2, stride, stride)


def solution(mesh):
    placed = (
        P(None, "row", "col"),
        P(None, "row", "col"),
        P(None, "row", "col"),
        P("row", "col", None, None),
    )
    return jax.shard_map(
        functools.partial(local, mesh.shape["row"], mesh.shape["col"]),
        mesh=mesh,
        in_specs=placed,
        out_specs=P(None, "row", "col"),
        check_vma=False,
    )
```

time: 925 us -> 191 us (0.21); the launches traced: 910 us -> 188 us
  matrix products: 353 us -> 0 us
  waiting for transfers between devices: 135 us -> 0 us
  local copies, waits for them, and re-layouts: 135 us -> 6.86 us
  loops' own time: 59.4 us -> 0 us
  Pallas kernels: 0 us -> 35.8 us
  blocking collectives: 180 us -> 145 us
  other arithmetic: 27.7 us -> 0 us
  starting transfers between devices: 18.4 us -> 0 us
    dot_general x64 -> x0, matrix products: 353 us -> none  [product(): return jnp.einsum(form, left, right, precision=lax.Precision.HIGHEST)]
    all_to_all x4 -> x0, waiting for transfers between devices: 122 us -> none  [the longest x3 78.9 us: column_swap(): lax.all_to_all(values, 'col', split_axis=2, concat_axis=2, tiled=True)]
    another operation x2 -> x0, loops' own time: 59.4 us -> none  [the longest x1 59.1 us: local(): total = lax.fori_loop(0, led_count, place, jnp.zeros_like(spectrum))]
    gather x48 -> x0, local copies, waits for them, and re-layouts: 46.4 us -> none
    dynamic_update_slice x16 -> x0, local copies, waits for them, and re-layouts: 39.1 us -> none  [place(): return lax.dynamic_update_slice(total, current + updates[led], corner)]
    pallas_call x0 -> x3, Pallas kernels: none -> 35.8 us  [call(): pl.pallas_call(kernel, out_shape=jax.ShapeDtypeStruct(shape, F32), in_spe...]
    all_to_all x4 -> x3, blocking collectives: 180 us -> 145 us  [the longest x1 58.6 us: local(): lax.all_to_all(field.reshape(row_count * col_count, rows, 2 * width), ('r...]
    all_to_all x4 -> x0, starting transfers between devices: 17.1 us -> none  [the longest x3 11.3 us: column_swap(): lax.all_to_all(values, 'col', split_axis=2, concat_axis=2, tiled=True)]
  transfers between devices with their start and end apart: 6 -> 0, of which waited for: 6 -> 0; matrix products, arithmetic and copies ran while one was open for 0% -> 0% of each run, Pallas kernels for 0% -> 0%
where the time goes in v1:
time: 191 us; the launch traced here: 188 us
  blocking collectives  145 us (76%)
  Pallas kernels  35.8 us (19%)
  local copies, waits for them, and re-layouts  6.86 us (4%)
    all_to_all x1, blocking collectives, local(): lax.all_to_all(field.reshape(row_count * col_count, rows, 2 * width), ('r...  58.6 us
    all_to_all x1, blocking collectives, local(): lax.all_to_all(field, 'row', split_axis=0, concat_axis=0, tiled=True)  50 us
    all_to_all x1, blocking collectives, local(): lax.all_to_all(field, 'col', split_axis=0, concat_axis=0, tiled=True)  36.5 us
    pallas_call x3, Pallas kernels, call(): pl.pallas_call(kernel, out_shape=jax.ShapeDtypeStruct(shape, F32), in_spe...  35.8 us

profile of v1, /device:TPU:8, one launch (start us, length us, event | category | flops | bytes accessed | tf_op | source)
XLA Modules:
  0.0 187.9 jit_solution(12815443724040781638)
XLA Ops:
  0.0 0.0 copy-start.1
  0.0 22.8 %shard_map.136 = f32[8,9,72,128]{3,2,1,0:T(8,128)} custom-call(s32[2,16]{1,0:T(2,128)} %bitcast.7, f32[2,576,576]{2,1,0:T(8,128)} %tiles.1, f32[2,128,128]{2,1,0:T(8,128)} %pupils.1, f32[16,128,128]{2,1,0:T(8,128)} %intensity.1, bf16[4,288,864]{2,1,0:T(8,128)(2,1)} %constant.20.clone.to_spectrum, bf16[4,288,864]{2,1,0:T(8,128)(2,1)} %constant.21.clone.to_object, ...), custom_call_target="tpu_custom_call" | custom-call | tf_op jit(solution)/shard_map/pallas_call | solution.py:387
  22.8 0.0 copy-start
  22.8 36.5 %all_to_all.15.values = f32[8,9,72,128]{3,2,1,0:T(8,128)S(1)} all-to-all(f32[8,9,72,128]{3,2,1,0:T(8,128)} %shard_map.136), channel_id=1, replica_groups=mesh['row'=4,'col'=8] {'col'}, dimensions={0} | all-to-all | bytes 5308416 | tf_op jit(solution)/shard_map/all_to_all | solution.py:431
  59.4 0.0 copy-done.1
  59.4 0.0 copy-done
  59.4 8.0 %shard_map.137 = f32[4,8,72,256]{3,2,1,0:T(8,128)S(1)} custom-call(f32[8,9,72,128]{3,2,1,0:T(8,128)S(1)} %all_to_all.15.values, bf16[32,256,256]{2,1,0:T(8,128)(2,1)S(1)} %copy-done.1, bf16[32,256,256]{2,1,0:T(8,128)(2,1)S(1)} %copy-done), custom_call_target="tpu_custom_call" | custom-call | tf_op jit(solution)/shard_map/pallas_call | solution.py:387
  67.4 0.0 copy-start.2
  67.4 0.0 copy-start.3
  67.4 58.6 %all_to_all.16 = f32[32,72,256]{2,1,0:T(8,128)S(1)} all-to-all(f32[32,72,256]{2,1,0:T(8,128)S(1)} %bitcast.4), channel_id=1, replica_groups=mesh['row'=4,'col'=8] {'row','col'}, dimensions={0} | all-to-all | bytes 4718592 | tf_op jit(solution)/shard_map/all_to_all | solution.py:441
  126.0 0.0 copy-done.2
  126.0 0.0 copy-done.3
  126.0 5.0 %shard_map.138 = f32[4,512,256]{2,1,0:T(8,128)S(1)} custom-call(f32[4,576,256]{2,1,0:T(8,128)S(1)} %bitcast.5, bf16[16,256,256]{2,1,0:T(8,128)(2,1)S(1)} %copy-done.3, bf16[16,256,256]{2,1,0:T(8,128)(2,1)S(1)} %copy-done.2), custom_call_target="tpu_custom_call" | custom-call | tf_op jit(solution)/shard_map/pallas_call | solution.py:387
  131.1 50.0 %all_to_all.17 = f32[4,512,256]{2,1,0:T(8,128)S(1)} all-to-all(f32[4,512,256]{2,1,0:T(8,128)S(1)} %shard_map.138), channel_id=1, replica_groups=mesh['row'=4,'col'=8] {'row'}, dimensions={0} | all-to-all | bytes 4194304 | tf_op jit(solution)/shard_map/all_to_all | solution.py:457
  181.1 2.1 %reshape.14 = f32[4,512,2,128]{3,2,1,0:T(2,128)} reshape(f32[4,512,256]{2,1,0:T(8,128)S(1)} %all_to_all.17) | data formatting | bytes 4194304 | tf_op jit(solution)/shard_map/reshape | solution.py:458
  183.1 2.9 %copy.15 = f32[2,512,4,128]{3,2,1,0:T(4,128)S(1)} copy(f32[2,512,4,128]{3,0,1,2:T(2,128)} %bitcast.6) | data formatting | bytes 4194304 | tf_op jit(solution)/shard_map/transpose | solution.py:458
  186.1 1.8 reshape.15
Async XLA Ops:
  0.0 59.4 %copy-start.1 = (bf16[32,256,256]{2,1,0:T(8,128)(2,1)S(1)}, bf16[32,256,256]{2,1,0:T(8,128)(2,1)}, u32[]{:S(2)}) copy-start(bf16[32,256,256]{2,1,0:T(8,128)(2,1)} %constant.26.clone.high_table) | copy-start | bytes 12582916
  22.8 36.5 %copy-start = (bf16[32,256,256]{2,1,0:T(8,128)(2,1)S(1)}, bf16[32,256,256]{2,1,0:T(8,128)(2,1)}, u32[]{:S(2)}) copy-start(bf16[32,256,256]{2,1,0:T(8,128)(2,1)} %constant.27.clone.low_table) | copy-start | bytes 12582916
  67.4 58.7 %copy-start.2 = (bf16[16,256,256]{2,1,0:T(8,128)(2,1)S(1)}, bf16[16,256,256]{2,1,0:T(8,128)(2,1)}, u32[]{:S(2)}) copy-start(bf16[16,256,256]{2,1,0:T(8,128)(2,1)} %constant.29.clone.low_table) | copy-start | bytes 6291460
  67.4 58.6 %copy-start.3 = (bf16[16,256,256]{2,1,0:T(8,128)(2,1)S(1)}, bf16[16,256,256]{2,1,0:T(8,128)(2,1)}, u32[]{:S(2)}) copy-start(bf16[16,256,256]{2,1,0:T(8,128)(2,1)} %constant.28.clone.high_table) | copy-start | bytes 6291460

commit v2 on v1

v2 whole, which is shorter than its diff:
```python
import functools
import math

import jax
import jax.numpy as jnp
import ml_dtypes
import numpy as np
from jax import lax
from jax.experimental import pallas as pl
from jax.experimental.pallas import tpu as pltpu
from jax.sharding import PartitionSpec as P

OVL = 64
STEP_SIZE = 0.05
LANES = 128
RADIX = 8
BF16 = jnp.bfloat16
F32 = jnp.float32


def halves(table):
    table = np.asarray(table, np.float64)
    high = table.astype(np.float32).astype(ml_dtypes.bfloat16)
    low = (table - high.astype(np.float64)).astype(np.float32).astype(ml_dtypes.bfloat16)
    return high, low


def left_half(matrix):
    return np.concatenate([matrix.real, matrix.imag], axis=0)


def right_half(matrix):
    return np.concatenate([matrix.real, matrix.imag], axis=1)


def left_block(matrix):
    return np.block([[matrix.real, -matrix.imag], [matrix.imag, matrix.real]])


def right_block(matrix):
    return np.block([[matrix.real, matrix.imag], [-matrix.imag, matrix.real]])


def along_left(block):
    high, low = halves(block)
    return np.concatenate([high, high, low], axis=-1)


def along_right(block):
    high, low = halves(block)
    return np.concatenate([high, high, low], axis=-2)


def dft_matrix(length):
    index = np.arange(length)
    turns = (index[:, None] * index[None, :]) % length
    return np.exp(-2j * np.pi * turns / length) / math.sqrt(length)


def tile_tables(length):
    part = length // RADIX
    index = np.arange(part)
    tables = []
    for residue in range(RADIX):
        turns = (index[None, :] * (residue + RADIX * index[:, None])) % length
        matrix = np.exp(-2j * np.pi * turns / length) / math.sqrt(length)
        tables.append(along_left(left_half(matrix)))
    return np.stack(tables)


def spread_tables(length, fresnel, count, block_of):
    signed = np.arange(length, dtype=np.float64)
    signed = np.where(signed < length // 2, signed, signed - length)
    square = signed * signed
    turns = square * (fresnel / (length * length))
    turns = turns - np.floor(turns)
    kernel = np.fft.ifft(np.exp(-2.0 * square / (length * length)) * np.exp(-2j * np.pi * turns))
    part = length // count
    shift = np.arange(part)[:, None] - np.arange(part)[None, :]
    places = (np.arange(count)[:, None] * part + np.arange(1 - part, part)[None, :]) % length
    classes = np.fft.fft(kernel[places], axis=0) / count
    pairs = [halves(block_of(line[shift + part - 1])) for line in classes]
    return np.stack([np.stack([pair[0] for pair in pairs]), np.stack([pair[1] for pair in pairs])])


def split(value):
    high = value.astype(BF16)
    low = (value - high.astype(F32)).astype(BF16)
    return high, low


def turned(value, eighth_turns, sign):
    real, imag = value
    angle = sign * 2.0 * math.pi * eighth_turns
    if eighth_turns == 0:
        return real, imag
    if eighth_turns == 0.25:
        return (imag, -real) if sign < 0 else (-imag, real)
    cosine, sine = math.cos(angle), math.sin(angle)
    return real * cosine - imag * sine, real * sine + imag * cosine


def short_fft(values, sign):
    count = len(values)
    if count == 1:
        return values
    even = short_fft(values[0::2], sign)
    odd = short_fft(values[1::2], sign)
    low, high = [], []
    for index in range(count // 2):
        real, imag = turned(odd[index], index / count, sign)
        low.append((even[index][0] + real, even[index][1] + imag))
        high.append((even[index][0] - real, even[index][1] - imag))
    return low + high


def tile_pass(load, target, table, sign):
    part = table.shape[1] // 2
    for chunk in range(target.shape[1]):
        values = [
            tuple(load(side, chunk, pl.ds(part * step, part)) for side in range(2))
            for step in range(RADIX)
        ]
        for residue, value in enumerate(short_fft(values, sign)):
            value = jnp.concatenate(value, axis=1)
            high = value.astype(BF16).astype(F32)
            stacked = jnp.concatenate([high, value - high, high], axis=0).astype(BF16)
            result = jnp.dot(table[residue], stacked, preferred_element_type=F32)
            plain, crossed = result[:part], result[part:]
            real, imag = plain[:, :LANES], plain[:, LANES:]
            if sign < 0:
                real, imag = real - crossed[:, LANES:], imag + crossed[:, :LANES]
            else:
                real, imag = real + crossed[:, LANES:], imag - crossed[:, :LANES]
            rows = pl.ds(residue, part, stride=RADIX)
            target[0, chunk, rows, :] = real
            target[1, chunk, rows, :] = imag


def transpose_all(source, target):
    chunks, length = source.shape[1], source.shape[2]
    for side in range(2):
        for chunk in range(chunks):
            rows = min(LANES, length - chunk * LANES)
            for other in range(chunks):
                width = min(LANES, length - other * LANES)
                block = source[side, chunk, pl.ds(other * LANES, width), :]
                target[side, other, pl.ds(chunk * LANES, rows), pl.ds(0, width)] = block.T[:rows]


def refine_kernel(starts, *refs):
    sources, (late, early, below), refs = refs[:6], refs[6:9], refs[9:]
    held, (first, second, updates, done) = refs[:6], refs[6:]
    tiles, table, pupils, intensity, row_table, col_table = held
    copies = [
        pltpu.make_async_copy(source, target, done.at[place])
        for place, (source, target) in enumerate(zip(sources, held))
    ]
    for copy in copies:
        copy.start()
    length = tiles.shape[1]
    window = pupils.shape[1]
    leds = intensity.shape[0]
    chunks = first.shape[1]
    rest = length - (chunks - 1) * LANES
    copies[0].wait()
    for side in range(2):
        second[side, chunks - 1, :, pl.ds(0, rest)] = tiles[side, :, pl.ds((chunks - 1) * LANES, rest)]

    def from_tiles(side, chunk, rows):
        if chunk == chunks - 1:
            return second[side, chunk, rows, :]
        return tiles[side, rows, pl.ds(chunk * LANES, LANES)]

    def from_first(side, chunk, rows):
        return first[side, chunk, rows, :]

    def from_second(side, chunk, rows):
        return second[side, chunk, rows, :]

    copies[1].wait()
    tile_pass(from_tiles, first, table, -1)
    transpose_all(first, second)
    tile_pass(from_second, first, table, -1)
    for copy in copies[2:]:
        copy.wait()
    lens_real, lens_imag = pupils[0].T, pupils[1].T
    lane = lax.broadcasted_iota(jnp.int32, (window, LANES), 1)
    group = 8 if leds % 8 == 0 else 1

    def place_of(led):
        start = starts[0, led]
        chunk = start // LANES
        return chunk, start - chunk * LANES, starts[1, led]

    def along_rows(value):
        high, low = split(value)
        return jnp.dot(
            jnp.concatenate([high, low, high], axis=1), row_table[...], preferred_element_type=F32
        )

    def along_cols(value):
        high, low = split(value)
        return jnp.dot(
            col_table[...], jnp.concatenate([high, low, high], axis=0), preferred_element_type=F32
        )

    def step(index, carry):
        crops = []
        for member in range(group):
            chunk, shift, row = place_of(index * group + member)
            crop = []
            for side in range(2):
                here = first[side, chunk, pl.ds(row, window), :]
                beyond = first[side, chunk + 1, pl.ds(row, window), :]
                joined = jnp.where(lane >= shift, here, beyond)
                crop.append(pltpu.roll(joined, lax.rem(LANES - shift, LANES), 1))
            crops.append(
                jnp.concatenate(
                    [
                        lens_real * crop[0] - lens_imag * crop[1],
                        -lens_real * crop[1] - lens_imag * crop[0],
                    ],
                    axis=1,
                )
            )
        wave = along_rows(jnp.concatenate(crops, axis=0))
        blocks = [wave[m * window : (m + 1) * window] for m in range(group)]
        blocks = [jnp.concatenate([b[:, :window], b[:, window:]], axis=0) for b in blocks]
        wave = along_cols(jnp.concatenate(blocks, axis=1))
        real, imag = wave[:window], wave[window:]
        measured = jnp.concatenate([intensity[index * group + m].T for m in range(group)], axis=1)
        excess = real * real + imag * imag - measured
        grad = along_cols(jnp.concatenate([real * excess, -imag * excess], axis=0))
        blocks = [grad[:, m * window : (m + 1) * window] for m in range(group)]
        blocks = [jnp.concatenate([b[:window], b[window:]], axis=1) for b in blocks]
        grad = along_rows(jnp.concatenate(blocks, axis=0))
        for m in range(group):
            real = grad[m * window : (m + 1) * window, :window]
            imag = grad[m * window : (m + 1) * window, window:]
            led = index * group + m
            updates[led, 0] = -STEP_SIZE * (lens_real * real + lens_imag * imag)
            updates[led, 1] = -STEP_SIZE * (lens_real * imag - lens_imag * real)
        return carry

    lax.fori_loop(0, leds // group, step, 0)

    def place(led, carry):
        chunk, shift, row = place_of(led)
        for side in range(2):
            moved = pltpu.roll(updates[led, side], shift, 1)
            first[side, chunk, pl.ds(row, window), :] += jnp.where(lane >= shift, moved, 0.0)
            first[side, chunk + 1, pl.ds(row, window), :] += jnp.where(lane >= shift, 0.0, moved)
        return carry

    lax.fori_loop(0, leds, place, 0, unroll=4)
    tile_pass(from_first, second, table, 1)
    transpose_all(second, first)
    tile_pass(from_first, second, table, 1)
    whole = (length - OVL) // LANES
    count, _, rows, _ = late.shape

    def emit(target, part, row, gain):
        here = pl.ds(row, rows)
        for side in range(2):
            for chunk in range(whole):
                target[part, side * whole + chunk] = scaled(second[side, chunk, here, :], gain)
        near = second[0, whole, here, :]
        far = pltpu.roll(second[1, whole, here, :], OVL, 1)
        low = lax.broadcasted_iota(jnp.int32, near.shape, 1) < OVL
        target[part, 2 * whole] = scaled(jnp.where(low, near, far), gain)

    for part in range(count):
        segment, offset = divmod(part * rows, OVL)
        emit(late, part, segment * LANES + OVL + offset, None)
        ramp = None
        if segment == 0:
            ramp = ramp_of(offset + lax.broadcasted_iota(jnp.int32, (rows, LANES), 0))
            emit(below, part, whole * LANES + offset, 1.0 - ramp)
        emit(early, part, segment * LANES + offset, ramp)


def scaled(value, gain):
    return value if gain is None else value * gain


def ramp_of(index):
    return (index.astype(F32) + 0.5) / OVL


def spread_kernel(place, early, above, *outs):
    blended = above.shape[0]
    for step, out in enumerate(outs):
        part = jnp.bitwise_xor(place[0], step)
        out[...] = early[part]

        @pl.when(part < blended)
        def _():
            out[...] += above[jnp.minimum(part, blended - 1)]


UNROLL = 4


class Fetch:
    def __init__(self, source, target, done):
        self.parts = done.shape[0]
        self.each = source.shape[1] // self.parts
        self.copies = [
            pltpu.make_async_copy(
                source.at[:, pl.ds(part * self.each, self.each)],
                target.at[:, pl.ds(part * self.each, self.each)],
                done.at[part],
            )
            for part in range(self.parts)
        ]
        for copy in self.copies:
            copy.start()

    def each_class(self, body):
        for part in range(self.parts):
            self.copies[part].wait()
            lax.fori_loop(part * self.each, (part + 1) * self.each, body, 0, unroll=UNROLL)


def col_kernel(place, late, *refs):
    *blocks, table_source, out, early, held, table, done = refs
    fetch = Fetch(table_source, table, done)
    for step, block in enumerate(blocks):
        early[jnp.bitwise_xor(place[0], step)] = block[...]
    tiles, pieces, half, _ = late.shape
    rows = 2 * half
    whole = (pieces - 1) // 2
    width = out.shape[3] // 2
    per = LANES // width

    def enter_from(values, first):
        def enter(strip, carry):
            here = pl.ds(pl.multiple_of(strip * 8, 8), 8)
            lane = lax.broadcasted_iota(jnp.int32, (8, LANES), 1)
            ramp = jnp.where(lane < OVL, ramp_of(lane), 1.0)
            rest = 1.0 - ramp
            segments = []
            for tile in range(tiles):
                halo = values[(tile - 1) % tiles, 2 * whole, here, :]
                for chunk in range(whole):
                    real = values[tile, chunk, here, :]
                    imag = values[tile, whole + chunk, here, :]
                    if chunk == 0:
                        real = ramp * real + rest * halo
                        imag = ramp * imag + rest * pltpu.roll(halo, OVL, 1)
                    segments.append((real, imag))
            here = pl.ds(pl.multiple_of(first + strip * 8, 8), 8)
            for index, (real, imag) in enumerate(short_fft(segments, -1)):
                held[index, 0, here, :] = real
                held[index, 1, here, :] = imag
            return carry

        lax.fori_loop(0, half // 8, enter, 0)

    enter_from(late, 0)
    enter_from(early, half)

    def multiply(index, carry):
        value = held[index].reshape(2 * rows, LANES)
        high = value.astype(BF16)
        both = jnp.concatenate([value, value - high.astype(F32)], axis=0).astype(BF16)
        main = jnp.dot(both, table[0, index], preferred_element_type=F32)
        rest = jnp.dot(high, table[1, index], preferred_element_type=F32)
        full = main[: 2 * rows] + (main[2 * rows :] + rest)
        held[index, 0] = full[:rows, :LANES] - full[rows:, LANES:]
        held[index, 1] = full[:rows, LANES:] + full[rows:, :LANES]
        return carry

    fetch.each_class(multiply)

    def leave(strip, carry):
        here = pl.ds(pl.multiple_of(strip * 8, 8), 8)
        segments = [
            (held[index, 0, here, :], held[index, 1, here, :]) for index in range(tiles * whole)
        ]
        for index, (real, imag) in enumerate(short_fft(segments, 1)):
            tile, chunk = index // whole, index % whole
            for piece in range(per):
                cut = slice(piece * width, (piece + 1) * width)
                out[chunk * per + piece, tile, here, pl.ds(0, width)] = real[:, cut]
                out[chunk * per + piece, tile, here, pl.ds(width, width)] = imag[:, cut]
        return carry

    lax.fori_loop(0, rows // 8, leave, 0)


def row_kernel(half, place, values, table_source, *refs):
    *outs, out, held, table, done = refs
    fetch = Fetch(table_source, table, done)
    tiles, _, both = values.shape
    width = both // 2
    stride = out.shape[1]
    part = table.shape[3]
    whole = stride // part

    def enter_from(offset, first):
        def enter(strip, carry):
            segments = []
            for tile in range(tiles):
                for chunk in range(whole):
                    row = chunk * OVL + strip * 8
                    row = row // half * (2 * half) + lax.rem(row, half) + offset
                    value = values[tile, pl.ds(pl.multiple_of(row, 8), 8), :]
                    segments.append((value[:, :width], value[:, width:]))
            here = pl.ds(pl.multiple_of(first + strip * 8, 8), 8)
            for index, (real, imag) in enumerate(short_fft(segments, -1)):
                held[index, here, pl.ds(0, width)] = real
                held[index, here, pl.ds(width, width)] = imag
            return carry

        lax.fori_loop(0, OVL // 8, enter, 0)

    enter_from(half, 0)
    enter_from(0, OVL)

    def multiply(index, carry):
        high, low = split(held[index])
        main = jnp.dot(
            table[0, index], jnp.concatenate([high, low], axis=1), preferred_element_type=F32
        )
        rest = jnp.dot(table[1, index], high, preferred_element_type=F32)
        full = main[:, :both] + (main[:, both:] + rest)
        held[index, :, pl.ds(0, width)] = full[:part, :width] - full[part:, width:]
        held[index, :, pl.ds(width, width)] = full[:part, width:] + full[part:, :width]
        return carry

    fetch.each_class(multiply)

    def leave(strip, carry):
        here = pl.ds(pl.multiple_of(strip * 8, 8), 8)
        segments = []
        for index in range(tiles * whole):
            value = held[index, here, :]
            segments.append((value[:, :width], value[:, width:]))
        for index, (real, imag) in enumerate(short_fft(segments, 1)):
            tile, chunk = index // whole, index % whole
            here = pl.ds(pl.multiple_of(chunk * part + strip * 8, 8), 8)
            out[tile, here, pl.ds(0, width)] = real
            out[tile, here, pl.ds(width, width)] = imag
        return carry

    lax.fori_loop(0, part // 8, leave, 0)
    for step, target in enumerate(outs):
        target[...] = out[jnp.bitwise_xor(place[1], step)]


def join_kernel(place, *refs):
    *blocks, out, ordered = refs
    count, _, both = ordered.shape
    width = both // 2
    for step, block in enumerate(blocks):
        part = jnp.bitwise_xor(place[1], step)
        if width % LANES:
            ordered[part] = block[...]
            continue
        for side in range(2):
            lanes = pl.ds(pl.multiple_of(part * width, LANES), width)
            out[side, :, lanes] = block[:, pl.ds(side * width, width)]
    if width % LANES:
        for part in range(count):
            for side in range(2):
                out[side, :, pl.ds(part * width, width)] = ordered[part, :, pl.ds(side * width, width)]


VMEM = pl.BlockSpec(memory_space=pltpu.VMEM)
SMEM = pl.BlockSpec(memory_space=pltpu.SMEM)
HBM = pl.BlockSpec(memory_space=pltpu.HBM)


def call(kernel, shapes, scratch, limit, micros, *operands, scalars=0, outside=()):
    return pl.pallas_call(
        kernel,
        out_shape=[jax.ShapeDtypeStruct(shape, F32) for shape in shapes],
        in_specs=[
            SMEM if place < scalars else HBM if place - len(operands) in outside else VMEM
            for place in range(len(operands))
        ],
        out_specs=[VMEM] * len(shapes),
        scratch_shapes=scratch,
        cost_estimate=pl.CostEstimate(
            flops=int(micros * 5e8), bytes_accessed=int(micros * 2e6), transcendentals=0
        ),
        compiler_params=pltpu.CompilerParams(vmem_limit_bytes=limit << 20),
    )(*operands)


def local(row_count, col_count, tiles, pupils, intensity, offsets):
    length = tiles.shape[1]
    window = pupils.shape[1]
    leds = intensity.shape[0]
    stride = length - OVL
    whole = stride // LANES
    chunks = whole + 1
    rows = stride // (2 * col_count)
    width = stride // row_count
    fresnel = stride * row_count // 2
    block = (2 * whole + 1, rows, LANES)
    operands = (
        tiles,
        tile_tables(length),
        pupils,
        intensity,
        along_right(right_block(dft_matrix(window))),
        along_left(left_block(dft_matrix(window))),
    )
    buffer = pltpu.VMEM((2, chunks, length, LANES), F32)
    late, early, below = call(
        refine_kernel,
        [(col_count, *block), (col_count, *block), (OVL // rows, *block)],
        [pltpu.VMEM(operand.shape, operand.dtype) for operand in operands]
        + [
            buffer,
            buffer,
            pltpu.VMEM((leds, 2, window, window), F32),
            pltpu.SemaphoreType.DMA((len(operands),)),
        ],
        56,
        22,
        offsets[0, 0],
        *operands,
        scalars=1,
        outside=range(-len(operands), 0),
    )
    above = lax.ppermute(below, "row", [(r, (r + 1) % row_count) for r in range(row_count)])
    late = lax.all_to_all(late, "col", split_axis=0, concat_axis=0, tiled=True)
    place = jnp.stack([lax.axis_index("col"), lax.axis_index("row")]).astype(jnp.int32)
    early = call(spread_kernel, [block] * col_count, [], 16, 1, place, early, above, scalars=1)
    early = [early[0]] + [
        lax.ppermute(early[step], "col", [(c, c ^ step) for c in range(col_count)])
        for step in range(1, col_count)
    ]
    col_classes = col_count * whole
    table = spread_tables(stride * col_count, fresnel, col_classes, lambda m: right_half(m.T))
    (field,) = call(
        col_kernel,
        [(row_count, col_count, 2 * rows, 2 * width)],
        [
            pltpu.VMEM((col_count, *block), F32),
            pltpu.VMEM((col_classes, 2, 2 * rows, LANES), F32),
            pltpu.VMEM(table.shape, BF16),
            pltpu.SemaphoreType.DMA((4,)),
        ],
        32,
        5,
        place,
        late,
        *early,
        table,
        scalars=1,
        outside=(-1,),
    )
    field = field.reshape(row_count * col_count, 2 * rows, 2 * width)
    field = lax.all_to_all(field, ("row", "col"), split_axis=0, concat_axis=0, tiled=True)
    row_classes = row_count * whole
    table = spread_tables(stride * row_count, fresnel, row_classes, left_half)
    shape = (stride, 2 * width)
    blocks = call(
        functools.partial(row_kernel, rows),
        [shape] * row_count,
        [
            pltpu.VMEM((row_count, *shape), F32),
            pltpu.VMEM((row_classes, LANES, 2 * width), F32),
            pltpu.VMEM(table.shape, BF16),
            pltpu.SemaphoreType.DMA((4,)),
        ],
        32,
        5,
        place,
        field.reshape(row_count, col_count * 2 * rows, 2 * width),
        table,
        scalars=1,
        outside=(-1,),
    )
    blocks = [blocks[0]] + [
        lax.ppermute(blocks[step], "row", [(r, r ^ step) for r in range(row_count)])
        for step in range(1, row_count)
    ]
    (field,) = call(
        join_kernel,
        [(2, stride, stride)],
        [pltpu.VMEM((row_count, *shape), F32)],
        16,
        2,
        place,
        *blocks,
        scalars=1,
    )
    return field


def solution(mesh):
    placed = (
        P(None, "row", "col"),
        P(None, "row", "col"),
        P(None, "row", "col"),
        P("row", "col", None, None),
    )
    return jax.shard_map(
        functools.partial(local, mesh.shape["row"], mesh.shape["col"]),
        mesh=mesh,
        in_specs=placed,
        out_specs=P(None, "row", "col"),
        check_vma=False,
    )
```

time: 191 us -> 166 us (0.87); the launches traced: 188 us -> 166 us
  blocking collectives: 145 us -> 51.9 us
  waiting for transfers between devices: 0 us -> 65.5 us
  starting transfers between devices: 0 us -> 15.5 us
  Pallas kernels: 35.8 us -> 30.5 us
  local copies, waits for them, and re-layouts: 6.86 us -> 2.2 us
    all_to_all x3 -> x1, blocking collectives: 145 us -> 51.9 us  [local(): lax.all_to_all(field, ('row', 'col'), split_axis=0, concat_axis=0, tiled=...]
    ppermute x0 -> x11, waiting for transfers between devices: none -> 65.5 us  [the longest x3 45.5 us: local(): lax.ppermute(blocks[step], 'row', [(r, r ^ step) for r in range(row_count)])]
    ppermute x0 -> x11, starting transfers between devices: none -> 11.7 us  [the longest x7 6.47 us: local(): lax.ppermute(early[step], 'col', [(c, c ^ step) for c in range(col_count)])]
    pallas_call x3 -> x5, Pallas kernels: 35.8 us -> 30.5 us  [call(): pl.pallas_call(kernel, out_shape=[jax.ShapeDtypeStruct(shape, F32) for sh...]
    reshape x2 -> x0, local copies, waits for them, and re-layouts: 3.9 us -> none  [the longest x1 2.06 us: local(): field = field.reshape(row_count, stride, 2, width).transpose(2, 1, 0, 3)]
    all_to_all x0 -> x1, starting transfers between devices: none -> 3.88 us  [local(): late = lax.all_to_all(late, 'col', split_axis=0, concat_axis=0, tiled=True)]
    transpose x1 -> x0, local copies, waits for them, and re-layouts: 2.94 us -> none  [local(): field = field.reshape(row_count, stride, 2, width).transpose(2, 1, 0, 3)]
    unnamed x8, local copies, waits for them, and re-layouts: 0.02 us -> 2.2 us
  transfers between devices with their start and end apart: 0 -> 12, of which waited for: 0 -> 9; matrix products, arithmetic and copies ran while one was open for 0% -> 0% of each run, Pallas kernels for 0% -> 0%
where the time goes in v2:
time: 166 us
  waiting for transfers between devices  65.5 us (39%)
  blocking collectives  51.9 us (31%)
  Pallas kernels  30.5 us (18%)
  starting transfers between devices  15.5 us (9%)
  local copies, waits for them, and re-layouts  2.2 us (1%)
    all_to_all x1, blocking collectives, local(): lax.all_to_all(field, ('row', 'col'), split_axis=0, concat_axis=0, tiled=...  51.9 us
    ppermute x3, waiting for transfers between devices, local(): lax.ppermute(blocks[step], 'row', [(r, r ^ step) for r in range(row_count)])  45.5 us
    pallas_call x5, Pallas kernels, call(): pl.pallas_call(kernel, out_shape=[jax.ShapeDtypeStruct(shape, F32) for sh...  30.5 us
    ppermute x7, waiting for transfers between devices, local(): lax.ppermute(early[step], 'col', [(c, c ^ step) for c in range(col_count)])  12.4 us
    ppermute x1, waiting for transfers between devices, local(): lax.ppermute(below, 'row', [(r, (r + 1) % row_count) for r in range(row_c...  7.7 us
    ppermute x7, starting transfers between devices, local(): lax.ppermute(early[step], 'col', [(c, c ^ step) for c in range(col_count)])  6.47 us
    all_to_all x1, starting transfers between devices, local(): late = lax.all_to_all(late, 'col', split_axis=0, concat_axis=0, tiled=True)  3.88 us
    ppermute x3, starting transfers between devices, local(): lax.ppermute(blocks[step], 'row', [(r, r ^ step) for r in range(row_count)])  3.55 us
  transfers between devices with their start and end apart: 12, of which 9 were waited for; matrix products, arithmetic and copies ran while one was open for 0% of the time, Pallas kernels for 0%

profile of v2, /device:TPU:8, one launch (start us, length us, event | category | flops | bytes accessed | tf_op | source)
XLA Modules:
  0.0 165.8 jit_solution(16756954400233023697)
XLA Ops:
  0.0 17.6 %shard_map.91 = (f32[8,9,32,128]{3,2,1,0:T(8,128)}, f32[8,9,32,128]{3,2,1,0:T(8,128)}, f32[2,9,32,128]{3,2,1,0:T(8,128)}) custom-call(s32[2,16]{1,0:T(2,128)} %bitcast.7, f32[2,576,576]{2,1,0:T(8,128)} %refs_0_.1, bf16[8,144,216]{2,1,0:T(8,128)(2,1)} %constant.18.clone.refs_1_, f32[2,128,128]{2,1,0:T(8,128)} %refs_2_.1, f32[16,128,128]{2,1,0:T(8,128)} %refs_3_.1, ...), custom_call_target="tpu_custom_call" | custom-call | flops 11000000512 | bytes 44000000 | tf_op jit(solution)/shard_map/pallas_call | solution.py:477
  17.6 0.0 copy-start.3
  17.6 0.0 copy-start.2
  17.6 3.9 %all-to-all-start = ((f32[8,9,32,128]{3,2,1,0:T(8,128)}), f32[8,9,32,128]{3,2,1,0:T(8,128)S(1)}, u32[]{:S(2)}, u32[]{:S(2)}) async-start(f32[8,9,32,128]{3,2,1,0:T(8,128)} %get-tuple-element.20), calls=%async_computation | async-start | bytes 2359296 | tf_op jit(solution)/shard_map/all_to_all | solution.py:531
  21.5 0.0 copy-done.3
  21.5 1.6 collective-permute-start
  23.2 0.1 pad_add_fusion.place
  23.2 7.7 %collective-permute-done.above = f32[2,9,32,128]{3,2,1,0:T(8,128)S(1)} collective-permute-done((f32[2,9,32,128]{3,2,1,0:T(8,128)S(1)}, f32[2,9,32,128]{3,2,1,0:T(8,128)S(1)}, u32[]{:S(2)}, u32[]{:S(2)}) %collective-permute-start) | collective-permute-done | bytes 294944 | tf_op jit(solution)/shard_map/ppermute | solution.py:530
  30.9 0.0 copy-done.2
  30.9 0.7 shard_map.92
  31.7 0.1 collective-permute-start.1
  31.7 1.7 %collective-permute-start.2 = (f32[9,32,128]{2,1,0:T(8,128)S(1)}, f32[9,32,128]{2,1,0:T(8,128)S(1)}, u32[]{:S(2)}, u32[]{:S(2)}) collective-permute-start(f32[9,32,128]{2,1,0:T(8,128)S(1)} %get-tuple-element.25), channel_id=1, source_target_pairs={{0,2},{1,3},{2,0},{3,1},{4,6},{5,7},{6,4},{7,5},{8,10},{9,11},{10,... | collective-permute-start | bytes 442376 | tf_op jit(solution)/shard_map/ppermute | solution.py:535
  33.5 0.1 collective-permute-start.3
  33.6 1.7 %collective-permute-start.4 = (f32[9,32,128]{2,1,0:T(8,128)S(1)}, f32[9,32,128]{2,1,0:T(8,128)S(1)}, u32[]{:S(2)}, u32[]{:S(2)}) collective-permute-start(f32[9,32,128]{2,1,0:T(8,128)S(1)} %get-tuple-element.27), channel_id=1, source_target_pairs={{0,4},{1,5},{2,6},{3,7},{4,0},{5,1},{6,2},{7,3},{8,12},{9,13},{10,... | collective-permute-start | bytes 442376 | tf_op jit(solution)/shard_map/ppermute | solution.py:535
  35.3 0.0 collective-permute-start.5
  35.3 0.0 collective-permute-done.1.refs_1_
  35.3 2.6 %collective-permute-start.6 = (f32[9,32,128]{2,1,0:T(8,128)S(1)}, f32[9,32,128]{2,1,0:T(8,128)S(1)}, u32[]{:S(2)}, u32[]{:S(2)}) collective-permute-start(f32[9,32,128]{2,1,0:T(8,128)S(1)} %get-tuple-element.29), channel_id=1, source_target_pairs={{0,6},{1,7},{2,4},{3,5},{4,2},{5,3},{6,0},{7,1},{8,14},{9,15},{10,... | collective-permute-start | bytes 442376 | tf_op jit(solution)/shard_map/ppermute | solution.py:535
  37.9 3.2 %collective-permute-done.2.refs_2_ = f32[9,32,128]{2,1,0:T(8,128)S(1)} collective-permute-done((f32[9,32,128]{2,1,0:T(8,128)S(1)}, f32[9,32,128]{2,1,0:T(8,128)S(1)}, u32[]{:S(2)}, u32[]{:S(2)}) %collective-permute-start.2) | collective-permute-done | bytes 147488 | tf_op jit(solution)/shard_map/ppermute | solution.py:535
  41.1 0.3 collective-permute-start.7
  41.3 1.9 %collective-permute-done.3.refs_3_ = f32[9,32,128]{2,1,0:T(8,128)S(1)} collective-permute-done((f32[9,32,128]{2,1,0:T(8,128)S(1)}, f32[9,32,128]{2,1,0:T(8,128)S(1)}, u32[]{:S(2)}, u32[]{:S(2)}) %collective-permute-start.3) | collective-permute-done | bytes 147488 | tf_op jit(solution)/shard_map/ppermute | solution.py:535
  43.3 0.0 collective-permute-done.4.refs_4_
  43.3 1.7 %collective-permute-done.5.refs_5_ = f32[9,32,128]{2,1,0:T(8,128)S(1)} collective-permute-done((f32[9,32,128]{2,1,0:T(8,128)S(1)}, f32[9,32,128]{2,1,0:T(8,128)S(1)}, u32[]{:S(2)}, u32[]{:S(2)}) %collective-permute-start.5) | collective-permute-done | bytes 147488 | tf_op jit(solution)/shard_map/ppermute | solution.py:535
  45.0 3.3 %collective-permute-done.6.refs_6_ = f32[9,32,128]{2,1,0:T(8,128)S(1)} collective-permute-done((f32[9,32,128]{2,1,0:T(8,128)S(1)}, f32[9,32,128]{2,1,0:T(8,128)S(1)}, u32[]{:S(2)}, u32[]{:S(2)}) %collective-permute-start.6) | collective-permute-done | bytes 147488 | tf_op jit(solution)/shard_map/ppermute | solution.py:535
  48.3 2.2 %collective-permute-done.7.refs_7_ = f32[9,32,128]{2,1,0:T(8,128)S(1)} collective-permute-done((f32[9,32,128]{2,1,0:T(8,128)S(1)}, f32[9,32,128]{2,1,0:T(8,128)S(1)}, u32[]{:S(2)}, u32[]{:S(2)}) %collective-permute-start.7) | collective-permute-done | bytes 147488 | tf_op jit(solution)/shard_map/ppermute | solution.py:535
  50.5 0.0 all-to-all-done.late
  50.5 0.0 copy-start
  50.5 2.2 %copy-done = bf16[2,32,128,256]{3,2,1,0:T(8,128)(2,1)S(1)} copy-done((bf16[2,32,128,256]{3,2,1,0:T(8,128)(2,1)S(1)}, bf16[2,32,128,256]{3,2,1,0:T(8,128)(2,1)}, u32[]{:S(2)}) %copy-start) | copy-done | bytes 4194328
  52.7 5.5 %shard_map.93 = f32[4,8,64,256]{3,2,1,0:T(8,128)S(1)} custom-call(s32[2]{0:T(128)S(1)} %pad_add_fusion.place, f32[8,9,32,128]{3,2,1,0:T(8,128)S(1)} %all-to-all-done.late, f32[9,32,128]{2,1,0:T(8,128)S(1)} %get-tuple-element.23.refs_0_, f32[9,32,128]{2,1,0:T(8,128)S(1)} %collective-permute-done.1.refs_1_, f32[9,32,128]{2,1,0:T(8,128)S(1)} %collective-permute-done.2.refs_2_, ...), custom_call_target="tpu_custom_call" | custom-call | flops 2500000000 | bytes 10000000 | tf_op jit(solution)/shard_map/pallas_call | solution.py:477
  58.2 0.0 copy-start.1
  58.2 51.9 %all_to_all.10 = f32[32,64,256]{2,1,0:T(8,128)S(1)} all-to-all(f32[32,64,256]{2,1,0:T(8,128)S(1)} %bitcast.5), channel_id=1, replica_groups=mesh['row'=4,'col'=8] {'row','col'}, dimensions={0} | all-to-all | bytes 4194304 | tf_op jit(solution)/shard_map/all_to_all | solution.py:559
  110.1 0.0 copy-done.1
  110.1 4.5 %shard_map.94 = (f32[512,256]{1,0:T(8,128)S(1)}, f32[512,256]{1,0:T(8,128)S(1)}, f32[512,256]{1,0:T(8,128)S(1)}, f32[512,256]{1,0:T(8,128)S(1)}) custom-call(s32[2]{0:T(128)S(1)} %pad_add_fusion.place, f32[4,512,256]{2,1,0:T(8,128)S(1)} %bitcast.6, bf16[2,16,256,128]{3,2,1,0:T(8,128)(2,1)S(1)} %copy-done.1), custom_call_target="tpu_custom_call" | custom-call | flops 2500000000 | bytes 10000000 | tf_op jit(solution)/shard_map/pallas_call | solution.py:477
  114.6 1.3 collective-permute-start.8
  115.9 0.8 collective-permute-start.9
  116.7 1.5 collective-permute-start.10
  118.1 18.9 %collective-permute-done.8.refs_1_ = f32[512,256]{1,0:T(8,128)S(1)} collective-permute-done((f32[512,256]{1,0:T(8,128)S(1)}, f32[512,256]{1,0:T(8,128)S(1)}, u32[]{:S(2)}, u32[]{:S(2)}) %collective-permute-start.8) | collective-permute-done | bytes 524320 | tf_op jit(solution)/shard_map/ppermute | solution.py:581
  137.1 14.3 %collective-permute-done.9.refs_2_ = f32[512,256]{1,0:T(8,128)S(1)} collective-permute-done((f32[512,256]{1,0:T(8,128)S(1)}, f32[512,256]{1,0:T(8,128)S(1)}, u32[]{:S(2)}, u32[]{:S(2)}) %collective-permute-start.9) | collective-permute-done | bytes 524320 | tf_op jit(solution)/shard_map/ppermute | solution.py:581
  151.4 12.2 %collective-permute-done.10.refs_3_ = f32[512,256]{1,0:T(8,128)S(1)} collective-permute-done((f32[512,256]{1,0:T(8,128)S(1)}, f32[512,256]{1,0:T(8,128)S(1)}, u32[]{:S(2)}, u32[]{:S(2)}) %collective-permute-start.10) | collective-permute-done | bytes 524320 | tf_op jit(solution)/shard_map/ppermute | solution.py:581
  163.6 2.2 %shard_map.95 = f32[2,512,512]{2,1,0:T(8,128)} custom-call(s32[2]{0:T(128)S(1)} %pad_add_fusion.place, f32[512,256]{1,0:T(8,128)S(1)} %get-tuple-element.31.refs_0_, f32[512,256]{1,0:T(8,128)S(1)} %collective-permute-done.8.refs_1_, f32[512,256]{1,0:T(8,128)S(1)} %collective-permute-done.9.refs_2_, f32[512,256]{1,0:T(8,128)S(1)} %collective-permute-done.10.refs_3_), custom_call_target="tpu_custom_call" | custom-call | flops 1000000000 | bytes 4000000 | tf_op jit(solution)/shard_map/pallas_call | solution.py:477
Async XLA Ops:
  17.6 3.9 %copy-start.3 = (f32[2,9,32,128]{3,2,1,0:T(8,128)S(1)}, f32[2,9,32,128]{3,2,1,0:T(8,128)}, u32[]{:S(2)}) copy-start(f32[2,9,32,128]{3,2,1,0:T(8,128)} %get-tuple-element.22) | copy-start | bytes 884740
  17.6 13.3 %copy-start.2 = (f32[8,9,32,128]{3,2,1,0:T(8,128)S(1)}, f32[8,9,32,128]{3,2,1,0:T(8,128)}, u32[]{:S(2)}) copy-start(f32[8,9,32,128]{3,2,1,0:T(8,128)} %get-tuple-element.21.early) | copy-start | bytes 3538948
  17.6 32.9 %all-to-all-start = ((f32[8,9,32,128]{3,2,1,0:T(8,128)}), f32[8,9,32,128]{3,2,1,0:T(8,128)S(1)}, u32[]{:S(2)}, u32[]{:S(2)}) async-start(f32[8,9,32,128]{3,2,1,0:T(8,128)} %get-tuple-element.20), calls=%async_computation | async-start | bytes 2359296 | tf_op jit(solution)/shard_map/all_to_all | solution.py:531
  21.5 9.4 %collective-permute-start = (f32[2,9,32,128]{3,2,1,0:T(8,128)S(1)}, f32[2,9,32,128]{3,2,1,0:T(8,128)S(1)}, u32[]{:S(2)}, u32[]{:S(2)}) collective-permute-start(f32[2,9,32,128]{3,2,1,0:T(8,128)S(1)} %copy-done.3), channel_id=1, source_target_pairs={{0,8},{8,16},{16,24},{24,0},{1,9},{9,17},{17,25},{25,1},{2,10},{10... | collective-permute-start | bytes 884744 | tf_op jit(solution)/shard_map/ppermute | solution.py:530
  31.7 3.7 %collective-permute-start.1 = (f32[9,32,128]{2,1,0:T(8,128)S(1)}, f32[9,32,128]{2,1,0:T(8,128)S(1)}, u32[]{:S(2)}, u32[]{:S(2)}) collective-permute-start(f32[9,32,128]{2,1,0:T(8,128)S(1)} %get-tuple-element.24), channel_id=1, source_target_pairs={{0,1},{1,0},{2,3},{3,2},{4,5},{5,4},{6,7},{7,6},{8,9},{9,8},{10,11... | collective-permute-start | bytes 442376 | tf_op jit(solution)/shard_map/ppermute | solution.py:535
  31.7 9.3 %collective-permute-start.2 = (f32[9,32,128]{2,1,0:T(8,128)S(1)}, f32[9,32,128]{2,1,0:T(8,128)S(1)}, u32[]{:S(2)}, u32[]{:S(2)}) collective-permute-start(f32[9,32,128]{2,1,0:T(8,128)S(1)} %get-tuple-element.25), channel_id=1, source_target_pairs={{0,2},{1,3},{2,0},{3,1},{4,6},{5,7},{6,4},{7,5},{8,10},{9,11},{10,... | collective-permute-start | bytes 442376 | tf_op jit(solution)/shard_map/ppermute | solution.py:535
  33.5 9.8 %collective-permute-start.3 = (f32[9,32,128]{2,1,0:T(8,128)S(1)}, f32[9,32,128]{2,1,0:T(8,128)S(1)}, u32[]{:S(2)}, u32[]{:S(2)}) collective-permute-start(f32[9,32,128]{2,1,0:T(8,128)S(1)} %get-tuple-element.26), channel_id=1, source_target_pairs={{0,3},{1,2},{2,1},{3,0},{4,7},{5,6},{6,5},{7,4},{8,11},{9,10},{10,... | collective-permute-start | bytes 442376 | tf_op jit(solution)/shard_map/ppermute | solution.py:535
  33.6 9.7 %collective-permute-start.4 = (f32[9,32,128]{2,1,0:T(8,128)S(1)}, f32[9,32,128]{2,1,0:T(8,128)S(1)}, u32[]{:S(2)}, u32[]{:S(2)}) collective-permute-start(f32[9,32,128]{2,1,0:T(8,128)S(1)} %get-tuple-element.27), channel_id=1, source_target_pairs={{0,4},{1,5},{2,6},{3,7},{4,0},{5,1},{6,2},{7,3},{8,12},{9,13},{10,... | collective-permute-start | bytes 442376 | tf_op jit(solution)/shard_map/ppermute | solution.py:535
  35.3 9.7 %collective-permute-start.5 = (f32[9,32,128]{2,1,0:T(8,128)S(1)}, f32[9,32,128]{2,1,0:T(8,128)S(1)}, u32[]{:S(2)}, u32[]{:S(2)}) collective-permute-start(f32[9,32,128]{2,1,0:T(8,128)S(1)} %get-tuple-element.28), channel_id=1, source_target_pairs={{0,5},{1,4},{2,7},{3,6},{4,1},{5,0},{6,3},{7,2},{8,13},{9,12},{10,... | collective-permute-start | bytes 442376 | tf_op jit(solution)/shard_map/ppermute | solution.py:535
  35.3 13.0 %collective-permute-start.6 = (f32[9,32,128]{2,1,0:T(8,128)S(1)}, f32[9,32,128]{2,1,0:T(8,128)S(1)}, u32[]{:S(2)}, u32[]{:S(2)}) collective-permute-start(f32[9,32,128]{2,1,0:T(8,128)S(1)} %get-tuple-element.29), channel_id=1, source_target_pairs={{0,6},{1,7},{2,4},{3,5},{4,2},{5,3},{6,0},{7,1},{8,14},{9,15},{10,... | collective-permute-start | bytes 442376 | tf_op jit(solution)/shard_map/ppermute | solution.py:535
  41.1 9.4 %collective-permute-start.7 = (f32[9,32,128]{2,1,0:T(8,128)S(1)}, f32[9,32,128]{2,1,0:T(8,128)S(1)}, u32[]{:S(2)}, u32[]{:S(2)}) collective-permute-start(f32[9,32,128]{2,1,0:T(8,128)S(1)} %get-tuple-element.30), channel_id=1, source_target_pairs={{0,7},{1,6},{2,5},{3,4},{4,3},{5,2},{6,1},{7,0},{8,15},{9,14},{10,... | collective-permute-start | bytes 442376 | tf_op jit(solution)/shard_map/ppermute | solution.py:535
  50.5 2.2 %copy-start = (bf16[2,32,128,256]{3,2,1,0:T(8,128)(2,1)S(1)}, bf16[2,32,128,256]{3,2,1,0:T(8,128)(2,1)}, u32[]{:S(2)}) copy-start(bf16[2,32,128,256]{3,2,1,0:T(8,128)(2,1)} %constant.21.clone.refs_8_) | copy-start | bytes 12582916
  58.2 51.9 %copy-start.1 = (bf16[2,16,256,128]{3,2,1,0:T(8,128)(2,1)S(1)}, bf16[2,16,256,128]{3,2,1,0:T(8,128)(2,1)}, u32[]{:S(2)}) copy-start(bf16[2,16,256,128]{3,2,1,0:T(8,128)(2,1)} %constant.22.clone.table_source) | copy-start | bytes 6291460
  114.6 22.5 %collective-permute-start.8 = (f32[512,256]{1,0:T(8,128)S(1)}, f32[512,256]{1,0:T(8,128)S(1)}, u32[]{:S(2)}, u32[]{:S(2)}) collective-permute-start(f32[512,256]{1,0:T(8,128)S(1)} %get-tuple-element.32), channel_id=1, source_target_pairs={{0,8},{8,0},{16,24},{24,16},{1,9},{9,1},{17,25},{25,17},{2,10},{10... | collective-permute-start | bytes 1572872 | tf_op jit(solution)/shard_map/ppermute | solution.py:581
  115.9 35.5 %collective-permute-start.9 = (f32[512,256]{1,0:T(8,128)S(1)}, f32[512,256]{1,0:T(8,128)S(1)}, u32[]{:S(2)}, u32[]{:S(2)}) collective-permute-start(f32[512,256]{1,0:T(8,128)S(1)} %get-tuple-element.33), channel_id=1, source_target_pairs={{0,16},{8,24},{16,0},{24,8},{1,17},{9,25},{17,1},{25,9},{2,18},{10... | collective-permute-start | bytes 1572872 | tf_op jit(solution)/shard_map/ppermute | solution.py:581
  116.7 46.9 %collective-permute-start.10 = (f32[512,256]{1,0:T(8,128)S(1)}, f32[512,256]{1,0:T(8,128)S(1)}, u32[]{:S(2)}, u32[]{:S(2)}) collective-permute-start(f32[512,256]{1,0:T(8,128)S(1)} %get-tuple-element.34), channel_id=1, source_target_pairs={{0,24},{8,16},{16,8},{24,0},{1,25},{9,17},{17,9},{25,1},{2,26},{10... | collective-permute-start | bytes 1572872 | tf_op jit(solution)/shard_map/ppermute | solution.py:581

commit v3 on v2

--- a/solution.py
+++ b/solution.py
@@ -150,24 +150,34 @@
 
 def refine_kernel(starts, *refs):
     sources, (late, early, below), refs = refs[:6], refs[6:9], refs[9:]
-    held, (first, second, updates, done) = refs[:6], refs[6:]
+    held, (first, second, updates, arrived, done) = refs[:6], refs[6:]
     tiles, table, pupils, intensity, row_table, col_table = held
-    copies = [
-        pltpu.make_async_copy(source, target, done.at[place])
-        for place, (source, target) in enumerate(zip(sources, held))
-    ]
-    for copy in copies:
-        copy.start()
     length = tiles.shape[1]
     window = pupils.shape[1]
     leds = intensity.shape[0]
     chunks = first.shape[1]
     rest = length - (chunks - 1) * LANES
-    copies[0].wait()
-    for side in range(2):
-        second[side, chunks - 1, :, pl.ds(0, rest)] = tiles[side, :, pl.ds((chunks - 1) * LANES, rest)]
+    tile_copies = []
+    for chunk in range(chunks):
+        lanes = pl.ds(chunk * LANES, min(LANES, length - chunk * LANES))
+        tile_copies.append(
+            pltpu.make_async_copy(sources[0].at[:, :, lanes], tiles.at[:, :, lanes], arrived.at[chunk])
+        )
+    copies = [
+        pltpu.make_async_copy(source, target, done.at[place])
+        for place, (source, target) in enumerate(zip(sources[1:], held[1:]))
+    ]
+    tile_copies[0].start()
+    copies[0].start()
+    for copy in tile_copies[1:] + copies[1:]:
+        copy.start()
 
     def from_tiles(side, chunk, rows):
+        if side == 0 and rows.start == 0:
+            tile_copies[chunk].wait()
+            if chunk == chunks - 1:
+                for part in range(2):
+                    second[part, chunk, :, pl.ds(0, rest)] = tiles[part, :, pl.ds(chunk * LANES, rest)]
         if chunk == chunks - 1:
             return second[side, chunk, rows, :]
         return tiles[side, rows, pl.ds(chunk * LANES, LANES)]
@@ -178,15 +188,15 @@
     def from_second(side, chunk, rows):
         return second[side, chunk, rows, :]
 
-    copies[1].wait()
+    copies[0].wait()
     tile_pass(from_tiles, first, table, -1)
     transpose_all(first, second)
     tile_pass(from_second, first, table, -1)
-    for copy in copies[2:]:
+    for copy in copies[1:]:
         copy.wait()
     lens_real, lens_imag = pupils[0].T, pupils[1].T
     lane = lax.broadcasted_iota(jnp.int32, (window, LANES), 1)
-    group = 8 if leds % 8 == 0 else 1
+    group, beside = (GROUP, BESIDE) if leds % (GROUP * BESIDE) == 0 else (1, 1)
 
     def place_of(led):
         start = starts[0, led]
@@ -205,45 +215,54 @@
             col_table[...], jnp.concatenate([high, low, high], axis=0), preferred_element_type=F32
         )
 
-    def step(index, carry):
-        crops = []
-        for member in range(group):
-            chunk, shift, row = place_of(index * group + member)
-            crop = []
-            for side in range(2):
-                here = first[side, chunk, pl.ds(row, window), :]
-                beyond = first[side, chunk + 1, pl.ds(row, window), :]
-                joined = jnp.where(lane >= shift, here, beyond)
-                crop.append(pltpu.roll(joined, lax.rem(LANES - shift, LANES), 1))
-            crops.append(
-                jnp.concatenate(
-                    [
-                        lens_real * crop[0] - lens_imag * crop[1],
-                        -lens_real * crop[1] - lens_imag * crop[0],
-                    ],
-                    axis=1,
-                )
-            )
-        wave = along_rows(jnp.concatenate(crops, axis=0))
-        blocks = [wave[m * window : (m + 1) * window] for m in range(group)]
+    def crop(led):
+        chunk, shift, row = place_of(led)
+        crop = []
+        for side in range(2):
+            here = first[side, chunk, pl.ds(row, window), :]
+            beyond = first[side, chunk + 1, pl.ds(row, window), :]
+            joined = jnp.where(lane >= shift, here, beyond)
+            crop.append(pltpu.roll(joined, lax.rem(LANES - shift, LANES), 1))
+        real = lens_real * crop[0] - lens_imag * crop[1]
+        imag = -lens_real * crop[1] - lens_imag * crop[0]
+        return jnp.concatenate([real, imag], axis=1)
+
+    def to_waves(leds):
+        return along_rows(jnp.concatenate([crop(led) for led in leds], axis=0))
+
+    def to_wave_cols(leds, wave):
+        blocks = [wave[m * window : (m + 1) * window] for m in range(len(leds))]
         blocks = [jnp.concatenate([b[:, :window], b[:, window:]], axis=0) for b in blocks]
-        wave = along_cols(jnp.concatenate(blocks, axis=1))
+        return along_cols(jnp.concatenate(blocks, axis=1))
+
+    def to_grad_cols(leds, wave):
         real, imag = wave[:window], wave[window:]
-        measured = jnp.concatenate([intensity[index * group + m].T for m in range(group)], axis=1)
+        measured = jnp.concatenate([intensity[led].T for led in leds], axis=1)
         excess = real * real + imag * imag - measured
-        grad = along_cols(jnp.concatenate([real * excess, -imag * excess], axis=0))
-        blocks = [grad[:, m * window : (m + 1) * window] for m in range(group)]
+        return along_cols(jnp.concatenate([real * excess, -imag * excess], axis=0))
+
+    def to_grads(leds, grad):
+        blocks = [grad[:, m * window : (m + 1) * window] for m in range(len(leds))]
         blocks = [jnp.concatenate([b[:window], b[window:]], axis=1) for b in blocks]
-        grad = along_rows(jnp.concatenate(blocks, axis=0))
-        for m in range(group):
+        return along_rows(jnp.concatenate(blocks, axis=0))
+
+    def to_updates(leds, grad):
+        for m, led in enumerate(leds):
             real = grad[m * window : (m + 1) * window, :window]
             imag = grad[m * window : (m + 1) * window, window:]
-            led = index * group + m
             updates[led, 0] = -STEP_SIZE * (lens_real * real + lens_imag * imag)
             updates[led, 1] = -STEP_SIZE * (lens_real * imag - lens_imag * real)
+
+    def step(index, carry):
+        groups = [
+            [(index * beside + g) * group + m for m in range(group)] for g in range(beside)
+        ]
+        values = [to_waves(g) for g in groups]
+        for stage in (to_wave_cols, to_grad_cols, to_grads, to_updates):
+            values = [stage(g, value) for g, value in zip(groups, values)]
         return carry
 
-    lax.fori_loop(0, leds // group, step, 0)
+    lax.fori_loop(0, leds // (group * beside), step, 0)
 
     def place(led, carry):
         chunk, shift, row = place_of(led)
@@ -289,6 +308,8 @@
 
 
 def spread_kernel(place, early, above, *outs):
+    *outs, token = outs
+    token[...] = jnp.zeros(token.shape, F32)
     blended = above.shape[0]
     for step, out in enumerate(outs):
         part = jnp.bitwise_xor(place[0], step)
@@ -299,67 +320,52 @@
             out[...] += above[jnp.minimum(part, blended - 1)]
 
 
-UNROLL = 4
-
-
-class Fetch:
-    def __init__(self, source, target, done):
-        self.parts = done.shape[0]
-        self.each = source.shape[1] // self.parts
-        self.copies = [
-            pltpu.make_async_copy(
-                source.at[:, pl.ds(part * self.each, self.each)],
-                target.at[:, pl.ds(part * self.each, self.each)],
-                done.at[part],
-            )
-            for part in range(self.parts)
-        ]
-        for copy in self.copies:
-            copy.start()
-
-    def each_class(self, body):
-        for part in range(self.parts):
-            self.copies[part].wait()
-            lax.fori_loop(part * self.each, (part + 1) * self.each, body, 0, unroll=UNROLL)
-
-
-def col_kernel(place, late, *refs):
-    *blocks, table_source, out, early, held, table, done = refs
-    fetch = Fetch(table_source, table, done)
+UNROLL = 8
+GROUP = 4
+BESIDE = 4
+
+
+def gather_kernel(place, finished, *refs):
+    *blocks, table, out, values, held = refs
+    rows = finished.shape[2]
     for step, block in enumerate(blocks):
-        early[jnp.bitwise_xor(place[0], step)] = block[...]
-    tiles, pieces, half, _ = late.shape
-    rows = 2 * half
+        values[jnp.bitwise_xor(place[0], step)] = block[...]
+    out[:, :, pl.ds(0, rows), :] = finished[...]
+    col_kernel(values, table, out.at[:, :, pl.ds(rows, rows), :], held)
+
+
+def after_kernel(after, *refs):
+    del after
+    col_kernel(*refs)
+
+
+def col_kernel(values, table, out, held):
+    tiles, pieces, rows, _ = values.shape
     whole = (pieces - 1) // 2
     width = out.shape[3] // 2
     per = LANES // width
 
-    def enter_from(values, first):
-        def enter(strip, carry):
-            here = pl.ds(pl.multiple_of(strip * 8, 8), 8)
-            lane = lax.broadcasted_iota(jnp.int32, (8, LANES), 1)
-            ramp = jnp.where(lane < OVL, ramp_of(lane), 1.0)
-            rest = 1.0 - ramp
-            segments = []
-            for tile in range(tiles):
-                halo = values[(tile - 1) % tiles, 2 * whole, here, :]
-                for chunk in range(whole):
-                    real = values[tile, chunk, here, :]
-                    imag = values[tile, whole + chunk, here, :]
-                    if chunk == 0:
-                        real = ramp * real + rest * halo
-                        imag = ramp * imag + rest * pltpu.roll(halo, OVL, 1)
-                    segments.append((real, imag))
-            here = pl.ds(pl.multiple_of(first + strip * 8, 8), 8)
-            for index, (real, imag) in enumerate(short_fft(segments, -1)):
-                held[index, 0, here, :] = real
-                held[index, 1, here, :] = imag
-            return carry
-
-        lax.fori_loop(0, half // 8, enter, 0)
-
-    enter_from(late, 0)
-    enter_from(early, half)
+    def enter(strip, carry):
+        here = pl.ds(pl.multiple_of(strip * 8, 8), 8)
+        lane = lax.broadcasted_iota(jnp.int32, (8, LANES), 1)
+        ramp = jnp.where(lane < OVL, ramp_of(lane), 1.0)
+        rest = 1.0 - ramp
+        segments = []
+        for tile in range(tiles):
+            halo = values[(tile - 1) % tiles, 2 * whole, here, :]
+            for chunk in range(whole):
+                real = values[tile, chunk, here, :]
+                imag = values[tile, whole + chunk, here, :]
+                if chunk == 0:
+                    real = ramp * real + rest * halo
+                    imag = ramp * imag + rest * pltpu.roll(halo, OVL, 1)
+                segments.append((real, imag))
+        for index, (real, imag) in enumerate(short_fft(segments, -1)):
+            held[index, 0, here, :] = real
+            held[index, 1, here, :] = imag
+        return carry
+
+    lax.fori_loop(0, rows // 8, enter, 0)
 
     def multiply(index, carry):
         value = held[index].reshape(2 * rows, LANES)
@@ -372,7 +378,7 @@
         held[index, 1] = full[:rows, LANES:] + full[rows:, :LANES]
         return carry
 
-    fetch.each_class(multiply)
+    lax.fori_loop(0, tiles * whole, multiply, 0, unroll=UNROLL)
 
     def leave(strip, carry):
         here = pl.ds(pl.multiple_of(strip * 8, 8), 8)
@@ -390,13 +396,12 @@
     lax.fori_loop(0, rows // 8, leave, 0)
 
 
-def row_kernel(half, place, values, table_source, *refs):
-    *outs, out, held, table, done = refs
-    fetch = Fetch(table_source, table, done)
+def row_kernel(half, place, values, table, *refs):
+    *outs, held = refs
     tiles, _, both = values.shape
     width = both // 2
-    stride = out.shape[1]
-    part = table.shape[3]
+    stride = outs[0].shape[0]
+    part = table.shape[3] // 2
     whole = stride // part
 
     def enter_from(offset, first):
@@ -410,8 +415,8 @@
                     segments.append((value[:, :width], value[:, width:]))
             here = pl.ds(pl.multiple_of(first + strip * 8, 8), 8)
             for index, (real, imag) in enumerate(short_fft(segments, -1)):
-                held[index, here, pl.ds(0, width)] = real
-                held[index, here, pl.ds(width, width)] = imag
+                held[index, here, :] = real
+                held[index, pl.ds(pl.multiple_of(part + first + strip * 8, 8), 8), :] = imag
             return carry
 
         lax.fori_loop(0, OVL // 8, enter, 0)
@@ -425,47 +430,60 @@
             table[0, index], jnp.concatenate([high, low], axis=1), preferred_element_type=F32
         )
         rest = jnp.dot(table[1, index], high, preferred_element_type=F32)
-        full = main[:, :both] + (main[:, both:] + rest)
-        held[index, :, pl.ds(0, width)] = full[:part, :width] - full[part:, width:]
-        held[index, :, pl.ds(width, width)] = full[:part, width:] + full[part:, :width]
+        held[index] = main[:, :width] + (main[:, width:] + rest)
         return carry
 
-    fetch.each_class(multiply)
-
-    def leave(strip, carry):
-        here = pl.ds(pl.multiple_of(strip * 8, 8), 8)
-        segments = []
-        for index in range(tiles * whole):
-            value = held[index, here, :]
-            segments.append((value[:, :width], value[:, width:]))
-        for index, (real, imag) in enumerate(short_fft(segments, 1)):
-            tile, chunk = index // whole, index % whole
-            here = pl.ds(pl.multiple_of(chunk * part + strip * 8, 8), 8)
-            out[tile, here, pl.ds(0, width)] = real
-            out[tile, here, pl.ds(width, width)] = imag
-        return carry
-
-    lax.fori_loop(0, part // 8, leave, 0)
-    for step, target in enumerate(outs):
-        target[...] = out[jnp.bitwise_xor(place[1], step)]
+    lax.fori_loop(0, tiles * whole, multiply, 0, unroll=UNROLL)
+
+    def leave_as(me):
+        def leave(strip, carry):
+            here = pl.ds(pl.multiple_of(strip * 8, 8), 8)
+            segments = []
+            for index in range(tiles * whole):
+                below = pl.ds(pl.multiple_of(part + strip * 8, 8), 8)
+                segments.append((held[index, here, :], held[index, below, :]))
+            for index, (real, imag) in enumerate(short_fft(segments, 1)):
+                tile, chunk = index // whole, index % whole
+                here = pl.ds(pl.multiple_of(chunk * part + strip * 8, 8), 8)
+                outs[tile ^ me][here, pl.ds(0, width)] = real
+                outs[tile ^ me][here, pl.ds(width, width)] = imag
+            return carry
+
+        @pl.when(place[1] == me)
+        def _():
+            lax.fori_loop(0, part // 8, leave, 0)
+
+    for me in range(tiles):
+        leave_as(me)
 
 
 def join_kernel(place, *refs):
-    *blocks, out, ordered = refs
-    count, _, both = ordered.shape
-    width = both // 2
+    *blocks, out, ordered, done = refs
+    width = blocks[0].shape[1] // 2
+    if width % LANES:
+        for step, block in enumerate(blocks):
+            part = jnp.bitwise_xor(place[1], step)
+            ordered[part] = block[...]
+        for part in range(len(blocks)):
+            for side in range(2):
+                lanes = pl.ds(part * width, width)
+                out[side, :, lanes] = ordered[part, :, pl.ds(side * width, width)]
+        return
+    copies = []
     for step, block in enumerate(blocks):
         part = jnp.bitwise_xor(place[1], step)
-        if width % LANES:
-            ordered[part] = block[...]
-            continue
+        lanes = pl.ds(pl.multiple_of(part * width, LANES), width)
         for side in range(2):
-            lanes = pl.ds(pl.multiple_of(part * width, LANES), width)
-            out[side, :, lanes] = block[:, pl.ds(side * width, width)]
-    if width % LANES:
-        for part in range(count):
-            for side in range(2):
-                out[side, :, pl.ds(part * width, width)] = ordered[part, :, pl.ds(side * width, width)]
+            copies.append(
+                pltpu.make_async_copy(
+                    block.at[:, pl.ds(side * width, width)],
+                    out.at[side, :, lanes],
+                    done.at[len(copies)],
+                )
+            )
+            copies[-1].start()
+    for copy in copies:
+        copy.wait()
 
 
 VMEM = pl.BlockSpec(memory_space=pltpu.VMEM)
@@ -518,7 +536,8 @@
             buffer,
             buffer,
             pltpu.VMEM((leds, 2, window, window), F32),
-            pltpu.SemaphoreType.DMA((len(operands),)),
+            pltpu.SemaphoreType.DMA((chunks,)),
+            pltpu.SemaphoreType.DMA((len(operands) - 1,)),
         ],
         56,
         22,
@@ -530,44 +549,49 @@
     above = lax.ppermute(below, "row", [(r, (r + 1) % row_count) for r in range(row_count)])
     late = lax.all_to_all(late, "col", split_axis=0, concat_axis=0, tiled=True)
     place = jnp.stack([lax.axis_index("col"), lax.axis_index("row")]).astype(jnp.int32)
-    early = call(spread_kernel, [block] * col_count, [], 16, 1, place, early, above, scalars=1)
+    *early, token = call(
+        spread_kernel, [block] * col_count + [(8, LANES)], [], 16, 40, place, early, above, scalars=1
+    )
     early = [early[0]] + [
         lax.ppermute(early[step], "col", [(c, c ^ step) for c in range(col_count)])
         for step in range(1, col_count)
     ]
     col_classes = col_count * whole
     table = spread_tables(stride * col_count, fresnel, col_classes, lambda m: right_half(m.T))
+    scratch = [pltpu.VMEM((col_classes, 2, rows, LANES), F32)]
     (field,) = call(
-        col_kernel,
+        after_kernel,
+        [(row_count, col_count, rows, 2 * width)],
+        scratch,
+        32,
+        4,
+        token,
+        late,
+        table,
+        outside=(-3,),
+    )
+    (field,) = call(
+        gather_kernel,
         [(row_count, col_count, 2 * rows, 2 * width)],
-        [
-            pltpu.VMEM((col_count, *block), F32),
-            pltpu.VMEM((col_classes, 2, 2 * rows, LANES), F32),
-            pltpu.VMEM(table.shape, BF16),
-            pltpu.SemaphoreType.DMA((4,)),
-        ],
+        [pltpu.VMEM((col_count, *block), F32)] + scratch,
         32,
-        5,
+        4,
         place,
-        late,
+        field,
         *early,
         table,
         scalars=1,
-        outside=(-1,),
     )
     field = field.reshape(row_count * col_count, 2 * rows, 2 * width)
     field = lax.all_to_all(field, ("row", "col"), split_axis=0, concat_axis=0, tiled=True)
     row_classes = row_count * whole
-    table = spread_tables(stride * row_count, fresnel, row_classes, left_half)
+    table = spread_tables(stride * row_count, fresnel, row_classes, left_block)
     shape = (stride, 2 * width)
     blocks = call(
         functools.partial(row_kernel, rows),
         [shape] * row_count,
         [
-            pltpu.VMEM((row_count, *shape), F32),
-            pltpu.VMEM((row_classes, LANES, 2 * width), F32),
-            pltpu.VMEM(table.shape, BF16),
-            pltpu.SemaphoreType.DMA((4,)),
+            pltpu.VMEM((row_classes, 2 * LANES, width), F32),
         ],
         32,
         5,
@@ -575,23 +599,22 @@
         field.reshape(row_count, col_count * 2 * rows, 2 * width),
         table,
         scalars=1,
-        outside=(-1,),
     )
     blocks = [blocks[0]] + [
         lax.ppermute(blocks[step], "row", [(r, r ^ step) for r in range(row_count)])
         for step in range(1, row_count)
     ]
-    (field,) = call(
+    return pl.pallas_call(
         join_kernel,
-        [(2, stride, stride)],
-        [pltpu.VMEM((row_count, *shape), F32)],
-        16,
-        2,
-        place,
-        *blocks,
-        scalars=1,
-    )
-    return field
+        out_shape=jax.ShapeDtypeStruct((2, stride, stride), F32),
+        in_specs=[SMEM] + [VMEM] * row_count,
+        out_specs=VMEM if width % LANES else HBM,
+        scratch_shapes=[
+            pltpu.VMEM((row_count, *shape) if width % LANES else (8, LANES), F32),
+            pltpu.SemaphoreType.DMA((2 * row_count,)),
+        ],
+        compiler_params=pltpu.CompilerParams(vmem_limit_bytes=16 << 20),
+    )(place, *blocks)
 
 
 def solution(mesh):

time: 166 us -> 159 us (0.958)
  waiting for transfers between devices: 65.5 us -> 61.4 us
  Pallas kernels: 30.5 us -> 27.4 us
    pallas_call x5, Pallas kernels: 30.5 us -> 25.5 us  [call(): pl.pallas_call(kernel, out_shape=[jax.ShapeDtypeStruct(shape, F32) for sh...]
    ppermute x1, waiting for transfers between devices: 7.7 us -> 3.59 us  [local(): lax.ppermute(below, 'row', [(r, (r + 1) % row_count) for r in range(row_c...]
    pallas_call x0 -> x1, Pallas kernels: none -> 1.92 us  [local(): pl.pallas_call(join_kernel, out_shape=jax.ShapeDtypeStruct((2, stride, st...]
  transfers between devices with their start and end apart: 12 -> 12, of which waited for: 9 -> 7; matrix products, arithmetic and copies ran while one was open for 0% -> 0% of each run, Pallas kernels for 0% -> 2%
where the time goes in v3:
time: 159 us
  waiting for transfers between devices  61.4 us (39%)
  blocking collectives  50.7 us (32%)
  Pallas kernels  27.4 us (17%)
  starting transfers between devices  15.2 us (10%)
  local copies, waits for them, and re-layouts  3.47 us (2%)
    all_to_all x1, blocking collectives, local(): lax.all_to_all(field, ('row', 'col'), split_axis=0, concat_axis=0, tiled=...  50.7 us
    ppermute x3, waiting for transfers between devices, local(): lax.ppermute(blocks[step], 'row', [(r, r ^ step) for r in range(row_count)])  45.5 us
    pallas_call x5, Pallas kernels, call(): pl.pallas_call(kernel, out_shape=[jax.ShapeDtypeStruct(shape, F32) for sh...  25.5 us
    ppermute x7, waiting for transfers between devices, local(): lax.ppermute(early[step], 'col', [(c, c ^ step) for c in range(col_count)])  12.4 us
    ppermute x7, starting transfers between devices, local(): lax.ppermute(early[step], 'col', [(c, c ^ step) for c in range(col_count)])  6.3 us
    all_to_all x1, starting transfers between devices, local(): late = lax.all_to_all(late, 'col', split_axis=0, concat_axis=0, tiled=True)  3.72 us
    ppermute x1, waiting for transfers between devices, local(): lax.ppermute(below, 'row', [(r, (r + 1) % row_count) for r in range(row_c...  3.59 us
    ppermute x3, starting transfers between devices, local(): lax.ppermute(blocks[step], 'row', [(r, r ^ step) for r in range(row_count)])  3.55 us
  transfers between devices with their start and end apart: 12, of which 7 were waited for; matrix products, arithmetic and copies ran while one was open for 0% of the time, Pallas kernels for 2%

profile of v3, /device:TPU:8, one launch (start us, length us, event | category | flops | bytes accessed | tf_op | source)
XLA Modules:
  0.0 158.6 jit_solution(16160795169910408147)
XLA Ops:
  0.0 15.9 %shard_map.91 = (f32[8,9,32,128]{3,2,1,0:T(8,128)}, f32[8,9,32,128]{3,2,1,0:T(8,128)}, f32[2,9,32,128]{3,2,1,0:T(8,128)}) custom-call(s32[2,16]{1,0:T(2,128)} %bitcast.7, f32[2,576,576]{2,1,0:T(8,128)} %refs_0_.1, bf16[8,144,216]{2,1,0:T(8,128)(2,1)} %constant.18.clone.refs_1_, f32[2,128,128]{2,1,0:T(8,128)} %refs_2_.1, f32[16,128,128]{2,1,0:T(8,128)} %refs_3_.1, ...), custom_call_target="tpu_custom_call" | custom-call | flops 11000000512 | bytes 44000000 | tf_op jit(solution)/shard_map/pallas_call | solution.py:495
  16.0 1.6 %collective-permute-start = (f32[2,9,32,128]{3,2,1,0:T(8,128)}, f32[2,9,32,128]{3,2,1,0:T(8,128)S(1)}, u32[]{:S(2)}, u32[]{:S(2)}) collective-permute-start(f32[2,9,32,128]{3,2,1,0:T(8,128)} %get-tuple-element.22), channel_id=1, source_target_pairs={{0,8},{8,16},{16,24},{24,0},{1,9},{9,17},{17,25},{25,1},{2,10},{10... | collective-permute-start | bytes 884744 | tf_op jit(solution)/shard_map/ppermute | solution.py:549
  17.6 3.7 %all-to-all-start = ((f32[8,9,32,128]{3,2,1,0:T(8,128)}), f32[8,9,32,128]{3,2,1,0:T(8,128)S(1)}, u32[]{:S(2)}, u32[]{:S(2)}) async-start(f32[8,9,32,128]{3,2,1,0:T(8,128)} %get-tuple-element.24), calls=%async_computation | async-start | bytes 2359296 | tf_op jit(solution)/shard_map/all_to_all | solution.py:550
  21.3 0.1 pad_add_fusion.place
  21.4 3.6 %collective-permute-done.above = f32[2,9,32,128]{3,2,1,0:T(8,128)S(1)} collective-permute-done((f32[2,9,32,128]{3,2,1,0:T(8,128)}, f32[2,9,32,128]{3,2,1,0:T(8,128)S(1)}, u32[]{:S(2)}, u32[]{:S(2)}) %collective-permute-start) | collective-permute-done | bytes 294944 | tf_op jit(solution)/shard_map/ppermute | solution.py:549
  25.0 0.0 copy-start.3
  25.0 1.3 copy-done.3
  26.2 0.9 shard_map.92
  27.1 0.1 collective-permute-start.1
  27.2 1.6 collective-permute-start.2
  28.8 0.3 collective-permute-start.3
  29.1 1.5 collective-permute-start.4
  30.6 0.2 collective-permute-start.5
  30.8 0.0 collective-permute-done.1.refs_1_
  30.8 2.4 %collective-permute-start.6 = (f32[9,32,128]{2,1,0:T(8,128)S(1)}, f32[9,32,128]{2,1,0:T(8,128)S(1)}, u32[]{:S(2)}, u32[]{:S(2)}) collective-permute-start(f32[9,32,128]{2,1,0:T(8,128)S(1)} %get-tuple-element.31), channel_id=1, source_target_pairs={{0,6},{1,7},{2,4},{3,5},{4,2},{5,3},{6,0},{7,1},{8,14},{9,15},{10,... | collective-permute-start | bytes 442376 | tf_op jit(solution)/shard_map/ppermute | solution.py:556
  33.2 7.7 %collective-permute-done.2.refs_2_ = f32[9,32,128]{2,1,0:T(8,128)S(1)} collective-permute-done((f32[9,32,128]{2,1,0:T(8,128)S(1)}, f32[9,32,128]{2,1,0:T(8,128)S(1)}, u32[]{:S(2)}, u32[]{:S(2)}) %collective-permute-start.2) | collective-permute-done | bytes 147488 | tf_op jit(solution)/shard_map/ppermute | solution.py:556
  40.9 0.2 collective-permute-start.7
  41.1 0.0 all-to-all-done.refs_0_
  41.1 0.0 copy-start
  41.1 2.2 %copy-done = bf16[2,32,128,256]{3,2,1,0:T(8,128)(2,1)S(1)} copy-done((bf16[2,32,128,256]{3,2,1,0:T(8,128)(2,1)S(1)}, bf16[2,32,128,256]{3,2,1,0:T(8,128)(2,1)}, u32[]{:S(2)}) %copy-start) | copy-done | bytes 4194328
  43.3 0.0 copy-start.1
  43.3 2.3 %shard_map.93.finished = f32[4,8,32,256]{3,2,1,0:T(8,128)S(1)} custom-call(f32[8,128]{1,0:T(8,128)S(1)} %get-tuple-element.23.after, f32[8,9,32,128]{3,2,1,0:T(8,128)S(1)} %all-to-all-done.refs_0_, bf16[2,32,128,256]{3,2,1,0:T(8,128)(2,1)S(1)} %copy-done), custom_call_target="tpu_custom_call" | custom-call | flops 2000000000 | bytes 8000000 | tf_op jit(solution)/shard_map/pallas_call | solution.py:495
  45.6 0.0 collective-permute-done.3.refs_3_
  45.6 0.0 collective-permute-done.4.refs_4_
  45.7 0.0 collective-permute-done.5.refs_5_
  45.7 2.5 %collective-permute-done.6.refs_6_ = f32[9,32,128]{2,1,0:T(8,128)S(1)} collective-permute-done((f32[9,32,128]{2,1,0:T(8,128)S(1)}, f32[9,32,128]{2,1,0:T(8,128)S(1)}, u32[]{:S(2)}, u32[]{:S(2)}) %collective-permute-start.6) | collective-permute-done | bytes 147488 | tf_op jit(solution)/shard_map/ppermute | solution.py:556
  48.1 2.2 %collective-permute-done.7.refs_7_ = f32[9,32,128]{2,1,0:T(8,128)S(1)} collective-permute-done((f32[9,32,128]{2,1,0:T(8,128)S(1)}, f32[9,32,128]{2,1,0:T(8,128)S(1)}, u32[]{:S(2)}, u32[]{:S(2)}) %collective-permute-start.7) | collective-permute-done | bytes 147488 | tf_op jit(solution)/shard_map/ppermute | solution.py:556
  50.3 0.0 copy-done.1
  50.3 3.0 %shard_map.94 = f32[4,8,64,256]{3,2,1,0:T(8,128)S(1)} custom-call(s32[2]{0:T(128)S(1)} %pad_add_fusion.place, f32[4,8,32,256]{3,2,1,0:T(8,128)S(1)} %shard_map.93.finished, f32[9,32,128]{2,1,0:T(8,128)S(1)} %get-tuple-element.25.refs_0_, f32[9,32,128]{2,1,0:T(8,128)S(1)} %collective-permute-done.1.refs_1_, f32[9,32,128]{2,1,0:T(8,128)S(1)} %collective-permute-done.2.refs_2_, ...), custom_call_target="tpu_custom_call" | custom-call | flops 2000000000 | bytes 8000000 | tf_op jit(solution)/shard_map/pallas_call | solution.py:495
  53.3 0.0 copy-start.2
  53.4 50.7 %all_to_all.10 = f32[32,64,256]{2,1,0:T(8,128)S(1)} all-to-all(f32[32,64,256]{2,1,0:T(8,128)S(1)} %bitcast.5), channel_id=1, replica_groups=mesh['row'=4,'col'=8] {'row','col'}, dimensions={0} | all-to-all | bytes 4194304 | tf_op jit(solution)/shard_map/all_to_all | solution.py:586
  104.1 0.0 copy-done.2
  104.1 3.4 %shard_map.95 = (f32[512,256]{1,0:T(8,128)S(1)}, f32[512,256]{1,0:T(8,128)S(1)}, f32[512,256]{1,0:T(8,128)S(1)}, f32[512,256]{1,0:T(8,128)S(1)}) custom-call(s32[2]{0:T(128)S(1)} %pad_add_fusion.place, f32[4,512,256]{2,1,0:T(8,128)S(1)} %bitcast.6, bf16[2,16,256,256]{3,2,1,0:T(8,128)(2,1)S(1)} %copy-done.2), custom_call_target="tpu_custom_call" | custom-call | flops 2500000000 | bytes 10000000 | tf_op jit(solution)/shard_map/pallas_call | solution.py:495
  107.5 1.3 collective-permute-start.8
  108.8 0.7 collective-permute-start.9
  109.5 1.5 collective-permute-start.10
  111.0 18.9 %collective-permute-done.8.refs_1_ = f32[512,256]{1,0:T(8,128)S(1)} collective-permute-done((f32[512,256]{1,0:T(8,128)S(1)}, f32[512,256]{1,0:T(8,128)S(1)}, u32[]{:S(2)}, u32[]{:S(2)}) %collective-permute-start.8) | collective-permute-done | bytes 524320 | tf_op jit(solution)/shard_map/ppermute | solution.py:604
  130.0 14.3 %collective-permute-done.9.refs_2_ = f32[512,256]{1,0:T(8,128)S(1)} collective-permute-done((f32[512,256]{1,0:T(8,128)S(1)}, f32[512,256]{1,0:T(8,128)S(1)}, u32[]{:S(2)}, u32[]{:S(2)}) %collective-permute-start.9) | collective-permute-done | bytes 524320 | tf_op jit(solution)/shard_map/ppermute | solution.py:604
  144.3 12.2 %collective-permute-done.10.refs_3_ = f32[512,256]{1,0:T(8,128)S(1)} collective-permute-done((f32[512,256]{1,0:T(8,128)S(1)}, f32[512,256]{1,0:T(8,128)S(1)}, u32[]{:S(2)}, u32[]{:S(2)}) %collective-permute-start.10) | collective-permute-done | bytes 524320 | tf_op jit(solution)/shard_map/ppermute | solution.py:604
  156.5 1.9 %shard_map.96 = f32[2,512,512]{2,1,0:T(8,128)} custom-call(s32[2]{0:T(128)S(1)} %pad_add_fusion.place, f32[512,256]{1,0:T(8,128)S(1)} %get-tuple-element.33.refs_0_, f32[512,256]{1,0:T(8,128)S(1)} %collective-permute-done.8.refs_1_, f32[512,256]{1,0:T(8,128)S(1)} %collective-permute-done.9.refs_2_, f32[512,256]{1,0:T(8,128)S(1)} %collective-permute-done.10.refs_3_), custom_call_target="tpu_custom_call" | custom-call | tf_op jit(solution)/shard_map/pallas_call | solution.py:607
Async XLA Ops:
  16.0 9.0 %collective-permute-start = (f32[2,9,32,128]{3,2,1,0:T(8,128)}, f32[2,9,32,128]{3,2,1,0:T(8,128)S(1)}, u32[]{:S(2)}, u32[]{:S(2)}) collective-permute-start(f32[2,9,32,128]{3,2,1,0:T(8,128)} %get-tuple-element.22), channel_id=1, source_target_pairs={{0,8},{8,16},{16,24},{24,0},{1,9},{9,17},{17,25},{25,1},{2,10},{10... | collective-permute-start | bytes 884744 | tf_op jit(solution)/shard_map/ppermute | solution.py:549
  17.6 23.5 %all-to-all-start = ((f32[8,9,32,128]{3,2,1,0:T(8,128)}), f32[8,9,32,128]{3,2,1,0:T(8,128)S(1)}, u32[]{:S(2)}, u32[]{:S(2)}) async-start(f32[8,9,32,128]{3,2,1,0:T(8,128)} %get-tuple-element.24), calls=%async_computation | async-start | bytes 2359296 | tf_op jit(solution)/shard_map/all_to_all | solution.py:550
  25.0 1.3 copy-start.3
  27.1 3.6 %collective-permute-start.1 = (f32[9,32,128]{2,1,0:T(8,128)S(1)}, f32[9,32,128]{2,1,0:T(8,128)S(1)}, u32[]{:S(2)}, u32[]{:S(2)}) collective-permute-start(f32[9,32,128]{2,1,0:T(8,128)S(1)} %get-tuple-element.26), channel_id=1, source_target_pairs={{0,1},{1,0},{2,3},{3,2},{4,5},{5,4},{6,7},{7,6},{8,9},{9,8},{10,11... | collective-permute-start | bytes 442376 | tf_op jit(solution)/shard_map/ppermute | solution.py:556
  27.2 13.7 %collective-permute-start.2 = (f32[9,32,128]{2,1,0:T(8,128)S(1)}, f32[9,32,128]{2,1,0:T(8,128)S(1)}, u32[]{:S(2)}, u32[]{:S(2)}) collective-permute-start(f32[9,32,128]{2,1,0:T(8,128)S(1)} %get-tuple-element.27), channel_id=1, source_target_pairs={{0,2},{1,3},{2,0},{3,1},{4,6},{5,7},{6,4},{7,5},{8,10},{9,11},{10,... | collective-permute-start | bytes 442376 | tf_op jit(solution)/shard_map/ppermute | solution.py:556
  28.8 16.9 %collective-permute-start.3 = (f32[9,32,128]{2,1,0:T(8,128)S(1)}, f32[9,32,128]{2,1,0:T(8,128)S(1)}, u32[]{:S(2)}, u32[]{:S(2)}) collective-permute-start(f32[9,32,128]{2,1,0:T(8,128)S(1)} %get-tuple-element.28), channel_id=1, source_target_pairs={{0,3},{1,2},{2,1},{3,0},{4,7},{5,6},{6,5},{7,4},{8,11},{9,10},{10,... | collective-permute-start | bytes 442376 | tf_op jit(solution)/shard_map/ppermute | solution.py:556
  29.1 16.6 %collective-permute-start.4 = (f32[9,32,128]{2,1,0:T(8,128)S(1)}, f32[9,32,128]{2,1,0:T(8,128)S(1)}, u32[]{:S(2)}, u32[]{:S(2)}) collective-permute-start(f32[9,32,128]{2,1,0:T(8,128)S(1)} %get-tuple-element.29), channel_id=1, source_target_pairs={{0,4},{1,5},{2,6},{3,7},{4,0},{5,1},{6,2},{7,3},{8,12},{9,13},{10,... | collective-permute-start | bytes 442376 | tf_op jit(solution)/shard_map/ppermute | solution.py:556
  30.6 15.1 %collective-permute-start.5 = (f32[9,32,128]{2,1,0:T(8,128)S(1)}, f32[9,32,128]{2,1,0:T(8,128)S(1)}, u32[]{:S(2)}, u32[]{:S(2)}) collective-permute-start(f32[9,32,128]{2,1,0:T(8,128)S(1)} %get-tuple-element.30), channel_id=1, source_target_pairs={{0,5},{1,4},{2,7},{3,6},{4,1},{5,0},{6,3},{7,2},{8,13},{9,12},{10,... | collective-permute-start | bytes 442376 | tf_op jit(solution)/shard_map/ppermute | solution.py:556
  30.8 17.4 %collective-permute-start.6 = (f32[9,32,128]{2,1,0:T(8,128)S(1)}, f32[9,32,128]{2,1,0:T(8,128)S(1)}, u32[]{:S(2)}, u32[]{:S(2)}) collective-permute-start(f32[9,32,128]{2,1,0:T(8,128)S(1)} %get-tuple-element.31), channel_id=1, source_target_pairs={{0,6},{1,7},{2,4},{3,5},{4,2},{5,3},{6,0},{7,1},{8,14},{9,15},{10,... | collective-permute-start | bytes 442376 | tf_op jit(solution)/shard_map/ppermute | solution.py:556
  40.9 9.4 %collective-permute-start.7 = (f32[9,32,128]{2,1,0:T(8,128)S(1)}, f32[9,32,128]{2,1,0:T(8,128)S(1)}, u32[]{:S(2)}, u32[]{:S(2)}) collective-permute-start(f32[9,32,128]{2,1,0:T(8,128)S(1)} %get-tuple-element.32), channel_id=1, source_target_pairs={{0,7},{1,6},{2,5},{3,4},{4,3},{5,2},{6,1},{7,0},{8,15},{9,14},{10,... | collective-permute-start | bytes 442376 | tf_op jit(solution)/shard_map/ppermute | solution.py:556
  41.1 2.2 %copy-start = (bf16[2,32,128,256]{3,2,1,0:T(8,128)(2,1)S(1)}, bf16[2,32,128,256]{3,2,1,0:T(8,128)(2,1)}, u32[]{:S(2)}) copy-start(bf16[2,32,128,256]{3,2,1,0:T(8,128)(2,1)} %constant.21.clone.refs_1_.refs_8_) | copy-start | bytes 12582916
  43.3 7.0 %copy-start.1 = (bf16[2,32,128,256]{3,2,1,0:T(8,128)(2,1)S(1)}, bf16[2,32,128,256]{3,2,1,0:T(8,128)(2,1)}, u32[]{:S(2)}) copy-start(bf16[2,32,128,256]{3,2,1,0:T(8,128)(2,1)} %constant.21.clone.refs_1_.refs_8_) | copy-start | bytes 12582916
  53.3 50.7 %copy-start.2 = (bf16[2,16,256,256]{3,2,1,0:T(8,128)(2,1)S(1)}, bf16[2,16,256,256]{3,2,1,0:T(8,128)(2,1)}, u32[]{:S(2)}) copy-start(bf16[2,16,256,256]{3,2,1,0:T(8,128)(2,1)} %constant.22.clone.table) | copy-start | bytes 12582916
  107.5 22.5 %collective-permute-start.8 = (f32[512,256]{1,0:T(8,128)S(1)}, f32[512,256]{1,0:T(8,128)S(1)}, u32[]{:S(2)}, u32[]{:S(2)}) collective-permute-start(f32[512,256]{1,0:T(8,128)S(1)} %get-tuple-element.34), channel_id=1, source_target_pairs={{0,8},{8,0},{16,24},{24,16},{1,9},{9,1},{17,25},{25,17},{2,10},{10... | collective-permute-start | bytes 1572872 | tf_op jit(solution)/shard_map/ppermute | solution.py:604
  108.8 35.5 %collective-permute-start.9 = (f32[512,256]{1,0:T(8,128)S(1)}, f32[512,256]{1,0:T(8,128)S(1)}, u32[]{:S(2)}, u32[]{:S(2)}) collective-permute-start(f32[512,256]{1,0:T(8,128)S(1)} %get-tuple-element.35), channel_id=1, source_target_pairs={{0,16},{8,24},{16,0},{24,8},{1,17},{9,25},{17,1},{25,9},{2,18},{10... | collective-permute-start | bytes 1572872 | tf_op jit(solution)/shard_map/ppermute | solution.py:604
  109.5 46.9 %collective-permute-start.10 = (f32[512,256]{1,0:T(8,128)S(1)}, f32[512,256]{1,0:T(8,128)S(1)}, u32[]{:S(2)}, u32[]{:S(2)}) collective-permute-start(f32[512,256]{1,0:T(8,128)S(1)} %get-tuple-element.36), channel_id=1, source_target_pairs={{0,24},{8,16},{16,8},{24,0},{1,25},{9,17},{17,9},{25,1},{2,26},{10... | collective-permute-start | bytes 1572872 | tf_op jit(solution)/shard_map/ppermute | solution.py:604

commit v4 on v3

--- a/solution.py
+++ b/solution.py
@@ -114,7 +114,7 @@
     return low + high
 
 
-def tile_pass(load, target, table, sign):
+def tile_pass(load, target, table, sign, after=None):
     part = table.shape[1] // 2
     for chunk in range(target.shape[1]):
         values = [
@@ -135,6 +135,8 @@
             rows = pl.ds(residue, part, stride=RADIX)
             target[0, chunk, rows, :] = real
             target[1, chunk, rows, :] = imag
+        if after is not None:
+            after(chunk)
 
 
 def transpose_all(source, target):
@@ -149,7 +151,8 @@
 
 
 def refine_kernel(starts, *refs):
-    sources, (late, early, below), refs = refs[:6], refs[6:9], refs[9:]
+    sources, results, refs = refs[:6], refs[6:9], refs[9:]
+    (late, early, below), sent, refs = refs[:3], refs[3], refs[4:]
     held, (first, second, updates, arrived, done) = refs[:6], refs[6:]
     tiles, table, pupils, intensity, row_table, col_table = held
     length = tiles.shape[1]
@@ -272,31 +275,44 @@
             first[side, chunk + 1, pl.ds(row, window), :] += jnp.where(lane >= shift, 0.0, moved)
         return carry
 
-    lax.fori_loop(0, leds, place, 0, unroll=4)
+    lax.fori_loop(0, leds, place, 0, unroll=8)
     tile_pass(from_first, second, table, 1)
     transpose_all(second, first)
-    tile_pass(from_first, second, table, 1)
     whole = (length - OVL) // LANES
     count, _, rows, _ = late.shape
-
-    def emit(target, part, row, gain):
-        here = pl.ds(row, rows)
-        for side in range(2):
-            for chunk in range(whole):
-                target[part, side * whole + chunk] = scaled(second[side, chunk, here, :], gain)
-        near = second[0, whole, here, :]
-        far = pltpu.roll(second[1, whole, here, :], OVL, 1)
-        low = lax.broadcasted_iota(jnp.int32, near.shape, 1) < OVL
-        target[part, 2 * whole] = scaled(jnp.where(low, near, far), gain)
-
-    for part in range(count):
-        segment, offset = divmod(part * rows, OVL)
-        emit(late, part, segment * LANES + OVL + offset, None)
-        ramp = None
-        if segment == 0:
-            ramp = ramp_of(offset + lax.broadcasted_iota(jnp.int32, (rows, LANES), 0))
-            emit(below, part, whole * LANES + offset, 1.0 - ramp)
-        emit(early, part, segment * LANES + offset, ramp)
+    sends = []
+
+    def emit(chunk):
+        def put(target, piece, part, row, gain):
+            here = pl.ds(row, rows)
+            if chunk < whole:
+                value = second[piece // whole, chunk, here, :]
+            else:
+                far = pltpu.roll(second[1, whole, here, :], OVL, 1)
+                low = lax.broadcasted_iota(jnp.int32, far.shape, 1) < OVL
+                value = jnp.where(low, second[0, whole, here, :], far)
+            target[part, piece] = scaled(value, gain)
+
+        for piece in (chunk, whole + chunk) if chunk < whole else (2 * whole,):
+            for part in range(count):
+                segment, offset = divmod(part * rows, OVL)
+                put(late, piece, part, segment * LANES + OVL + offset, None)
+                ramp = None
+                if segment == 0:
+                    ramp = ramp_of(offset + lax.broadcasted_iota(jnp.int32, (rows, LANES), 0))
+                    put(below, piece, part, whole * LANES + offset, 1.0 - ramp)
+                put(early, piece, part, segment * LANES + offset, ramp)
+            for source, target in zip((late, early, below), results):
+                sends.append(
+                    pltpu.make_async_copy(
+                        source.at[:, piece], target.at[:, piece], sent.at[len(sends)]
+                    )
+                )
+                sends[-1].start()
+
+    tile_pass(from_first, second, table, 1, emit)
+    for copy in sends:
+        copy.wait()
 
 
 def scaled(value, gain):
@@ -320,18 +336,20 @@
             out[...] += above[jnp.minimum(part, blended - 1)]
 
 
-UNROLL = 8
+UNROLL = 16
 GROUP = 4
 BESIDE = 4
 
 
 def gather_kernel(place, finished, *refs):
-    *blocks, table, out, values, held = refs
+    *blocks, table, out, values, held, done = refs
     rows = finished.shape[2]
+    copy = pltpu.make_async_copy(finished, out.at[:, :, pl.ds(0, rows), :], done)
+    copy.start()
     for step, block in enumerate(blocks):
         values[jnp.bitwise_xor(place[0], step)] = block[...]
-    out[:, :, pl.ds(0, rows), :] = finished[...]
     col_kernel(values, table, out.at[:, :, pl.ds(rows, rows), :], held)
+    copy.wait()
 
 
 def after_kernel(after, *refs):
@@ -457,20 +475,11 @@
         leave_as(me)
 
 
-def join_kernel(place, *refs):
-    *blocks, out, ordered, done = refs
+def join_kernel(steps, place, *refs):
+    blocks, out, done = refs[: len(steps)], refs[-2], refs[-1]
     width = blocks[0].shape[1] // 2
-    if width % LANES:
-        for step, block in enumerate(blocks):
-            part = jnp.bitwise_xor(place[1], step)
-            ordered[part] = block[...]
-        for part in range(len(blocks)):
-            for side in range(2):
-                lanes = pl.ds(part * width, width)
-                out[side, :, lanes] = ordered[part, :, pl.ds(side * width, width)]
-        return
     copies = []
-    for step, block in enumerate(blocks):
+    for step, block in zip(steps, blocks):
         part = jnp.bitwise_xor(place[1], step)
         lanes = pl.ds(pl.multiple_of(part * width, LANES), width)
         for side in range(2):
@@ -486,12 +495,23 @@
         copy.wait()
 
 
+def narrow_join_kernel(place, *refs):
+    *blocks, out, ordered = refs
+    width = blocks[0].shape[1] // 2
+    for step, block in enumerate(blocks):
+        ordered[jnp.bitwise_xor(place[1], step)] = block[...]
+    for part in range(len(blocks)):
+        for side in range(2):
+            lanes = pl.ds(part * width, width)
+            out[side, :, lanes] = ordered[part, :, pl.ds(side * width, width)]
+
+
 VMEM = pl.BlockSpec(memory_space=pltpu.VMEM)
 SMEM = pl.BlockSpec(memory_space=pltpu.SMEM)
 HBM = pl.BlockSpec(memory_space=pltpu.HBM)
 
 
-def call(kernel, shapes, scratch, limit, micros, *operands, scalars=0, outside=()):
+def call(kernel, shapes, scratch, limit, micros, *operands, scalars=0, outside=(), to=None):
     return pl.pallas_call(
         kernel,
         out_shape=[jax.ShapeDtypeStruct(shape, F32) for shape in shapes],
@@ -499,7 +519,7 @@
             SMEM if place < scalars else HBM if place - len(operands) in outside else VMEM
             for place in range(len(operands))
         ],
-        out_specs=[VMEM] * len(shapes),
+        out_specs=[to or VMEM] * len(shapes),
         scratch_shapes=scratch,
         cost_estimate=pl.CostEstimate(
             flops=int(micros * 5e8), bytes_accessed=int(micros * 2e6), transcendentals=0
@@ -528,10 +548,13 @@
         along_left(left_block(dft_matrix(window))),
     )
     buffer = pltpu.VMEM((2, chunks, length, LANES), F32)
+    results = [(col_count, *block), (col_count, *block), (OVL // rows, *block)]
     late, early, below = call(
         refine_kernel,
-        [(col_count, *block), (col_count, *block), (OVL // rows, *block)],
-        [pltpu.VMEM(operand.shape, operand.dtype) for operand in operands]
+        results,
+        [pltpu.VMEM(shape, F32) for shape in results]
+        + [pltpu.SemaphoreType.DMA((len(results) * block[0],))]
+        + [pltpu.VMEM(operand.shape, operand.dtype) for operand in operands]
         + [
             buffer,
             buffer,
@@ -545,6 +568,7 @@
         *operands,
         scalars=1,
         outside=range(-len(operands), 0),
+        to=HBM,
     )
     above = lax.ppermute(below, "row", [(r, (r + 1) % row_count) for r in range(row_count)])
     late = lax.all_to_all(late, "col", split_axis=0, concat_axis=0, tiled=True)
@@ -573,7 +597,7 @@
     (field,) = call(
         gather_kernel,
         [(row_count, col_count, 2 * rows, 2 * width)],
-        [pltpu.VMEM((col_count, *block), F32)] + scratch,
+        [pltpu.VMEM((col_count, *block), F32)] + scratch + [pltpu.SemaphoreType.DMA],
         32,
         4,
         place,
@@ -604,17 +628,27 @@
         lax.ppermute(blocks[step], "row", [(r, r ^ step) for r in range(row_count)])
         for step in range(1, row_count)
     ]
-    return pl.pallas_call(
-        join_kernel,
-        out_shape=jax.ShapeDtypeStruct((2, stride, stride), F32),
-        in_specs=[SMEM] + [VMEM] * row_count,
-        out_specs=VMEM if width % LANES else HBM,
-        scratch_shapes=[
-            pltpu.VMEM((row_count, *shape) if width % LANES else (8, LANES), F32),
-            pltpu.SemaphoreType.DMA((2 * row_count,)),
-        ],
-        compiler_params=pltpu.CompilerParams(vmem_limit_bytes=16 << 20),
-    )(place, *blocks)
+    whole_shape = (2, stride, stride)
+    if width % LANES:
+        scratch = [pltpu.VMEM((row_count, *shape), F32)]
+        (field,) = call(
+            narrow_join_kernel, [whole_shape], scratch, 32, 2, place, *blocks, scalars=1
+        )
+        return field
+
+    def join(steps, field):
+        prior = [] if field is None else [field]
+        return pl.pallas_call(
+            functools.partial(join_kernel, steps),
+            out_shape=jax.ShapeDtypeStruct(whole_shape, F32),
+            in_specs=[SMEM] + [VMEM] * len(steps) + [HBM] * len(prior),
+            out_specs=HBM,
+            scratch_shapes=[pltpu.SemaphoreType.DMA((2 * len(steps),))],
+            input_output_aliases={1 + len(steps): 0} if prior else {},
+            compiler_params=pltpu.CompilerParams(vmem_limit_bytes=16 << 20),
+        )(place, *[blocks[step] for step in steps], *prior)
+
+    return join([row_count - 1], join(range(row_count - 1), None))
 
 
 def solution(mesh):

time: 159 us -> 157 us (0.987)
    ppermute x3, waiting for transfers between devices: 45.5 us -> 43.7 us  [local(): lax.ppermute(blocks[step], 'row', [(r, r ^ step) for r in range(row_count)])]
  transfers between devices with their start and end apart: 12 -> 12, of which waited for: 7 -> 7; matrix products, arithmetic and copies ran while one was open for 0% -> 0% of each run, Pallas kernels for 2% -> 3%
where the time goes in v4:
time: 157 us
  waiting for transfers between devices  60 us (38%)
  blocking collectives  50.7 us (32%)
  Pallas kernels  27.3 us (17%)
  starting transfers between devices  15.2 us (10%)
  local copies, waits for them, and re-layouts  3.47 us (2%)
    all_to_all x1, blocking collectives, local(): lax.all_to_all(field, ('row', 'col'), split_axis=0, concat_axis=0, tiled=...  50.7 us
    ppermute x3, waiting for transfers between devices, local(): lax.ppermute(blocks[step], 'row', [(r, r ^ step) for r in range(row_count)])  43.7 us
    pallas_call x5, Pallas kernels, call(): pl.pallas_call(kernel, out_shape=[jax.ShapeDtypeStruct(shape, F32) for sh...  24.2 us
    ppermute x7, waiting for transfers between devices, local(): lax.ppermute(early[step], 'col', [(c, c ^ step) for c in range(col_count)])  12.7 us
    ppermute x7, starting transfers between devices, local(): lax.ppermute(early[step], 'col', [(c, c ^ step) for c in range(col_count)])  6.27 us
    all_to_all x1, starting transfers between devices, local(): late = lax.all_to_all(late, 'col', split_axis=0, concat_axis=0, tiled=True)  3.72 us
    ppermute x1, waiting for transfers between devices, local(): lax.ppermute(below, 'row', [(r, (r + 1) % row_count) for r in range(row_c...  3.59 us
    ppermute x3, starting transfers between devices, local(): lax.ppermute(blocks[step], 'row', [(r, r ^ step) for r in range(row_count)])  3.55 us
  transfers between devices with their start and end apart: 12, of which 7 were waited for; matrix products, arithmetic and copies ran while one was open for 0% of the time, Pallas kernels for 3%

profile of v4, /device:TPU:8, one launch (start us, length us, event | category | flops | bytes accessed | tf_op | source)
XLA Modules:
  0.0 157.0 jit_solution(2824183524070438880)
XLA Ops:
  0.0 15.3 %shard_map.91 = (f32[8,9,32,128]{3,2,1,0:T(8,128)}, f32[8,9,32,128]{3,2,1,0:T(8,128)}, f32[2,9,32,128]{3,2,1,0:T(8,128)}) custom-call(s32[2,16]{1,0:T(2,128)} %bitcast.7, f32[2,576,576]{2,1,0:T(8,128)} %refs_0_.1, bf16[8,144,216]{2,1,0:T(8,128)(2,1)} %constant.18.clone.refs_1_, f32[2,128,128]{2,1,0:T(8,128)} %refs_2_.1, f32[16,128,128]{2,1,0:T(8,128)} %refs_3_.1, ...), custom_call_target="tpu_custom_call" | custom-call | flops 11000000512 | bytes 44000000 | tf_op jit(solution)/shard_map/pallas_call | solution.py:515
  15.3 1.7 %collective-permute-start = (f32[2,9,32,128]{3,2,1,0:T(8,128)}, f32[2,9,32,128]{3,2,1,0:T(8,128)S(1)}, u32[]{:S(2)}, u32[]{:S(2)}) collective-permute-start(f32[2,9,32,128]{3,2,1,0:T(8,128)} %get-tuple-element.22), channel_id=1, source_target_pairs={{0,8},{8,16},{16,24},{24,0},{1,9},{9,17},{17,25},{25,1},{2,10},{10... | collective-permute-start | bytes 884744 | tf_op jit(solution)/shard_map/ppermute | solution.py:573
  17.0 3.7 %all-to-all-start = ((f32[8,9,32,128]{3,2,1,0:T(8,128)}), f32[8,9,32,128]{3,2,1,0:T(8,128)S(1)}, u32[]{:S(2)}, u32[]{:S(2)}) async-start(f32[8,9,32,128]{3,2,1,0:T(8,128)} %get-tuple-element.24), calls=%async_computation | async-start | bytes 2359296 | tf_op jit(solution)/shard_map/all_to_all | solution.py:574
  20.7 0.1 pad_add_fusion.place
  20.8 3.6 %collective-permute-done.above = f32[2,9,32,128]{3,2,1,0:T(8,128)S(1)} collective-permute-done((f32[2,9,32,128]{3,2,1,0:T(8,128)}, f32[2,9,32,128]{3,2,1,0:T(8,128)S(1)}, u32[]{:S(2)}, u32[]{:S(2)}) %collective-permute-start) | collective-permute-done | bytes 294944 | tf_op jit(solution)/shard_map/ppermute | solution.py:573
  24.4 0.0 copy-start.3
  24.4 1.3 copy-done.3
  25.7 0.9 shard_map.92
  26.5 0.1 collective-permute-start.1
  26.6 1.5 collective-permute-start.2
  28.2 0.3 collective-permute-start.3
  28.5 1.5 collective-permute-start.4
  30.0 0.2 collective-permute-start.5
  30.2 0.0 collective-permute-done.1.refs_1_
  30.2 2.4 %collective-permute-start.6 = (f32[9,32,128]{2,1,0:T(8,128)S(1)}, f32[9,32,128]{2,1,0:T(8,128)S(1)}, u32[]{:S(2)}, u32[]{:S(2)}) collective-permute-start(f32[9,32,128]{2,1,0:T(8,128)S(1)} %get-tuple-element.31), channel_id=1, source_target_pairs={{0,6},{1,7},{2,4},{3,5},{4,2},{5,3},{6,0},{7,1},{8,14},{9,15},{10,... | collective-permute-start | bytes 442376 | tf_op jit(solution)/shard_map/ppermute | solution.py:580
  32.6 7.7 %collective-permute-done.2.refs_2_ = f32[9,32,128]{2,1,0:T(8,128)S(1)} collective-permute-done((f32[9,32,128]{2,1,0:T(8,128)S(1)}, f32[9,32,128]{2,1,0:T(8,128)S(1)}, u32[]{:S(2)}, u32[]{:S(2)}) %collective-permute-start.2) | collective-permute-done | bytes 147488 | tf_op jit(solution)/shard_map/ppermute | solution.py:580
  40.3 0.2 collective-permute-start.7
  40.5 0.0 all-to-all-done.refs_0_
  40.5 0.0 copy-start
  40.5 2.2 %copy-done = bf16[2,32,128,256]{3,2,1,0:T(8,128)(2,1)S(1)} copy-done((bf16[2,32,128,256]{3,2,1,0:T(8,128)(2,1)S(1)}, bf16[2,32,128,256]{3,2,1,0:T(8,128)(2,1)}, u32[]{:S(2)}) %copy-start) | copy-done | bytes 4194328
  42.7 0.0 copy-start.1
  42.7 2.0 %shard_map.93.finished = f32[4,8,32,256]{3,2,1,0:T(8,128)S(1)} custom-call(f32[8,128]{1,0:T(8,128)S(1)} %get-tuple-element.23.after, f32[8,9,32,128]{3,2,1,0:T(8,128)S(1)} %all-to-all-done.refs_0_, bf16[2,32,128,256]{3,2,1,0:T(8,128)(2,1)S(1)} %copy-done), custom_call_target="tpu_custom_call" | custom-call | flops 2000000000 | bytes 8000000 | tf_op jit(solution)/shard_map/pallas_call | solution.py:515
  44.7 0.0 collective-permute-done.3.refs_3_
  44.8 0.0 collective-permute-done.4.refs_4_
  44.8 0.0 collective-permute-done.5.refs_5_
  44.8 2.8 %collective-permute-done.6.refs_6_ = f32[9,32,128]{2,1,0:T(8,128)S(1)} collective-permute-done((f32[9,32,128]{2,1,0:T(8,128)S(1)}, f32[9,32,128]{2,1,0:T(8,128)S(1)}, u32[]{:S(2)}, u32[]{:S(2)}) %collective-permute-start.6) | collective-permute-done | bytes 147488 | tf_op jit(solution)/shard_map/ppermute | solution.py:580
  47.5 2.2 %collective-permute-done.7.refs_7_ = f32[9,32,128]{2,1,0:T(8,128)S(1)} collective-permute-done((f32[9,32,128]{2,1,0:T(8,128)S(1)}, f32[9,32,128]{2,1,0:T(8,128)S(1)}, u32[]{:S(2)}, u32[]{:S(2)}) %collective-permute-start.7) | collective-permute-done | bytes 147488 | tf_op jit(solution)/shard_map/ppermute | solution.py:580
  49.7 0.0 copy-done.1
  49.7 2.8 %shard_map.94 = f32[4,8,64,256]{3,2,1,0:T(8,128)S(1)} custom-call(s32[2]{0:T(128)S(1)} %pad_add_fusion.place, f32[4,8,32,256]{3,2,1,0:T(8,128)S(1)} %shard_map.93.finished, f32[9,32,128]{2,1,0:T(8,128)S(1)} %get-tuple-element.25.refs_0_, f32[9,32,128]{2,1,0:T(8,128)S(1)} %collective-permute-done.1.refs_1_, f32[9,32,128]{2,1,0:T(8,128)S(1)} %collective-permute-done.2.refs_2_, ...), custom_call_target="tpu_custom_call" | custom-call | flops 2000000000 | bytes 8000000 | tf_op jit(solution)/shard_map/pallas_call | solution.py:515
  52.5 0.0 copy-start.2
  52.5 50.7 %all_to_all.10 = f32[32,64,256]{2,1,0:T(8,128)S(1)} all-to-all(f32[32,64,256]{2,1,0:T(8,128)S(1)} %bitcast.5), channel_id=1, replica_groups=mesh['row'=4,'col'=8] {'row','col'}, dimensions={0} | all-to-all | bytes 4194304 | tf_op jit(solution)/shard_map/all_to_all | solution.py:610
  103.2 0.0 copy-done.2
  103.2 3.2 %shard_map.95 = (f32[512,256]{1,0:T(8,128)S(1)}, f32[512,256]{1,0:T(8,128)S(1)}, f32[512,256]{1,0:T(8,128)S(1)}, f32[512,256]{1,0:T(8,128)S(1)}) custom-call(s32[2]{0:T(128)S(1)} %pad_add_fusion.place, f32[4,512,256]{2,1,0:T(8,128)S(1)} %bitcast.6, bf16[2,16,256,256]{3,2,1,0:T(8,128)(2,1)S(1)} %copy-done.2), custom_call_target="tpu_custom_call" | custom-call | flops 2500000000 | bytes 10000000 | tf_op jit(solution)/shard_map/pallas_call | solution.py:515
  106.5 1.4 collective-permute-start.9
  107.8 0.7 collective-permute-start.10
  108.6 1.5 collective-permute-start.8
  110.0 19.0 %collective-permute-done.9.refs_1_ = f32[512,256]{1,0:T(8,128)S(1)} collective-permute-done((f32[512,256]{1,0:T(8,128)S(1)}, f32[512,256]{1,0:T(8,128)S(1)}, u32[]{:S(2)}, u32[]{:S(2)}) %collective-permute-start.9) | collective-permute-done | bytes 524320 | tf_op jit(solution)/shard_map/ppermute | solution.py:628
  129.0 14.3 %collective-permute-done.10.refs_2_ = f32[512,256]{1,0:T(8,128)S(1)} collective-permute-done((f32[512,256]{1,0:T(8,128)S(1)}, f32[512,256]{1,0:T(8,128)S(1)}, u32[]{:S(2)}, u32[]{:S(2)}) %collective-permute-start.10) | collective-permute-done | bytes 524320 | tf_op jit(solution)/shard_map/ppermute | solution.py:628
  143.3 1.7 %shard_map.96.refs_1_ = f32[2,512,512]{2,1,0:T(8,128)} custom-call(s32[2]{0:T(128)S(1)} %pad_add_fusion.place, f32[512,256]{1,0:T(8,128)S(1)} %get-tuple-element.34.refs_0_, f32[512,256]{1,0:T(8,128)S(1)} %collective-permute-done.9.refs_1_, f32[512,256]{1,0:T(8,128)S(1)} %collective-permute-done.10.refs_2_), custom_call_target="tpu_custom_call" | custom-call | tf_op jit(solution)/shard_map/pallas_call | solution.py:641
  145.1 10.4 %collective-permute-done.8.refs_0_ = f32[512,256]{1,0:T(8,128)S(1)} collective-permute-done((f32[512,256]{1,0:T(8,128)S(1)}, f32[512,256]{1,0:T(8,128)S(1)}, u32[]{:S(2)}, u32[]{:S(2)}) %collective-permute-start.8) | collective-permute-done | bytes 524320 | tf_op jit(solution)/shard_map/ppermute | solution.py:628
  155.5 1.3 shard_map.97
Async XLA Ops:
  15.3 9.0 %collective-permute-start = (f32[2,9,32,128]{3,2,1,0:T(8,128)}, f32[2,9,32,128]{3,2,1,0:T(8,128)S(1)}, u32[]{:S(2)}, u32[]{:S(2)}) collective-permute-start(f32[2,9,32,128]{3,2,1,0:T(8,128)} %get-tuple-element.22), channel_id=1, source_target_pairs={{0,8},{8,16},{16,24},{24,0},{1,9},{9,17},{17,25},{25,1},{2,10},{10... | collective-permute-start | bytes 884744 | tf_op jit(solution)/shard_map/ppermute | solution.py:573
  17.0 23.5 %all-to-all-start = ((f32[8,9,32,128]{3,2,1,0:T(8,128)}), f32[8,9,32,128]{3,2,1,0:T(8,128)S(1)}, u32[]{:S(2)}, u32[]{:S(2)}) async-start(f32[8,9,32,128]{3,2,1,0:T(8,128)} %get-tuple-element.24), calls=%async_computation | async-start | bytes 2359296 | tf_op jit(solution)/shard_map/all_to_all | solution.py:574
  24.4 1.3 copy-start.3
  26.5 3.6 %collective-permute-start.1 = (f32[9,32,128]{2,1,0:T(8,128)S(1)}, f32[9,32,128]{2,1,0:T(8,128)S(1)}, u32[]{:S(2)}, u32[]{:S(2)}) collective-permute-start(f32[9,32,128]{2,1,0:T(8,128)S(1)} %get-tuple-element.26), channel_id=1, source_target_pairs={{0,1},{1,0},{2,3},{3,2},{4,5},{5,4},{6,7},{7,6},{8,9},{9,8},{10,11... | collective-permute-start | bytes 442376 | tf_op jit(solution)/shard_map/ppermute | solution.py:580
  26.6 13.7 %collective-permute-start.2 = (f32[9,32,128]{2,1,0:T(8,128)S(1)}, f32[9,32,128]{2,1,0:T(8,128)S(1)}, u32[]{:S(2)}, u32[]{:S(2)}) collective-permute-start(f32[9,32,128]{2,1,0:T(8,128)S(1)} %get-tuple-element.27), channel_id=1, source_target_pairs={{0,2},{1,3},{2,0},{3,1},{4,6},{5,7},{6,4},{7,5},{8,10},{9,11},{10,... | collective-permute-start | bytes 442376 | tf_op jit(solution)/shard_map/ppermute | solution.py:580
  28.2 16.6 %collective-permute-start.3 = (f32[9,32,128]{2,1,0:T(8,128)S(1)}, f32[9,32,128]{2,1,0:T(8,128)S(1)}, u32[]{:S(2)}, u32[]{:S(2)}) collective-permute-start(f32[9,32,128]{2,1,0:T(8,128)S(1)} %get-tuple-element.28), channel_id=1, source_target_pairs={{0,3},{1,2},{2,1},{3,0},{4,7},{5,6},{6,5},{7,4},{8,11},{9,10},{10,... | collective-permute-start | bytes 442376 | tf_op jit(solution)/shard_map/ppermute | solution.py:580
  28.5 16.3 %collective-permute-start.4 = (f32[9,32,128]{2,1,0:T(8,128)S(1)}, f32[9,32,128]{2,1,0:T(8,128)S(1)}, u32[]{:S(2)}, u32[]{:S(2)}) collective-permute-start(f32[9,32,128]{2,1,0:T(8,128)S(1)} %get-tuple-element.29), channel_id=1, source_target_pairs={{0,4},{1,5},{2,6},{3,7},{4,0},{5,1},{6,2},{7,3},{8,12},{9,13},{10,... | collective-permute-start | bytes 442376 | tf_op jit(solution)/shard_map/ppermute | solution.py:580
  30.0 14.8 %collective-permute-start.5 = (f32[9,32,128]{2,1,0:T(8,128)S(1)}, f32[9,32,128]{2,1,0:T(8,128)S(1)}, u32[]{:S(2)}, u32[]{:S(2)}) collective-permute-start(f32[9,32,128]{2,1,0:T(8,128)S(1)} %get-tuple-element.30), channel_id=1, source_target_pairs={{0,5},{1,4},{2,7},{3,6},{4,1},{5,0},{6,3},{7,2},{8,13},{9,12},{10,... | collective-permute-start | bytes 442376 | tf_op jit(solution)/shard_map/ppermute | solution.py:580
  30.2 17.3 %collective-permute-start.6 = (f32[9,32,128]{2,1,0:T(8,128)S(1)}, f32[9,32,128]{2,1,0:T(8,128)S(1)}, u32[]{:S(2)}, u32[]{:S(2)}) collective-permute-start(f32[9,32,128]{2,1,0:T(8,128)S(1)} %get-tuple-element.31), channel_id=1, source_target_pairs={{0,6},{1,7},{2,4},{3,5},{4,2},{5,3},{6,0},{7,1},{8,14},{9,15},{10,... | collective-permute-start | bytes 442376 | tf_op jit(solution)/shard_map/ppermute | solution.py:580
  40.3 9.4 %collective-permute-start.7 = (f32[9,32,128]{2,1,0:T(8,128)S(1)}, f32[9,32,128]{2,1,0:T(8,128)S(1)}, u32[]{:S(2)}, u32[]{:S(2)}) collective-permute-start(f32[9,32,128]{2,1,0:T(8,128)S(1)} %get-tuple-element.32), channel_id=1, source_target_pairs={{0,7},{1,6},{2,5},{3,4},{4,3},{5,2},{6,1},{7,0},{8,15},{9,14},{10,... | collective-permute-start | bytes 442376 | tf_op jit(solution)/shard_map/ppermute | solution.py:580
  40.5 2.2 %copy-start = (bf16[2,32,128,256]{3,2,1,0:T(8,128)(2,1)S(1)}, bf16[2,32,128,256]{3,2,1,0:T(8,128)(2,1)}, u32[]{:S(2)}) copy-start(bf16[2,32,128,256]{3,2,1,0:T(8,128)(2,1)} %constant.21.clone.refs_1_.refs_8_) | copy-start | bytes 12582916
  42.7 7.0 %copy-start.1 = (bf16[2,32,128,256]{3,2,1,0:T(8,128)(2,1)S(1)}, bf16[2,32,128,256]{3,2,1,0:T(8,128)(2,1)}, u32[]{:S(2)}) copy-start(bf16[2,32,128,256]{3,2,1,0:T(8,128)(2,1)} %constant.21.clone.refs_1_.refs_8_) | copy-start | bytes 12582916
  52.5 50.7 %copy-start.2 = (bf16[2,16,256,256]{3,2,1,0:T(8,128)(2,1)S(1)}, bf16[2,16,256,256]{3,2,1,0:T(8,128)(2,1)}, u32[]{:S(2)}) copy-start(bf16[2,16,256,256]{3,2,1,0:T(8,128)(2,1)} %constant.22.clone.table) | copy-start | bytes 12582916
  106.5 22.5 %collective-permute-start.9 = (f32[512,256]{1,0:T(8,128)S(1)}, f32[512,256]{1,0:T(8,128)S(1)}, u32[]{:S(2)}, u32[]{:S(2)}) collective-permute-start(f32[512,256]{1,0:T(8,128)S(1)} %get-tuple-element.35), channel_id=1, source_target_pairs={{0,8},{8,0},{16,24},{24,16},{1,9},{9,1},{17,25},{25,17},{2,10},{10... | collective-permute-start | bytes 1572872 | tf_op jit(solution)/shard_map/ppermute | solution.py:628
  107.8 35.5 %collective-permute-start.10 = (f32[512,256]{1,0:T(8,128)S(1)}, f32[512,256]{1,0:T(8,128)S(1)}, u32[]{:S(2)}, u32[]{:S(2)}) collective-permute-start(f32[512,256]{1,0:T(8,128)S(1)} %get-tuple-element.36), channel_id=1, source_target_pairs={{0,16},{8,24},{16,0},{24,8},{1,17},{9,25},{17,1},{25,9},{2,18},{10... | collective-permute-start | bytes 1572872 | tf_op jit(solution)/shard_map/ppermute | solution.py:628
  108.6 46.9 %collective-permute-start.8 = (f32[512,256]{1,0:T(8,128)S(1)}, f32[512,256]{1,0:T(8,128)S(1)}, u32[]{:S(2)}, u32[]{:S(2)}) collective-permute-start(f32[512,256]{1,0:T(8,128)S(1)} %get-tuple-element.33), channel_id=1, source_target_pairs={{0,24},{8,16},{16,8},{24,0},{1,25},{9,17},{17,9},{25,1},{2,26},{10... | collective-permute-start | bytes 1572872 | tf_op jit(solution)/shard_map/ppermute | solution.py:628

commit v5 on v4

--- a/solution.py
+++ b/solution.py
@@ -230,7 +230,7 @@
         imag = -lens_real * crop[1] - lens_imag * crop[0]
         return jnp.concatenate([real, imag], axis=1)
 
-    def to_waves(leds):
+    def to_waves(leds, value):
         return along_rows(jnp.concatenate([crop(led) for led in leds], axis=0))
 
     def to_wave_cols(leds, wave):
@@ -255,17 +255,6 @@
             imag = grad[m * window : (m + 1) * window, window:]
             updates[led, 0] = -STEP_SIZE * (lens_real * real + lens_imag * imag)
             updates[led, 1] = -STEP_SIZE * (lens_real * imag - lens_imag * real)
-
-    def step(index, carry):
-        groups = [
-            [(index * beside + g) * group + m for m in range(group)] for g in range(beside)
-        ]
-        values = [to_waves(g) for g in groups]
-        for stage in (to_wave_cols, to_grad_cols, to_grads, to_updates):
-            values = [stage(g, value) for g, value in zip(groups, values)]
-        return carry
-
-    lax.fori_loop(0, leds // (group * beside), step, 0)
 
     def place(led, carry):
         chunk, shift, row = place_of(led)
@@ -275,7 +264,28 @@
             first[side, chunk + 1, pl.ds(row, window), :] += jnp.where(lane >= shift, 0.0, moved)
         return carry
 
-    lax.fori_loop(0, leds, place, 0, unroll=8)
+    def to_sum(leds, value):
+        for led in leds:
+            place(led, 0)
+
+    stages = (to_waves, to_wave_cols, to_grad_cols, to_grads, to_updates)
+    if group * beside == leds:
+        stages = stages + (to_sum,)
+        groups = [range(g * group, (g + 1) * group) for g in range(beside)]
+        values = [None] * beside
+        for stage in stages:
+            values = [stage(g, value) for g, value in zip(groups, values)]
+    else:
+
+        def step(index, carry):
+            groups = [[(index * beside + g) * group + m for m in range(group)] for g in range(beside)]
+            values = [None] * beside
+            for stage in stages:
+                values = [stage(g, value) for g, value in zip(groups, values)]
+            return carry
+
+        lax.fori_loop(0, leds // (group * beside), step, 0)
+        lax.fori_loop(0, leds, place, 0, unroll=8)
     tile_pass(from_first, second, table, 1)
     transpose_all(second, first)
     whole = (length - OVL) // LANES
@@ -323,13 +333,19 @@
     return (index.astype(F32) + 0.5) / OVL
 
 
-def spread_kernel(place, early, above, *outs):
-    *outs, token = outs
+def order_kernel(place, early, *outs):
+    for step, out in enumerate(outs):
+        out[...] = early[jnp.bitwise_xor(place[0], step)]
+
+
+def spread_kernel(place, above, *refs):
+    count = len(refs) // 2
+    blocks, outs, token = refs[:count], refs[count:-1], refs[-1]
     token[...] = jnp.zeros(token.shape, F32)
     blended = above.shape[0]
-    for step, out in enumerate(outs):
+    for step, (block, out) in enumerate(zip(blocks, outs)):
         part = jnp.bitwise_xor(place[0], step)
-        out[...] = early[part]
+        out[...] = block[...]
 
         @pl.when(part < blended)
         def _():
@@ -573,8 +589,9 @@
     above = lax.ppermute(below, "row", [(r, (r + 1) % row_count) for r in range(row_count)])
     late = lax.all_to_all(late, "col", split_axis=0, concat_axis=0, tiled=True)
     place = jnp.stack([lax.axis_index("col"), lax.axis_index("row")]).astype(jnp.int32)
+    early = call(order_kernel, [block] * col_count, [], 16, 2, place, early, scalars=1)
     *early, token = call(
-        spread_kernel, [block] * col_count + [(8, LANES)], [], 16, 40, place, early, above, scalars=1
+        spread_kernel, [block] * col_count + [(8, LANES)], [], 16, 40, place, above, *early, scalars=1
     )
     early = [early[0]] + [
         lax.ppermute(early[step], "col", [(c, c ^ step) for c in range(col_count)])

time: 157 us -> 157 us (level)
    pallas_call x5 -> x6, Pallas kernels: 24.2 us -> 24.5 us  [call(): pl.pallas_call(kernel, out_shape=[jax.ShapeDtypeStruct(shape, F32) for sh...]
where the time goes in v5:
time: 157 us
  waiting for transfers between devices  60.6 us (39%)
  blocking collectives  50.7 us (32%)
  Pallas kernels  27.6 us (18%)
  starting transfers between devices  15.3 us (10%)
  local copies, waits for them, and re-layouts  2.2 us (1%)
    all_to_all x1, blocking collectives, local(): lax.all_to_all(field, ('row', 'col'), split_axis=0, concat_axis=0, tiled=...  50.7 us
    ppermute x3, waiting for transfers between devices, local(): lax.ppermute(blocks[step], 'row', [(r, r ^ step) for r in range(row_count)])  43.7 us
    pallas_call x6, Pallas kernels, call(): pl.pallas_call(kernel, out_shape=[jax.ShapeDtypeStruct(shape, F32) for sh...  24.5 us
    ppermute x7, waiting for transfers between devices, local(): lax.ppermute(early[step], 'col', [(c, c ^ step) for c in range(col_count)])  14 us
    ppermute x7, starting transfers between devices, local(): lax.ppermute(early[step], 'col', [(c, c ^ step) for c in range(col_count)])  6.32 us
    all_to_all x1, starting transfers between devices, local(): late = lax.all_to_all(late, 'col', split_axis=0, concat_axis=0, tiled=True)  3.7 us
    ppermute x3, starting transfers between devices, local(): lax.ppermute(blocks[step], 'row', [(r, r ^ step) for r in range(row_count)])  3.55 us
  transfers between devices with their start and end apart: 12, of which 7 were waited for; matrix products, arithmetic and copies ran while one was open for 0% of the time, Pallas kernels for 3%

profile of v5, /device:TPU:8, one launch (start us, length us, event | category | flops | bytes accessed | tf_op | source)
XLA Modules:
  0.0 156.7 jit_solution(9274719356939943034)
XLA Ops:
  0.0 15.0 %shard_map.91 = (f32[8,9,32,128]{3,2,1,0:T(8,128)}, f32[8,9,32,128]{3,2,1,0:T(8,128)}, f32[2,9,32,128]{3,2,1,0:T(8,128)}) custom-call(s32[2,16]{1,0:T(2,128)} %bitcast.7, f32[2,576,576]{2,1,0:T(8,128)} %refs_0_.1, bf16[8,144,216]{2,1,0:T(8,128)(2,1)} %constant.18.clone.refs_1_, f32[2,128,128]{2,1,0:T(8,128)} %refs_2_.1, f32[16,128,128]{2,1,0:T(8,128)} %refs_3_.1, ...), custom_call_target="tpu_custom_call" | custom-call | flops 11000000512 | bytes 44000000 | tf_op jit(solution)/shard_map/pallas_call | solution.py:531
  15.0 0.0 copy-start.3
  15.1 1.7 %collective-permute-start = (f32[2,9,32,128]{3,2,1,0:T(8,128)}, f32[2,9,32,128]{3,2,1,0:T(8,128)S(1)}, u32[]{:S(2)}, u32[]{:S(2)}) collective-permute-start(f32[2,9,32,128]{3,2,1,0:T(8,128)} %get-tuple-element.29), channel_id=1, source_target_pairs={{0,8},{8,16},{16,24},{24,0},{1,9},{9,17},{17,25},{25,1},{2,10},{10... | collective-permute-start | bytes 884744 | tf_op jit(solution)/shard_map/ppermute | solution.py:589
  16.7 3.7 %all-to-all-start = ((f32[8,9,32,128]{3,2,1,0:T(8,128)}), f32[8,9,32,128]{3,2,1,0:T(8,128)S(1)}, u32[]{:S(2)}, u32[]{:S(2)}) async-start(f32[8,9,32,128]{3,2,1,0:T(8,128)} %get-tuple-element.40), calls=%async_computation | async-start | bytes 2359296 | tf_op jit(solution)/shard_map/all_to_all | solution.py:590
  20.4 0.1 pad_add_fusion.place
  20.5 0.0 copy-done.3
  20.5 0.6 shard_map.92
  21.1 2.9 %collective-permute-done.above = f32[2,9,32,128]{3,2,1,0:T(8,128)S(1)} collective-permute-done((f32[2,9,32,128]{3,2,1,0:T(8,128)}, f32[2,9,32,128]{3,2,1,0:T(8,128)S(1)}, u32[]{:S(2)}, u32[]{:S(2)}) %collective-permute-start) | collective-permute-done | bytes 294944 | tf_op jit(solution)/shard_map/ppermute | solution.py:589
  24.1 0.8 shard_map.93
  24.9 0.1 collective-permute-start.1
  25.0 1.6 %collective-permute-start.2 = (f32[9,32,128]{2,1,0:T(8,128)S(1)}, f32[9,32,128]{2,1,0:T(8,128)S(1)}, u32[]{:S(2)}, u32[]{:S(2)}) collective-permute-start(f32[9,32,128]{2,1,0:T(8,128)S(1)} %get-tuple-element.43), channel_id=1, source_target_pairs={{0,2},{1,3},{2,0},{3,1},{4,6},{5,7},{6,4},{7,5},{8,10},{9,11},{10,... | collective-permute-start | bytes 442376 | tf_op jit(solution)/shard_map/ppermute | solution.py:597
  26.6 0.3 collective-permute-start.3
  26.8 1.5 collective-permute-start.4
  28.3 0.2 collective-permute-start.5
  28.5 0.0 collective-permute-done.1.refs_1_
  28.5 2.5 %collective-permute-start.6 = (f32[9,32,128]{2,1,0:T(8,128)S(1)}, f32[9,32,128]{2,1,0:T(8,128)S(1)}, u32[]{:S(2)}, u32[]{:S(2)}) collective-permute-start(f32[9,32,128]{2,1,0:T(8,128)S(1)} %get-tuple-element.47), channel_id=1, source_target_pairs={{0,6},{1,7},{2,4},{3,5},{4,2},{5,3},{6,0},{7,1},{8,14},{9,15},{10,... | collective-permute-start | bytes 442376 | tf_op jit(solution)/shard_map/ppermute | solution.py:597
  31.0 9.0 %collective-permute-done.2.refs_2_ = f32[9,32,128]{2,1,0:T(8,128)S(1)} collective-permute-done((f32[9,32,128]{2,1,0:T(8,128)S(1)}, f32[9,32,128]{2,1,0:T(8,128)S(1)}, u32[]{:S(2)}, u32[]{:S(2)}) %collective-permute-start.2) | collective-permute-done | bytes 147488 | tf_op jit(solution)/shard_map/ppermute | solution.py:597
  40.0 0.2 collective-permute-start.7
  40.3 0.0 all-to-all-done.refs_0_
  40.3 0.0 copy-start
  40.3 2.2 %copy-done = bf16[2,32,128,256]{3,2,1,0:T(8,128)(2,1)S(1)} copy-done((bf16[2,32,128,256]{3,2,1,0:T(8,128)(2,1)S(1)}, bf16[2,32,128,256]{3,2,1,0:T(8,128)(2,1)}, u32[]{:S(2)}) %copy-start) | copy-done | bytes 4194328
  42.4 0.0 copy-start.1
  42.4 2.0 %shard_map.94.finished = f32[4,8,32,256]{3,2,1,0:T(8,128)S(1)} custom-call(f32[8,128]{1,0:T(8,128)S(1)} %get-tuple-element.39.after, f32[8,9,32,128]{3,2,1,0:T(8,128)S(1)} %all-to-all-done.refs_0_, bf16[2,32,128,256]{3,2,1,0:T(8,128)(2,1)S(1)} %copy-done), custom_call_target="tpu_custom_call" | custom-call | flops 2000000000 | bytes 8000000 | tf_op jit(solution)/shard_map/pallas_call | solution.py:531
  44.5 0.0 collective-permute-done.3.refs_3_
  44.5 0.0 collective-permute-done.4.refs_4_
  44.5 0.0 collective-permute-done.5.refs_5_
  44.5 2.8 %collective-permute-done.6.refs_6_ = f32[9,32,128]{2,1,0:T(8,128)S(1)} collective-permute-done((f32[9,32,128]{2,1,0:T(8,128)S(1)}, f32[9,32,128]{2,1,0:T(8,128)S(1)}, u32[]{:S(2)}, u32[]{:S(2)}) %collective-permute-start.6) | collective-permute-done | bytes 147488 | tf_op jit(solution)/shard_map/ppermute | solution.py:597
  47.2 2.2 %collective-permute-done.7.refs_7_ = f32[9,32,128]{2,1,0:T(8,128)S(1)} collective-permute-done((f32[9,32,128]{2,1,0:T(8,128)S(1)}, f32[9,32,128]{2,1,0:T(8,128)S(1)}, u32[]{:S(2)}, u32[]{:S(2)}) %collective-permute-start.7) | collective-permute-done | bytes 147488 | tf_op jit(solution)/shard_map/ppermute | solution.py:597
  49.5 0.0 copy-done.1
  49.5 2.8 %shard_map.95 = f32[4,8,64,256]{3,2,1,0:T(8,128)S(1)} custom-call(s32[2]{0:T(128)S(1)} %pad_add_fusion.place, f32[4,8,32,256]{3,2,1,0:T(8,128)S(1)} %shard_map.94.finished, f32[9,32,128]{2,1,0:T(8,128)S(1)} %get-tuple-element.41.refs_0_, f32[9,32,128]{2,1,0:T(8,128)S(1)} %collective-permute-done.1.refs_1_, f32[9,32,128]{2,1,0:T(8,128)S(1)} %collective-permute-done.2.refs_2_, ...), custom_call_target="tpu_custom_call" | custom-call | flops 2000000000 | bytes 8000000 | tf_op jit(solution)/shard_map/pallas_call | solution.py:531
  52.2 0.0 copy-start.2
  52.2 50.7 %all_to_all.10 = f32[32,64,256]{2,1,0:T(8,128)S(1)} all-to-all(f32[32,64,256]{2,1,0:T(8,128)S(1)} %bitcast.5), channel_id=1, replica_groups=mesh['row'=4,'col'=8] {'row','col'}, dimensions={0} | all-to-all | bytes 4194304 | tf_op jit(solution)/shard_map/all_to_all | solution.py:627
  102.9 0.0 copy-done.2
  102.9 3.2 %shard_map.96 = (f32[512,256]{1,0:T(8,128)S(1)}, f32[512,256]{1,0:T(8,128)S(1)}, f32[512,256]{1,0:T(8,128)S(1)}, f32[512,256]{1,0:T(8,128)S(1)}) custom-call(s32[2]{0:T(128)S(1)} %pad_add_fusion.place, f32[4,512,256]{2,1,0:T(8,128)S(1)} %bitcast.6, bf16[2,16,256,256]{3,2,1,0:T(8,128)(2,1)S(1)} %copy-done.2), custom_call_target="tpu_custom_call" | custom-call | flops 2500000000 | bytes 10000000 | tf_op jit(solution)/shard_map/pallas_call | solution.py:531
  106.2 1.4 collective-permute-start.9
  107.5 0.7 collective-permute-start.10
  108.3 1.5 collective-permute-start.8
  109.7 19.0 %collective-permute-done.9.refs_1_ = f32[512,256]{1,0:T(8,128)S(1)} collective-permute-done((f32[512,256]{1,0:T(8,128)S(1)}, f32[512,256]{1,0:T(8,128)S(1)}, u32[]{:S(2)}, u32[]{:S(2)}) %collective-permute-start.9) | collective-permute-done | bytes 524320 | tf_op jit(solution)/shard_map/ppermute | solution.py:645
  128.7 14.3 %collective-permute-done.10.refs_2_ = f32[512,256]{1,0:T(8,128)S(1)} collective-permute-done((f32[512,256]{1,0:T(8,128)S(1)}, f32[512,256]{1,0:T(8,128)S(1)}, u32[]{:S(2)}, u32[]{:S(2)}) %collective-permute-start.10) | collective-permute-done | bytes 524320 | tf_op jit(solution)/shard_map/ppermute | solution.py:645
  143.0 1.7 %shard_map.97.refs_1_ = f32[2,512,512]{2,1,0:T(8,128)} custom-call(s32[2]{0:T(128)S(1)} %pad_add_fusion.place, f32[512,256]{1,0:T(8,128)S(1)} %get-tuple-element.50.refs_0_, f32[512,256]{1,0:T(8,128)S(1)} %collective-permute-done.9.refs_1_, f32[512,256]{1,0:T(8,128)S(1)} %collective-permute-done.10.refs_2_), custom_call_target="tpu_custom_call" | custom-call | tf_op jit(solution)/shard_map/pallas_call | solution.py:658
  144.7 10.4 %collective-permute-done.8.refs_0_ = f32[512,256]{1,0:T(8,128)S(1)} collective-permute-done((f32[512,256]{1,0:T(8,128)S(1)}, f32[512,256]{1,0:T(8,128)S(1)}, u32[]{:S(2)}, u32[]{:S(2)}) %collective-permute-start.8) | collective-permute-done | bytes 524320 | tf_op jit(solution)/shard_map/ppermute | solution.py:645
  155.2 1.3 shard_map.98
Async XLA Ops:
  15.0 5.5 %copy-start.3 = (f32[8,9,32,128]{3,2,1,0:T(8,128)S(1)}, f32[8,9,32,128]{3,2,1,0:T(8,128)}, u32[]{:S(2)}) copy-start(f32[8,9,32,128]{3,2,1,0:T(8,128)} %get-tuple-element.30.early) | copy-start | bytes 3538948
  15.1 9.0 %collective-permute-start = (f32[2,9,32,128]{3,2,1,0:T(8,128)}, f32[2,9,32,128]{3,2,1,0:T(8,128)S(1)}, u32[]{:S(2)}, u32[]{:S(2)}) collective-permute-start(f32[2,9,32,128]{3,2,1,0:T(8,128)} %get-tuple-element.29), channel_id=1, source_target_pairs={{0,8},{8,16},{16,24},{24,0},{1,9},{9,17},{17,25},{25,1},{2,10},{10... | collective-permute-start | bytes 884744 | tf_op jit(solution)/shard_map/ppermute | solution.py:589
  16.7 23.5 %all-to-all-start = ((f32[8,9,32,128]{3,2,1,0:T(8,128)}), f32[8,9,32,128]{3,2,1,0:T(8,128)S(1)}, u32[]{:S(2)}, u32[]{:S(2)}) async-start(f32[8,9,32,128]{3,2,1,0:T(8,128)} %get-tuple-element.40), calls=%async_computation | async-start | bytes 2359296 | tf_op jit(solution)/shard_map/all_to_all | solution.py:590
  24.9 3.6 %collective-permute-start.1 = (f32[9,32,128]{2,1,0:T(8,128)S(1)}, f32[9,32,128]{2,1,0:T(8,128)S(1)}, u32[]{:S(2)}, u32[]{:S(2)}) collective-permute-start(f32[9,32,128]{2,1,0:T(8,128)S(1)} %get-tuple-element.42), channel_id=1, source_target_pairs={{0,1},{1,0},{2,3},{3,2},{4,5},{5,4},{6,7},{7,6},{8,9},{9,8},{10,11... | collective-permute-start | bytes 442376 | tf_op jit(solution)/shard_map/ppermute | solution.py:597
  25.0 15.0 %collective-permute-start.2 = (f32[9,32,128]{2,1,0:T(8,128)S(1)}, f32[9,32,128]{2,1,0:T(8,128)S(1)}, u32[]{:S(2)}, u32[]{:S(2)}) collective-permute-start(f32[9,32,128]{2,1,0:T(8,128)S(1)} %get-tuple-element.43), channel_id=1, source_target_pairs={{0,2},{1,3},{2,0},{3,1},{4,6},{5,7},{6,4},{7,5},{8,10},{9,11},{10,... | collective-permute-start | bytes 442376 | tf_op jit(solution)/shard_map/ppermute | solution.py:597
  26.6 17.9 %collective-permute-start.3 = (f32[9,32,128]{2,1,0:T(8,128)S(1)}, f32[9,32,128]{2,1,0:T(8,128)S(1)}, u32[]{:S(2)}, u32[]{:S(2)}) collective-permute-start(f32[9,32,128]{2,1,0:T(8,128)S(1)} %get-tuple-element.44), channel_id=1, source_target_pairs={{0,3},{1,2},{2,1},{3,0},{4,7},{5,6},{6,5},{7,4},{8,11},{9,10},{10,... | collective-permute-start | bytes 442376 | tf_op jit(solution)/shard_map/ppermute | solution.py:597
  26.8 17.6 %collective-permute-start.4 = (f32[9,32,128]{2,1,0:T(8,128)S(1)}, f32[9,32,128]{2,1,0:T(8,128)S(1)}, u32[]{:S(2)}, u32[]{:S(2)}) collective-permute-start(f32[9,32,128]{2,1,0:T(8,128)S(1)} %get-tuple-element.45), channel_id=1, source_target_pairs={{0,4},{1,5},{2,6},{3,7},{4,0},{5,1},{6,2},{7,3},{8,12},{9,13},{10,... | collective-permute-start | bytes 442376 | tf_op jit(solution)/shard_map/ppermute | solution.py:597
  28.3 16.1 %collective-permute-start.5 = (f32[9,32,128]{2,1,0:T(8,128)S(1)}, f32[9,32,128]{2,1,0:T(8,128)S(1)}, u32[]{:S(2)}, u32[]{:S(2)}) collective-permute-start(f32[9,32,128]{2,1,0:T(8,128)S(1)} %get-tuple-element.46), channel_id=1, source_target_pairs={{0,5},{1,4},{2,7},{3,6},{4,1},{5,0},{6,3},{7,2},{8,13},{9,12},{10,... | collective-permute-start | bytes 442376 | tf_op jit(solution)/shard_map/ppermute | solution.py:597
  28.5 18.7 %collective-permute-start.6 = (f32[9,32,128]{2,1,0:T(8,128)S(1)}, f32[9,32,128]{2,1,0:T(8,128)S(1)}, u32[]{:S(2)}, u32[]{:S(2)}) collective-permute-start(f32[9,32,128]{2,1,0:T(8,128)S(1)} %get-tuple-element.47), channel_id=1, source_target_pairs={{0,6},{1,7},{2,4},{3,5},{4,2},{5,3},{6,0},{7,1},{8,14},{9,15},{10,... | collective-permute-start | bytes 442376 | tf_op jit(solution)/shard_map/ppermute | solution.py:597
  40.0 9.4 %collective-permute-start.7 = (f32[9,32,128]{2,1,0:T(8,128)S(1)}, f32[9,32,128]{2,1,0:T(8,128)S(1)}, u32[]{:S(2)}, u32[]{:S(2)}) collective-permute-start(f32[9,32,128]{2,1,0:T(8,128)S(1)} %get-tuple-element.48), channel_id=1, source_target_pairs={{0,7},{1,6},{2,5},{3,4},{4,3},{5,2},{6,1},{7,0},{8,15},{9,14},{10,... | collective-permute-start | bytes 442376 | tf_op jit(solution)/shard_map/ppermute | solution.py:597
  40.3 2.2 %copy-start = (bf16[2,32,128,256]{3,2,1,0:T(8,128)(2,1)S(1)}, bf16[2,32,128,256]{3,2,1,0:T(8,128)(2,1)}, u32[]{:S(2)}) copy-start(bf16[2,32,128,256]{3,2,1,0:T(8,128)(2,1)} %constant.21.clone.refs_1_.refs_8_) | copy-start | bytes 12582916
  42.4 7.0 %copy-start.1 = (bf16[2,32,128,256]{3,2,1,0:T(8,128)(2,1)S(1)}, bf16[2,32,128,256]{3,2,1,0:T(8,128)(2,1)}, u32[]{:S(2)}) copy-start(bf16[2,32,128,256]{3,2,1,0:T(8,128)(2,1)} %constant.21.clone.refs_1_.refs_8_) | copy-start | bytes 12582916
  52.2 50.7 %copy-start.2 = (bf16[2,16,256,256]{3,2,1,0:T(8,128)(2,1)S(1)}, bf16[2,16,256,256]{3,2,1,0:T(8,128)(2,1)}, u32[]{:S(2)}) copy-start(bf16[2,16,256,256]{3,2,1,0:T(8,128)(2,1)} %constant.22.clone.table) | copy-start | bytes 12582916
  106.2 22.5 %collective-permute-start.9 = (f32[512,256]{1,0:T(8,128)S(1)}, f32[512,256]{1,0:T(8,128)S(1)}, u32[]{:S(2)}, u32[]{:S(2)}) collective-permute-start(f32[512,256]{1,0:T(8,128)S(1)} %get-tuple-element.51), channel_id=1, source_target_pairs={{0,8},{8,0},{16,24},{24,16},{1,9},{9,1},{17,25},{25,17},{2,10},{10... | collective-permute-start | bytes 1572872 | tf_op jit(solution)/shard_map/ppermute | solution.py:645
  107.5 35.5 %collective-permute-start.10 = (f32[512,256]{1,0:T(8,128)S(1)}, f32[512,256]{1,0:T(8,128)S(1)}, u32[]{:S(2)}, u32[]{:S(2)}) collective-permute-start(f32[512,256]{1,0:T(8,128)S(1)} %get-tuple-element.52), channel_id=1, source_target_pairs={{0,16},{8,24},{16,0},{24,8},{1,17},{9,25},{17,1},{25,9},{2,18},{10... | collective-permute-start | bytes 1572872 | tf_op jit(solution)/shard_map/ppermute | solution.py:645
  108.3 46.9 %collective-permute-start.8 = (f32[512,256]{1,0:T(8,128)S(1)}, f32[512,256]{1,0:T(8,128)S(1)}, u32[]{:S(2)}, u32[]{:S(2)}) collective-permute-start(f32[512,256]{1,0:T(8,128)S(1)} %get-tuple-element.49), channel_id=1, source_target_pairs={{0,24},{8,16},{16,8},{24,0},{1,25},{9,17},{17,9},{25,1},{2,26},{10... | collective-permute-start | bytes 1572872 | tf_op jit(solution)/shard_map/ppermute | solution.py:645
